TPU v7x, 128 devices: a whole 4x4x4 slice. The times are simulated.
128 devices in a mesh: grp: 2 (over x_lo), ep: 64 (over x_hi, y, z, core).
Axes of the slice: x: 4 (x_hi: 2, x_lo: 2; x = x_hi * 2 + x_lo), y: 4, z: 4, core: 2. Of those that a mesh axis runs over, the one named last changes fastest.
Arguments:
- tokens: bfloat16 [16384, 2048], P(('grp', 'ep')), may hold values from -6 to 6
- cotangent: bfloat16 [16384, 2048], P(('grp', 'ep')), may hold values from -6 to 6
- combine: float32 [16384, 4], P(('grp', 'ep')), may hold values from 0.05 to 1
- route: int32 [16384, 4], P(('grp', 'ep')), may hold values from 0 to 127, all different within a row; in each aligned block of 128 rows (0 to 127, 128 to 255, ...) at most 6 rows name the same one
- anchors: int32 [64], replicated, may hold values from 0 to 63, as said below
- w_gate: bfloat16 [128, 2048, 768], P(('grp', 'ep')), may hold values from -0.125 to 0.125
- w_up: bfloat16 [128, 2048, 768], P(('grp', 'ep')), may hold values from -0.125 to 0.125
- w_down: bfloat16 [128, 768, 2048], P(('grp', 'ep')), may hold values from -0.21875 to 0.21875
Outputs:
- mixed: bfloat16 [16384, 2048], P(('grp', 'ep'))
- input_grad: bfloat16 [16384, 2048], P(('grp', 'ep'))
- grad_gate: float32 [64, 2048, 768], P('ep', 'grp')
- grad_up: float32 [64, 2048, 768], P('ep', 'grp')
- grad_down: float32 [64, 768, 2048], P('ep', None, 'grp')
Inputs may be any that keep to these rules, and one draw needn't show every extreme that they name: route[t, k] names the slot g * 64 + p that choice k of token t goes to; a token's 4 choices name different slots; among the tokens of one device no slot is named more than 6 times. anchors[p] is p, or p - 1 for an odd p; every even p holds its own expert; anchors[63] = 62 and anchors[33] = 32.
All inputs are finite; a program needn't handle non-finite values.
Results may differ from a plain program's by a relative error of at most 0.0064.
Values may be sent and summed in bfloat16 or wider, within the bound.
No kernel may reach another device: no remote copies, remote signals or barrier semaphores. Data moves between devices by JAX's collectives and lax.ppermute only.
A program may use at most 192 MiB of HBM per device.

v0:
```python
import jax
import jax.numpy as jnp
from jax import lax
from jax.sharding import PartitionSpec as P


def shifted(block, axis, distance):
    devices = range(lax.axis_size(axis))
    route = [(i - distance, i) for i in devices if i - distance in devices]
    return lax.ppermute(block, axis, route)


def from_partner(block, axis, distance):
    count = lax.axis_size(axis)
    route = []
    for low in range(count):
        high = low | 1 << distance
        if high != low and high < count:
            route += [(low, high), (high, low)]
    return lax.ppermute(block, axis, route)


def expert_pass(inputs, cot_rows, gate_weight, up_weight, down_weight):
    gate = jnp.dot(inputs, gate_weight, preferred_element_type=jnp.float32)
    up_proj = jnp.dot(inputs, up_weight, preferred_element_type=jnp.float32)
    sigma = jax.nn.sigmoid(gate)
    active = gate * sigma
    hidden = (active * up_proj).astype(jnp.bfloat16)
    expert_out = jnp.dot(hidden, down_weight, preferred_element_type=jnp.float32).astype(
        jnp.bfloat16
    )
    back = lax.dot_general(
        cot_rows, down_weight, (((1,), (1,)), ((), ())), preferred_element_type=jnp.float32
    )
    d_gate = (back * up_proj * sigma * (1.0 + gate * (1.0 - sigma))).astype(jnp.bfloat16)
    d_up = (back * active).astype(jnp.bfloat16)
    row_grad = (
        lax.dot_general(
            d_gate, gate_weight, (((1,), (1,)), ((), ())), preferred_element_type=jnp.float32
        )
        + lax.dot_general(
            d_up, up_weight, (((1,), (1,)), ((), ())), preferred_element_type=jnp.float32
        )
    ).astype(jnp.bfloat16)
    part_gate = lax.dot_general(
        inputs, d_gate, (((0,), (0,)), ((), ())), preferred_element_type=jnp.float32
    ).astype(jnp.bfloat16)
    part_up = lax.dot_general(
        inputs, d_up, (((0,), (0,)), ((), ())), preferred_element_type=jnp.float32
    ).astype(jnp.bfloat16)
    part_down_t = lax.dot_general(
        cot_rows, hidden, (((0,), (0,)), ((), ())), preferred_element_type=jnp.float32
    ).astype(jnp.bfloat16)
    return (expert_out, row_grad, jnp.stack([part_gate, part_up, part_down_t]))


def half_of(stacked, which):
    size = stacked.shape[1] // 2
    return lax.dynamic_slice_in_dim(stacked, which * size, size, 1)


def on_device(tokens, cotangent, combine, route, anchors, w_gate, w_up, w_down):
    grp_count = lax.axis_size("grp")
    ep_count = lax.axis_size("ep")
    slot_count = grp_count * ep_count
    grp_index = lax.axis_index("grp")
    ep_index = lax.axis_index("ep")
    token_count, width = tokens.shape
    top_count = route.shape[1]
    row_count = token_count * top_count
    pair_rows = 3 * row_count // (2 * slot_count)
    slot_gate = w_gate[0]
    slot_up = w_up[0]
    slot_down = w_down[0]
    my_anchor = anchors[ep_index]
    target = route.reshape(row_count)
    marks = (target[:, None] == jnp.arange(slot_count, dtype=jnp.int32)[None, :]).astype(jnp.int32)
    target_rank = jnp.sum(jnp.cumsum(marks, axis=0) * marks, axis=1) - 1
    position = target * pair_rows + target_rank
    source_row = (
        jnp.full((slot_count * pair_rows,), row_count, jnp.int32)
        .at[position]
        .set(jnp.arange(row_count, dtype=jnp.int32))
    )
    tokens_ext = jnp.concatenate([tokens, jnp.zeros((1, width), tokens.dtype)])
    cot_rows = (combine[:, :, None] * cotangent[:, None, :].astype(jnp.float32)).astype(
        jnp.bfloat16
    )
    cot_ext = jnp.concatenate(
        [cot_rows.reshape(row_count, width), jnp.zeros((1, width), jnp.bfloat16)]
    )
    outgoing = jnp.stack([tokens_ext[source_row // top_count], cot_ext[source_row]]).reshape(
        2, slot_count, pair_rows, width
    )
    arrived = lax.all_to_all(outgoing, ("grp", "ep"), split_axis=1, concat_axis=1, tiled=True)
    inputs = arrived[0].reshape(slot_count * pair_rows, width)
    cot_in = arrived[1].reshape(slot_count * pair_rows, width)
    expert_out, row_grad, stacked = expert_pass(inputs, cot_in, slot_gate, slot_up, slot_down)
    returning = jnp.stack([expert_out, row_grad]).reshape(2, slot_count, pair_rows, width)
    came_back = lax.all_to_all(returning, ("grp", "ep"), split_axis=1, concat_axis=1, tiled=True)
    came_back = came_back.reshape(2, slot_count * pair_rows, width)
    out_rows = came_back[0][position].reshape(token_count, top_count, width).astype(jnp.float32)
    grad_rows = came_back[1][position].reshape(token_count, top_count, width).astype(jnp.float32)
    mixed = jnp.sum(combine[:, :, None] * out_rows, axis=1).astype(jnp.bfloat16)
    input_grad = jnp.sum(grad_rows, axis=1).astype(jnp.bfloat16)
    is_anchor = my_anchor == ep_index
    next_index = jnp.minimum(ep_index + 1, ep_count - 1)
    right_joins = (ep_index + 1 < ep_count) & (anchors[next_index] == ep_index)
    from_right = shifted(stacked, "ep", -1)
    own_terms = stacked.astype(jnp.float32)
    joined = own_terms + jnp.where(right_joins, from_right.astype(jnp.float32), 0.0)
    base = jnp.where(grp_index == 0, own_terms, joined)
    received = from_partner(half_of(base, 1 - grp_index).astype(jnp.bfloat16), "grp", 0).astype(
        jnp.float32
    )
    kept = half_of(base, grp_index)
    total = jnp.where(
        grp_index == 0,
        kept + jnp.where(is_anchor, received, 0.0),
        received + jnp.where(is_anchor, kept, 0.0),
    )
    grad_gate = total[0][None]
    grad_up = total[1][None]
    grad_down = jnp.transpose(total[2])[None]
    return (mixed, input_grad, grad_gate, grad_up, grad_down)


def solution(mesh):
    placed = (
        P(("grp", "ep"), None),
        P(("grp", "ep"), None),
        P(("grp", "ep"), None),
        P(("grp", "ep"), None),
        P(),
        P(("grp", "ep"), None, None),
        P(("grp", "ep"), None, None),
        P(("grp", "ep"), None, None),
    )
    return jax.shard_map(
        on_device,
        mesh=mesh,
        in_specs=placed,
        out_specs=(
            P(("grp", "ep"), None),
            P(("grp", "ep"), None),
            P("ep", "grp", None),
            P("ep", "grp", None),
            P("ep", None, "grp"),
        ),
        check_vma=False,
    )
```

profile of v0, /device:TPU:4, one launch (start us, length us, event | category | flops | bytes accessed | tf_op | source)
XLA Modules:
  0.0 560.3 jit_solution(13234749529463481917)
XLA Ops:
  0.6 0.8 broadcast_multiply_fusion
  1.5 0.9 copy.25
  2.4 0.1 eq.39
  2.5 0.1 eq.35
  2.6 0.1 copy.24
  2.7 0.1 mul.75
  2.8 0.8 copy.23
  3.6 0.1 mul.77
  3.7 0.5 copy-done.8
  4.2 0.1 copy.27
  4.4 0.2 fusion.17
  4.7 0.2 fusion.16
  4.9 2.4 scatter_custom_fusion
  7.4 1.9 concatenate.8
  9.3 8.2 %gather_fusion = bf16[768,2048]{1,0:T(8,128)(2,1)} fusion(bf16[129,2048]{1,0:T(8,128)(2,1)} %concatenate.8, s32[1024]{0:T(1024)S(1)} %get-tuple-element.35), kind=kCustom, calls=%fused_computation | custom fusion | bytes 6294528 | tf_op jit(solution)/shard_map/gather | solution.py:92
  17.5 6.3 %stack.30 = bf16[1,128,6,2048]{3,2,1,0:T(8,128)(2,1)} reshape(bf16[768,2048]{1,0:T(8,128)(2,1)} %gather_fusion) | data formatting | bytes 6291456 | tf_op jit(solution)/shard_map/stack | solution.py:92
  23.8 4.1 mul.79
  27.9 5.3 mul.80
  33.2 2.5 multiply_convert_fusion
  35.7 1.5 concatenate.9
  37.2 9.0 %gather_fusion.1 = bf16[768,2048]{1,0:T(8,128)(2,1)} fusion(bf16[513,2048]{1,0:T(8,128)(2,1)} %concatenate.9, s32[1024]{0:T(1024)S(1)} %get-tuple-element.34), kind=kCustom, calls=%fused_computation.1 | custom fusion | bytes 6294528 | tf_op jit(solution)/shard_map/gather | solution.py:92
  46.1 6.3 %stack.31 = bf16[1,128,6,2048]{3,2,1,0:T(8,128)(2,1)} reshape(bf16[768,2048]{1,0:T(8,128)(2,1)} %gather_fusion.1) | data formatting | bytes 6291456 | tf_op jit(solution)/shard_map/stack | solution.py:92
  52.4 8.9 %pad_maximum_fusion.1 = bf16[2,128,6,2048]{3,2,1,0:T(8,128)(2,1)} fusion(bf16[1,128,6,2048]{3,2,1,0:T(8,128)(2,1)} %stack.31, bf16[1,128,6,2048]{3,2,1,0:T(8,128)(2,1)} %stack.30), kind=kLoop, calls=%fused_computation.12 | loop fusion | flops 3145728 | bytes 12582912 | tf_op jit(solution)/shard_map/stack | solution.py:92
  61.3 9.7 %copy.30 = bf16[2,128,6,2048]{3,0,2,1:T(2,128)(2,1)S(1)} copy(bf16[2,128,6,2048]{3,2,1,0:T(8,128)(2,1)} %pad_maximum_fusion.1) | data formatting | bytes 12582912 | tf_op jit(solution)/shard_map/stack | solution.py:92
  71.0 84.7 %all_to_all.10 = bf16[2,128,6,2048]{3,0,2,1:T(2,128)(2,1)S(1)} all-to-all(bf16[2,128,6,2048]{3,0,2,1:T(2,128)(2,1)S(1)} %copy.30), channel_id=1, replica_groups=mesh['grp'=2,'ep'=64] {'grp','ep'}, dimensions={1} | all-to-all | bytes 12582912 | tf_op jit(solution)/shard_map/all_to_all | solution.py:95
  155.7 32.3 %slice_reduce_fusion.2 = (bf16[128,6,2048]{2,1,0:T(8,128)(2,1)}, bf16[128,6,2048]{2,1,0:T(8,128)(2,1)}) fusion(bf16[2,128,6,2048]{3,0,2,1:T(2,128)(2,1)S(1)} %all_to_all.10), kind=kLoop, calls=%fused_computation.16 | loop fusion | bytes 12582912 | tf_op jit(solution)/shard_map/slice | solution.py:97
  188.0 6.3 %reshape_squeeze.7 = bf16[768,2048]{1,0:T(8,128)(2,1)} reshape(bf16[128,6,2048]{2,1,0:T(8,128)(2,1)} %get-tuple-element.22) | data formatting | bytes 6291456 | tf_op jit(solution)/shard_map/reshape;squeeze | solution.py:97
  194.4 6.3 %reshape_squeeze.6 = bf16[768,2048]{1,0:T(8,128)(2,1)} reshape(bf16[128,6,2048]{2,1,0:T(8,128)(2,1)} %get-tuple-element.23) | data formatting | bytes 6291456 | tf_op jit(solution)/shard_map/reshape;squeeze | solution.py:96
  200.7 5.6 %fusion.2 = f32[768,768]{1,0:T(8,128)S(1)} fusion(bf16[768,2048]{1,0:T(8,128)(2,1)} %reshape_squeeze.7, bf16[1,768,2048]{2,1,0:T(8,128)(2,1)} %param.15), kind=kOutput, calls=%fused_computation.26 | convolution fusion | flops 2415919104 | bytes 8650752 | tf_op jit(solution)/shard_map/dot_general | solution.py:32
  206.3 2.6 fusion.10
  209.0 3.4 multiply_convert_fusion.3
  212.4 3.3 fusion.14
  215.7 2.9 fusion.12
  218.7 2.9 fusion.13
  221.7 4.7 pad_maximum_fusion
  226.3 0.4 copy-done.5
  226.7 5.4 collective-permute-start
  232.2 4.0 convolution_convert_fusion.3
  236.1 6.2 %stack.33 = bf16[1,128,6,2048]{3,2,1,0:T(8,128)(2,1)} reshape(bf16[768,2048]{1,0:T(8,128)(2,1)} %convolution_convert_fusion.3) | data formatting | bytes 6291456 | tf_op jit(solution)/shard_map/stack | solution.py:99
  242.4 5.0 fusion.8
  247.3 4.0 add_convert_fusion
  251.4 6.2 %stack.34 = bf16[1,128,6,2048]{3,2,1,0:T(8,128)(2,1)} reshape(bf16[768,2048]{1,0:T(8,128)(2,1)} %add_convert_fusion) | data formatting | bytes 6291456 | tf_op jit(solution)/shard_map/stack | solution.py:99
  257.6 9.0 %pad_maximum_fusion.2 = bf16[2,128,6,2048]{3,2,1,0:T(8,128)(2,1)} fusion(bf16[1,128,6,2048]{3,2,1,0:T(8,128)(2,1)} %stack.34, bf16[1,128,6,2048]{3,2,1,0:T(8,128)(2,1)} %stack.33), kind=kLoop, calls=%fused_computation.13 | loop fusion | flops 3145728 | bytes 12582912 | tf_op jit(solution)/shard_map/stack | solution.py:99
  266.6 10.5 %copy.31 = bf16[2,128,6,2048]{3,0,2,1:T(2,128)(2,1)} copy(bf16[2,128,6,2048]{3,2,1,0:T(8,128)(2,1)} %pad_maximum_fusion.2) | data formatting | bytes 12582912 | tf_op jit(solution)/shard_map/stack | solution.py:99
  277.1 8.1 %all-to-all-start.1 = ((bf16[2,128,6,2048]{3,0,2,1:T(2,128)(2,1)}), bf16[2,128,6,2048]{3,0,2,1:T(2,128)(2,1)}, u32[]{:S(2)}, u32[]{:S(2)}) async-start(bf16[2,128,6,2048]{3,0,2,1:T(2,128)(2,1)} %copy.31), calls=%async_computation.1 | async-start | bytes 12582912 | tf_op jit(solution)/shard_map/all_to_all | solution.py:100
  285.2 0.6 fusion.24
  286.5 106.9 %collective-permute-done = bf16[3,2048,768]{2,1,0:T(8,128)(2,1)} collective-permute-done((bf16[3,2048,768]{2,1,0:T(8,128)(2,1)}, bf16[3,2048,768]{2,1,0:T(8,128)(2,1)}, u32[]{:S(2)}, u32[]{:S(2)}) %collective-permute-start) | collective-permute-done | bytes 9437216 | tf_op jit(solution)/shard_map/ppermute | solution.py:10
  393.3 14.1 %add_select_fusion = f32[3,2048,768]{2,1,0:T(8,128)} fusion(bf16[3,2048,768]{2,1,0:T(8,128)(2,1)} %collective-permute-done, pred[]{:T(512)S(6)} %and.11, pred[]{:T(512)S(6)} %eq.43, bf16[1,2048,768]{2,1,0:T(8,128)(2,1)S(1)} %copy-done.3, bf16[1,2048,768]{2,1,0:T(8,128)(2,1)} %copy-done.5, bf16[1,2048,768]{2,1,0:T(8,128)(2,1)} %copy-done.4), kind=kLoop, calls=%fused_computation.5 | loop fusion | flops 33030144 | bytes 37748736 | tf_op jit(solution)/shard_map/jit(_where)/select_n | solution.py:112
  407.4 6.3 %dynamic-slice_convert_fusion = bf16[3,1024,768]{2,1,0:T(8,128)(2,1)} fusion(f32[3,2048,768]{2,1,0:T(8,128)} %add_select_fusion, s32[]{:T(128)S(6)} %select_n.84), kind=kLoop, calls=%fused_computation.11 | loop fusion | bytes 9437188 | tf_op jit(solution)/shard_map/convert_element_type | solution.py:113
  413.7 9.4 %collective-permute-start.1 = (bf16[3,1024,768]{2,1,0:T(8,128)(2,1)}, bf16[3,1024,768]{2,1,0:T(8,128)(2,1)}, u32[]{:S(2)}, u32[]{:S(2)}) collective-permute-start(bf16[3,1024,768]{2,1,0:T(8,128)(2,1)} %dynamic-slice_convert_fusion), channel_id=1, source_target_pairs={{0,64},{64,0},{1,65},{65,1},{2,66},{66,2},{3,67},{67,3},{4,68},{68... | collective-permute-start | bytes 14155784 | tf_op jit(solution)/shard_map/ppermute | solution.py:20
  423.7 9.6 %all-to-all-done.1 = bf16[2,128,6,2048]{3,0,2,1:T(2,128)(2,1)} async-done(((bf16[2,128,6,2048]{3,0,2,1:T(2,128)(2,1)}), bf16[2,128,6,2048]{3,0,2,1:T(2,128)(2,1)}, u32[]{:S(2)}, u32[]{:S(2)}) %all-to-all-start.1) | async-done | bytes 6291488 | tf_op jit(solution)/shard_map/all_to_all | solution.py:100
  433.3 32.9 %slice_reduce_fusion = (bf16[128,6,2048]{2,1,0:T(8,128)(2,1)}, bf16[128,6,2048]{2,1,0:T(8,128)(2,1)}) fusion(bf16[2,128,6,2048]{3,0,2,1:T(2,128)(2,1)} %all-to-all-done.1), kind=kLoop, calls=%fused_computation.14 | loop fusion | bytes 12582912 | tf_op jit(solution)/shard_map/slice | solution.py:103
  466.2 4.9 squeeze.28
  471.1 3.3 gather_fusion.3
  474.4 2.7 reshape.89
  477.1 3.9 reduce_sum.32
  481.0 4.9 squeeze.27
  485.9 3.3 gather_fusion.2
  489.1 5.0 reshape.90
  494.1 6.2 %multiply_reduce_fusion = bf16[128,2048]{1,0:T(8,128)(2,1)} fusion(f32[128,4,2048]{2,1,0:T(4,128)} %reshape.90, f32[128,4]{1,0:T(8,128)S(1)} %copy-done.9), kind=kLoop, calls=%fused_computation.19 | loop fusion | flops 1835008 | bytes 4720640 | tf_op jit(solution)/shard_map/reduce_sum | solution.py:104
  500.3 37.6 %collective-permute-done.1 = bf16[3,1024,768]{2,1,0:T(8,128)(2,1)} collective-permute-done((bf16[3,1024,768]{2,1,0:T(8,128)(2,1)}, bf16[3,1024,768]{2,1,0:T(8,128)(2,1)}, u32[]{:S(2)}, u32[]{:S(2)}) %collective-permute-start.1) | collective-permute-done | bytes 4718624 | tf_op jit(solution)/shard_map/ppermute | solution.py:20
  538.0 10.7 %fusion.1 = f32[3,1024,768]{2,1,0:T(8,128)} fusion(bf16[3,1024,768]{2,1,0:T(8,128)(2,1)} %collective-permute-done.1, f32[3,2048,768]{2,1,0:T(8,128)} %add_select_fusion, s32[]{:T(128)S(6)} %select_n.81, pred[]{:T(512)S(6)} %eq.45, pred[]{:T(512)S(6)} %eq.43), kind=kLoop, calls=%fused_computation.9 | loop fusion | flops 14155776 | bytes 23592966 | tf_op jit(solution)/shard_map/jit(_where)/select_n | solution.py:117
  548.6 7.7 %slice_bitcast_fusion = (f32[1,768,1024]{1,2,0:T(8,128)}, f32[1,1024,768]{2,1,0:T(8,128)}, f32[1,1024,768]{2,1,0:T(8,128)}) fusion(f32[3,1024,768]{2,1,0:T(8,128)} %fusion.1), kind=kLoop, calls=%fused_computation.25 | loop fusion | bytes 18874368 | tf_op jit(solution)/shard_map/broadcast_in_dim | solution.py:124
  556.3 3.7 copy.32
  (42 shorter events, 0.2 us)
Async XLA Ops:
  0.6 208.3 %copy-start = (bf16[1,2048,768]{2,1,0:T(8,128)(2,1)S(1)}, bf16[1,2048,768]{2,1,0:T(8,128)(2,1)}, u32[]{:S(2)}) copy-start(bf16[1,2048,768]{2,1,0:T(8,128)(2,1)} %param.14) | copy-start | bytes 9437188
  3.6 0.6 copy-start.8
  200.7 5.6 %copy-start.6 = (bf16[768,2048]{1,0:T(8,128)(2,1)S(1)}, bf16[768,2048]{1,0:T(8,128)(2,1)}, u32[]{:S(2)}) copy-start(bf16[768,2048]{1,0:T(8,128)(2,1)} %reshape_squeeze.6) | copy-start | bytes 9437188
  200.7 5.6 %copy-start.12 = (bf16[1,2048,768]{2,1,0:T(8,128)(2,1)S(1)}, bf16[1,2048,768]{2,1,0:T(8,128)(2,1)}, u32[]{:S(2)}) copy-start(bf16[1,2048,768]{2,1,0:T(8,128)(2,1)} %param.13) | copy-start | bytes 9437188
  209.0 3.4 copy-start.7
  212.3 3.4 copy-start.13
  212.3 6.3 %copy-start.14 = (bf16[768,768]{1,0:T(8,128)(2,1)}, bf16[768,768]{1,0:T(8,128)(2,1)S(1)}, u32[]{:S(2)}) copy-start(bf16[768,768]{1,0:T(8,128)(2,1)S(1)} %get-tuple-element.29) | copy-start | bytes 3538948
  215.7 5.9 %copy-start.2 = (bf16[1,2048,768]{2,1,0:T(8,128)(2,1)}, bf16[1,2048,768]{2,1,0:T(8,128)(2,1)S(1)}, u32[]{:S(2)}) copy-start(bf16[1,2048,768]{2,1,0:T(8,128)(2,1)S(1)} %fusion.14) | copy-start | bytes 9437188
  218.7 3.0 copy-start.4
  221.6 5.1 copy-start.5
  221.6 10.5 %copy-start.11 = (bf16[1,768,2048]{2,1,0:T(8,128)(2,1)S(1)}, bf16[1,768,2048]{2,1,0:T(8,128)(2,1)}, u32[]{:S(2)}) copy-start(bf16[1,768,2048]{2,1,0:T(8,128)(2,1)} %param.15) | copy-start | bytes 9437188
  226.7 166.6 %collective-permute-start = (bf16[3,2048,768]{2,1,0:T(8,128)(2,1)}, bf16[3,2048,768]{2,1,0:T(8,128)(2,1)}, u32[]{:S(2)}, u32[]{:S(2)}) collective-permute-start(bf16[3,2048,768]{2,1,0:T(8,128)(2,1)} %pad_maximum_fusion), channel_id=1, source_target_pairs={{1,0},{2,1},{3,2},{4,3},{5,4},{6,5},{7,6},{8,7},{9,8},{10,9},{11,1... | collective-permute-start | bytes 28311560 | tf_op jit(solution)/shard_map/ppermute | solution.py:10
  242.4 5.0 copy-start.15
  277.1 8.2 %copy-start.10 = (s32[64]{0:T(128)S(1)}, s32[64]{0:T(128)}, u32[]{:S(2)}) copy-start(s32[64]{0:T(128)} %param.12) | copy-start | bytes 772
  277.1 116.3 %copy-start.3 = (bf16[1,2048,768]{2,1,0:T(8,128)(2,1)S(1)}, bf16[1,2048,768]{2,1,0:T(8,128)(2,1)}, u32[]{:S(2)}) copy-start(bf16[1,2048,768]{2,1,0:T(8,128)(2,1)} %copy-done.2) | copy-start | bytes 9437188
  277.1 156.3 %all-to-all-start.1 = ((bf16[2,128,6,2048]{3,0,2,1:T(2,128)(2,1)}), bf16[2,128,6,2048]{3,0,2,1:T(2,128)(2,1)}, u32[]{:S(2)}, u32[]{:S(2)}) async-start(bf16[2,128,6,2048]{3,0,2,1:T(2,128)(2,1)} %copy.31), calls=%async_computation.1 | async-start | bytes 12582912 | tf_op jit(solution)/shard_map/all_to_all | solution.py:100
  413.7 124.3 %collective-permute-start.1 = (bf16[3,1024,768]{2,1,0:T(8,128)(2,1)}, bf16[3,1024,768]{2,1,0:T(8,128)(2,1)}, u32[]{:S(2)}, u32[]{:S(2)}) collective-permute-start(bf16[3,1024,768]{2,1,0:T(8,128)(2,1)} %dynamic-slice_convert_fusion), channel_id=1, source_target_pairs={{0,64},{64,0},{1,65},{65,1},{2,66},{66,2},{3,67},{67,3},{4,68},{68... | collective-permute-start | bytes 14155784 | tf_op jit(solution)/shard_map/ppermute | solution.py:20
  489.1 5.0 copy-start.9
  556.3 3.7 copy-start.1
where the time goes:
time: 570 us; the launch traced here: 560 us
  local copies, waits for them, and re-layouts  201 us (35%)
  waiting for transfers between devices  154 us (27%)
  blocking collectives  84.7 us (15%)
  other arithmetic  61.2 us (11%)
  matrix products  33.7 us (6%)
  starting transfers between devices  22.9 us (4%)
    ppermute x1, waiting for transfers between devices, shifted(): return lax.ppermute(block, axis, route)  107 us
    all_to_all x1, blocking collectives, on_device(): lax.all_to_all(outgoing, ('grp', 'ep'), split_axis=1, concat_axis=1, tile...  84.7 us
    ppermute x1, waiting for transfers between devices, from_partner(): return lax.ppermute(block, axis, route)  37.6 us
    slice x1, local copies, waits for them, and re-layouts, on_device(): came_back[1][position].reshape(token_count, top_count, width)  32.9 us
    slice x1, local copies, waits for them, and re-layouts, on_device(): cot_in = arrived[1].reshape(slot_count * pair_rows, width)  32.3 us
    another operation x3, local copies, waits for them, and re-layouts, on_device(): jnp.stack([expert_out, row_grad]).reshape(2, slot_count, pair_rows, width)  22.9 us
    another operation x3, local copies, waits for them, and re-layouts, on_device(): jnp.stack([tokens_ext[source_row // top_count], cot_ext[source_row]])  22.2 us
    select_n x1, other arithmetic, on_device(): base = jnp.where(grp_index == 0, own_terms, joined)  14.1 us
  transfers between devices with their start and end apart: 3, of which 3 were waited for; matrix products, arithmetic and copies ran while one was open for 24% of the time, Pallas kernels for 0%

commit v1 on v0

v1 whole, which is shorter than its diff:
```python
import functools

import jax
import jax.numpy as jnp
from jax import lax
from jax.experimental import pallas as pl
from jax.experimental.pallas import tpu as pltpu
from jax.sharding import Mesh, PartitionSpec as P

AXES = ("xlo", "xhi", "y", "z", "core")
PLANE = ("y", "z", "core")
LANES = 128
MIB = 1 << 20


def pack_kernel(pair_rows, dest, weight, tok_ref, cot_ref, out_ref, tok32, cot32):
    tokens, width = tok_ref.shape
    parts = width // LANES
    top = dest.shape[0] // tokens
    step = 1536
    blank = jnp.zeros((step, LANES), out_ref.dtype)

    @pl.loop(0, out_ref.shape[0] // step)
    def _(i):
        out_ref[pl.ds(pl.multiple_of(i * step, step), step), :] = blank

    for j in range(parts):
        cols = slice(j * LANES, (j + 1) * LANES)
        tok32[pl.ds(j, tokens, stride=parts), :] = tok_ref[:, cols].astype(jnp.float32)
        cot32[pl.ds(j, tokens, stride=parts), :] = cot_ref[:, cols].astype(jnp.float32)

    @pl.loop(0, tokens, unroll=2)
    def _(t):
        rows = pl.ds(pl.multiple_of(t * parts, parts), parts)
        tok = tok32[rows, :].astype(out_ref.dtype)
        cot = cot32[rows, :]
        for k in range(top):
            place = dest[t * top + k]
            out_ref[pl.ds(pl.multiple_of(place * parts, parts), parts), :] = tok
            out_ref[pl.ds(pl.multiple_of((place + pair_rows) * parts, parts), parts), :] = (
                cot * weight[t * top + k]
            ).astype(out_ref.dtype)


def pack(dest, weight, tokens, cotangent, slots, pair_rows):
    count, width = tokens.shape
    parts = width // LANES
    total = slots * 2 * pair_rows * parts
    return pl.pallas_call(
        functools.partial(pack_kernel, pair_rows),
        out_shape=jax.ShapeDtypeStruct((total, LANES), jnp.bfloat16),
        in_specs=[pl.BlockSpec(memory_space=pltpu.SMEM)] * 2
        + [pl.BlockSpec(memory_space=pltpu.VMEM)] * 2,
        out_specs=pl.BlockSpec(memory_space=pltpu.VMEM),
        scratch_shapes=[pltpu.VMEM((count * parts, LANES), jnp.float32)] * 2,
        compiler_params=pltpu.CompilerParams(vmem_limit_bytes=24 * MIB),
        cost_estimate=pl.CostEstimate(flops=0, bytes_accessed=12 * MIB, transcendentals=0),
    )(dest, weight, tokens, cotangent)


def unpack_kernel(in_ref, out_ref, wide):
    rings, members, _, tall, _ = in_ref.shape
    rows, width = out_ref.shape
    parts = width // LANES
    for m in range(members):
        for x in range(rings):
            wide[pl.ds((m * rings + x) * tall, tall), :] = in_ref[x, m, 0].astype(jnp.float32)
    for j in range(parts):
        out_ref[:, j * LANES : (j + 1) * LANES] = wide[pl.ds(j, rows, stride=parts), :].astype(
            out_ref.dtype
        )


def unpack(arrived, which, width):
    rings, plane, _, tall, _ = arrived.shape
    parts = width // LANES
    rows = rings * plane * tall // parts
    block = 8
    step = rows * block // plane
    return pl.pallas_call(
        unpack_kernel,
        grid=(plane // block,),
        out_shape=jax.ShapeDtypeStruct((rows, width), jnp.bfloat16),
        in_specs=[
            pl.BlockSpec((rings, block, 1, tall, LANES), lambda i: (0, i, which, 0, 0)),
        ],
        out_specs=pl.BlockSpec((step, width), lambda i: (i, 0)),
        scratch_shapes=[pltpu.VMEM((step * parts, LANES), jnp.float32)],
        compiler_params=pltpu.CompilerParams(vmem_limit_bytes=24 * MIB),
        cost_estimate=pl.CostEstimate(flops=0, bytes_accessed=6 * MIB, transcendentals=0),
    )(arrived)


def over(axes, sizes, move):
    pairs = []
    total = 1
    for n in sizes:
        total *= n
    for i in range(total):
        at, rest = [], i
        for n in reversed(sizes):
            at.append(rest % n)
            rest //= n
        to = move(tuple(reversed(at)))
        if to is not None:
            j = 0
            for n, c in zip(sizes, to, strict=True):
                j = j * n + c
            pairs.append((i, j))
    return pairs


def swap_low(block):
    return lax.ppermute(block, "xlo", [(0, 1), (1, 0)])


def swap_high(block):
    route = over(("xlo", "xhi"), (2, 2), lambda c: (1 - c[0], 1 - c[1]))
    return lax.ppermute(block, ("xlo", "xhi"), route)


def dot(a, b, over_a=1, over_b=0):
    return lax.dot_general(
        a, b, (((over_a,), (over_b,)), ((), ())), preferred_element_type=jnp.float32
    )


def on_device(tokens, cotangent, combine, route, anchors, w_gate, w_up, w_down):
    token_count, width = tokens.shape
    top = route.shape[1]
    rings = lax.axis_size(("xlo", "xhi"))
    plane = lax.axis_size(PLANE)
    slots = rings * plane
    row_count = token_count * top
    pair_rows = 3 * row_count // (2 * slots)
    parts = width // LANES
    half = width // 2
    group = lax.axis_index("xlo")
    ring_at = lax.axis_index(("xlo", "xhi"))
    ep_index = lax.axis_index(("xhi",) + PLANE)
    ep_count = lax.axis_size(("xhi",) + PLANE)

    target = route.reshape(row_count)
    marks = (target[:, None] == jnp.arange(slots, dtype=jnp.int32)[None, :]).astype(jnp.int32)
    rank = jnp.sum(jnp.cumsum(marks, axis=0) * marks, axis=1) - 1
    packed = pack(
        target * (2 * pair_rows) + rank, combine.reshape(row_count), tokens, cotangent, slots, pair_rows
    )
    arrived = lax.all_to_all(
        packed.reshape(slots, 2 * pair_rows * parts, LANES), AXES, 0, 0, tiled=True
    ).reshape(rings, plane, 2, pair_rows * parts, LANES)

    ring_of = jnp.full((token_count, 1), ring_at, jnp.float32)
    facts = jnp.concatenate(
        [target.reshape(token_count, top).astype(jnp.float32), rank.reshape(token_count, top).astype(jnp.float32), combine, ring_of],
        axis=1,
    )
    near = jnp.concatenate([facts, swap_low(facts)])
    facts = jnp.concatenate([swap_high(near), near])
    slot_of = facts[:, :top].astype(jnp.int32) - ring_at * plane
    rank_of = facts[:, top : 2 * top].astype(jnp.int32)
    weight_of = facts[:, 2 * top : 3 * top]
    ring_of = facts[:, 3 * top :].astype(jnp.int32)
    inside = (slot_of >= 0) & (slot_of < plane)
    column = jnp.where(inside, (slot_of * rings + ring_of) * pair_rows + rank_of, -1)
    places = jnp.arange(slots * pair_rows, dtype=jnp.int32)[None, :]
    coarse_of = lax.reduce_precision(weight_of, 8, 7)
    fine_of = weight_of - coarse_of
    ones, coarse, fine = 0.0, 0.0, 0.0
    for k in range(top):
        hit = column[:, k : k + 1] == places
        ones = ones + jnp.where(hit, 1.0, 0.0)
        coarse = coarse + jnp.where(hit, coarse_of[:, k : k + 1], 0.0)
        fine = fine + jnp.where(hit, fine_of[:, k : k + 1], 0.0)
    ones = ones.astype(jnp.bfloat16)
    coarse = coarse.astype(jnp.bfloat16)
    fine = fine.astype(jnp.bfloat16)

    gate_weight, up_weight, down_weight = w_gate[0], w_up[0], w_down[0]
    inputs = unpack(arrived, 0, width)
    gate = dot(inputs, gate_weight)
    up_proj = dot(inputs, up_weight)
    sigma = jax.nn.sigmoid(gate)
    active = gate * sigma
    hidden = (active * up_proj).astype(jnp.bfloat16)
    expert_out = dot(hidden, down_weight).astype(jnp.bfloat16)
    cot_in = unpack(arrived, 1, width)
    back = dot(cot_in, down_weight, 1, 1)
    d_gate = (back * up_proj * sigma * (1.0 + gate * (1.0 - sigma))).astype(jnp.bfloat16)
    d_up = (back * active).astype(jnp.bfloat16)

    def to_plane(rows):
        chunks = rows.reshape(plane, rings * pair_rows, width)
        return lax.all_to_all(chunks, PLANE, 0, 0, tiled=True).reshape(slots * pair_rows, width)

    def home(sums):
        far = swap_high(sums(slice(0, 2 * token_count)).astype(jnp.bfloat16)).astype(jnp.float32)
        mine = sums(slice(2 * token_count, 3 * token_count)) + far[:token_count]
        others = sums(slice(3 * token_count, 4 * token_count)) + far[token_count:]
        return (mine + swap_low(others.astype(jnp.bfloat16)).astype(jnp.float32)).astype(jnp.bfloat16)

    out_rows = to_plane(expert_out)

    def halves_of(array, which):
        return lax.dynamic_slice_in_dim(array, which * half, half, 1)

    away_in, away_cot = halves_of(inputs, 1 - group), halves_of(cot_in, 1 - group)
    here_in, here_cot = halves_of(inputs, group), halves_of(cot_in, group)
    send = [
        dot(hidden, away_cot, 0, 0).astype(jnp.bfloat16),
        dot(away_in, d_gate, 0, 0).astype(jnp.bfloat16),
        dot(away_in, d_up, 0, 0).astype(jnp.bfloat16),
    ]
    received = [swap_low(s) for s in send]
    row_grad = (dot(d_gate, gate_weight, 1, 1) + dot(d_up, up_weight, 1, 1)).astype(jnp.bfloat16)
    grad_rows = to_plane(row_grad)
    kept = [
        dot(hidden, here_cot, 0, 0).astype(jnp.bfloat16),
        dot(here_in, d_gate, 0, 0).astype(jnp.bfloat16),
        dot(here_in, d_up, 0, 0).astype(jnp.bfloat16),
    ]
    is_anchor = anchors[ep_index] == ep_index
    beside = jnp.minimum(ep_index + 1, ep_count - 1)
    joins = (ep_index + 1 < ep_count) & (anchors[beside] == ep_index)
    totals = []
    for keep, got in zip(kept, received, strict=True):
        passed = lax.ppermute(jnp.where(group == 0, got, keep), "core", [(1, 0)]).astype(jnp.float32)
        keep, got = keep.astype(jnp.float32), got.astype(jnp.float32)
        first = jnp.where(group == 0, keep, got)
        second = jnp.where(group == 0, got, keep)
        totals.append(first + jnp.where(is_anchor, second, 0.0) + jnp.where(joins, passed, 0.0))

    mixed = home(lambda s: dot(coarse[s], out_rows) + dot(fine[s], out_rows))
    input_grad = home(lambda s: dot(ones[s], grad_rows))
    grad_down, grad_gate, grad_up = totals
    return (mixed, input_grad, grad_gate[None], grad_up[None], grad_down[None])


def solution(mesh):
    fine = Mesh(mesh.devices.reshape(2, 2, 4, 4, 2), AXES)
    rows = P(AXES, None)
    slot = P(AXES, None, None)
    experts = ("xhi",) + PLANE
    return jax.shard_map(
        on_device,
        mesh=fine,
        in_specs=(rows, rows, rows, rows, P(), slot, slot, slot),
        out_specs=(
            rows,
            rows,
            P(experts, "xlo", None),
            P(experts, "xlo", None),
            P(experts, None, "xlo"),
        ),
        check_vma=False,
    )
```

time: 570 us -> 331 us (0.58)
  the two profiles are of different devices: /device:TPU:4 before, /device:TPU:1 now
where the time goes in v1:
time: 331 us; the launch traced here: 330 us
  waiting for transfers between devices  166 us (50%)
  matrix products  69.5 us (21%)
  starting transfers between devices  47.7 us (14%)
  other arithmetic  20.9 us (6%)
  Pallas kernels  14.5 us (4%)
  local copies, waits for them, and re-layouts  8.22 us (2%)
    ppermute x6, waiting for transfers between devices, swap_low(): return lax.ppermute(block, 'xlo', [(0, 1), (1, 0)])  122 us
    dot_general x21, matrix products, dot(): lax.dot_general(a, b, (((over_a,), (over_b,)), ((), ())), preferred_eleme...  69.5 us
    all_to_all x2, waiting for transfers between devices, to_plane(): lax.all_to_all(chunks, PLANE, 0, 0, tiled=True)  22.3 us
    ppermute x3, waiting for transfers between devices, swap_high(): return lax.ppermute(block, ('xlo', 'xhi'), route)  18.9 us
    all_to_all x2, starting transfers between devices, to_plane(): lax.all_to_all(chunks, PLANE, 0, 0, tiled=True)  14.8 us
    broadcast_in_dim x3, other arithmetic, on_device(): return (mixed, input_grad, grad_gate[None], grad_up[None], grad_down[None])  13.7 us
    ppermute x3, starting transfers between devices, on_device(): lax.ppermute(jnp.where(group == 0, got, keep), 'core', [(1, 0)])  13.3 us
    all_to_all x1, starting transfers between devices, on_device(): lax.all_to_all(packed.reshape(slots, 2 * pair_rows * parts, LANES), AXES,...  11.9 us
  transfers between devices with their start and end apart: 15, of which 9 were waited for; matrix products, arithmetic and copies ran while one was open for 23% of the time, Pallas kernels for 0%

profile of v1, /device:TPU:1, one launch (start us, length us, event | category | flops | bytes accessed | tf_op | source)
XLA Modules:
  0.0 329.6 jit_solution(12688027933989014385)
XLA Ops:
  0.6 0.9 copy.27
  1.6 0.1 eq.106
  1.7 0.1 eq.102
  1.8 0.1 copy.29
  1.9 0.2 fusion.41
  2.2 0.2 fusion.40
  2.5 0.8 copy.32
  3.3 0.1 reshape.55.weight
  3.4 1.0 copy-done.8
  4.4 1.0 copy-done.9
  5.5 4.6 %shard_map.119 = bf16[24576,128]{1,0:T(8,128)(2,1)S(1)} custom-call(s32[512]{0:T(512)S(1)} %get-tuple-element.26.dest, f32[512]{0:T(512)S(1)} %reshape.55.weight, bf16[128,2048]{1,0:T(8,128)(2,1)S(1)} %copy-done.8, bf16[128,2048]{1,0:T(8,128)(2,1)S(1)} %copy-done.9), custom_call_target="tpu_custom_call" | custom-call | bytes 12582912 | tf_op jit(solution)/shard_map/pallas_call | solution.py:49
  10.1 2.7 copy-done.2
  12.8 11.9 %all-to-all-start = ((bf16[128,192,128]{2,1,0:T(8,128)(2,1)}), bf16[128,192,128]{2,1,0:T(8,128)(2,1)}, u32[]{:S(2)}, u32[]{:S(2)}) async-start(bf16[128,192,128]{2,1,0:T(8,128)(2,1)} %bitcast.76), calls=%async_computation | async-start | bytes 12582912 | tf_op jit(solution)/shard_map/all_to_all | solution.py:149
  25.0 1.5 collective-permute-start
  26.4 68.8 %collective-permute-done = f32[128,13]{0,1:T(8,128)S(1)} collective-permute-done((f32[128,13]{0,1:T(8,128)S(1)}, f32[128,13]{0,1:T(8,128)S(1)}, u32[]{:S(2)}, u32[]{:S(2)}) %collective-permute-start) | collective-permute-done | bytes 6688 | tf_op jit(solution)/shard_map/ppermute | solution.py:114
  95.2 1.9 collective-permute-start.1
  97.2 0.6 fusion.70
  99.0 0.5 collective-permute-done.1
  99.6 3.1 all-to-all-done
  102.7 4.6 %shard_map.120 = bf16[768,2048]{1,0:T(8,128)(2,1)S(1)} custom-call(bf16[4,32,2,96,128]{4,3,2,1,0:T(8,128)(2,1)} %bitcast.13.in_ref), custom_call_target="tpu_custom_call" | custom-call | bytes 6291456 | tf_op jit(solution)/shard_map/pallas_call | solution.py:80
  107.3 5.3 %shard_map.121 = bf16[768,2048]{1,0:T(8,128)(2,1)S(1)} custom-call(bf16[4,32,2,96,128]{4,3,2,1,0:T(8,128)(2,1)} %bitcast.13.in_ref), custom_call_target="tpu_custom_call" | custom-call | bytes 6291456 | tf_op jit(solution)/shard_map/pallas_call | solution.py:80
  112.7 2.6 fusion.20
  115.3 0.4 copy-done.21
  115.7 2.6 fusion.16
  118.4 4.7 %multiply_convert_fusion = (bf16[768,768]{1,0:T(8,128)(2,1)}, bf16[768,768]{1,0:T(8,128)(2,1)}, bf16[768,768]{1,0:T(8,128)(2,1)S(1)}) fusion(f32[768,768]{1,0:T(8,128)S(1)} %fusion.20, f32[768,768]{1,0:T(8,128)S(1)} %fusion.16, bf16[768,2048]{1,0:T(8,128)(2,1)S(1)} %shard_map.121, bf16[1,768,2048]{2,1,0:T(8,128)(2,1)S(1)} %copy-done), kind=kOutput, calls=%fused_computation.35 | convolution fusion | flops 2424766464 | bytes 14548992 | tf_op jit(solution)/shard_map/dot_general | solution.py:123
  123.1 4.0 %convolution_convert_fusion = bf16[768,2048]{1,0:T(8,128)(2,1)} fusion(bf16[768,768]{1,0:T(8,128)(2,1)S(1)} %get-tuple-element.9, bf16[1,768,2048]{2,1,0:T(8,128)(2,1)S(1)} %copy-done), kind=kOutput, calls=%fused_computation.7 | convolution fusion | flops 2417491968 | bytes 7471104 | tf_op jit(solution)/shard_map/dot_general | solution.py:123
  127.1 9.8 %all-to-all-start.1 = ((bf16[32,24,2048]{2,1,0:T(8,128)(2,1)}), bf16[32,24,2048]{2,1,0:T(8,128)(2,1)}, u32[]{:S(2)}, u32[]{:S(2)}) async-start(bf16[32,24,2048]{2,1,0:T(8,128)(2,1)} %bitcast.78), calls=%async_computation.1 | async-start | bytes 6291456 | tf_op jit(solution)/shard_map/all_to_all | solution.py:194
  136.9 3.9 %convolution_convert_fusion.6 = bf16[1024,768]{1,0:T(8,128)(2,1)} fusion(bf16[768,768]{1,0:T(8,128)(2,1)} %get-tuple-element.8, bf16[768,2048]{1,0:T(8,128)(2,1)S(1)} %copy-done.6, s32[]{:T(128)S(6)} %select_n.155), kind=kOutput, calls=%fused_computation.44 | convolution fusion | flops 1208745984 | bytes 4325380 | tf_op jit(solution)/shard_map/dot_general | solution.py:123
  140.9 2.6 convolution_convert_fusion.4
  143.5 1.4 collective-permute-start.8
  144.9 2.6 fusion.18
  147.6 2.7 convolution_convert_fusion.2
  150.3 4.0 %add_convert_fusion = bf16[768,2048]{1,0:T(8,128)(2,1)} fusion(f32[768,2048]{1,0:T(8,128)S(1)} %fusion.18, bf16[768,768]{1,0:T(8,128)(2,1)S(1)} %copy-done.26, bf16[1,2048,768]{2,1,0:T(8,128)(2,1)S(1)} %copy-done.22), kind=kOutput, calls=%fused_computation | convolution fusion | flops 2419064832 | bytes 13762560 | tf_op jit(solution)/shard_map/dot_general | solution.py:123
  154.3 22.3 %all-to-all-done.1 = bf16[32,24,2048]{2,1,0:T(8,128)(2,1)} async-done(((bf16[32,24,2048]{2,1,0:T(8,128)(2,1)}), bf16[32,24,2048]{2,1,0:T(8,128)(2,1)}, u32[]{:S(2)}, u32[]{:S(2)}) %all-to-all-start.1) | async-done | bytes 3145760 | tf_op jit(solution)/shard_map/all_to_all | solution.py:194
  176.6 5.0 %all-to-all-start.2 = ((bf16[32,24,2048]{2,1,0:T(8,128)(2,1)}), bf16[32,24,2048]{2,1,0:T(8,128)(2,1)}, u32[]{:S(2)}, u32[]{:S(2)}) async-start(bf16[32,24,2048]{2,1,0:T(8,128)(2,1)} %bitcast.77), calls=%async_computation.2 | async-start | bytes 6291456 | tf_op jit(solution)/shard_map/all_to_all | solution.py:194
  181.7 2.9 add_convert_fusion.1
  184.6 5.3 %broadcast_select_fusion.1 = (bf16[1024,768]{1,0:T(8,128)(2,1)}, bf16[1024,768]{1,0:T(8,128)(2,1)}) fusion(bf16[1024,768]{1,0:T(8,128)(2,1)} %collective-permute-done.6, pred[]{:T(512)S(6)} %eq.126, bf16[768,768]{1,0:T(8,128)(2,1)S(1)} %copy-done.29, bf16[768,2048]{1,0:T(8,128)(2,1)} %copy-done.5, s32[]{:T(128)S(6)} %select_n.154), kind=kOutput, calls=%fused_computation.56 | convolution fusion | flops 1209532416 | bytes 7471109 | tf_op jit(solution)/shard_map/dot_general | solution.py:123
  189.9 3.5 %collective-permute-start.7 = (bf16[1024,768]{1,0:T(8,128)(2,1)}, bf16[1024,768]{1,0:T(8,128)(2,1)}, u32[]{:S(2)}, u32[]{:S(2)}) collective-permute-start(bf16[1024,768]{1,0:T(8,128)(2,1)} %get-tuple-element.29), channel_id=1, source_target_pairs={{1,0},{3,2},{5,4},{7,6},{9,8},{11,10},{13,12},{15,14},{17,16},{19,... | collective-permute-start | bytes 4718600 | tf_op jit(solution)/shard_map/ppermute | solution.py:227
  193.4 16.9 %collective-permute-done.8 = bf16[1024,768]{1,0:T(8,128)(2,1)} collective-permute-done((bf16[1024,768]{1,0:T(8,128)(2,1)}, bf16[1024,768]{1,0:T(8,128)(2,1)}, u32[]{:S(2)}, u32[]{:S(2)}) %collective-permute-start.8) | collective-permute-done | bytes 1572896 | tf_op jit(solution)/shard_map/ppermute | solution.py:114
  210.4 4.5 %broadcast_select_fusion.2 = (bf16[1024,768]{1,0:T(8,128)(2,1)}, bf16[1024,768]{1,0:T(8,128)(2,1)}) fusion(bf16[1024,768]{1,0:T(8,128)(2,1)} %collective-permute-done.8, pred[]{:T(512)S(6)} %eq.126, bf16[768,768]{1,0:T(8,128)(2,1)S(1)} %copy-done.27, bf16[768,2048]{1,0:T(8,128)(2,1)S(1)} %copy-done.7, s32[]{:T(128)S(6)} %select_n.154), kind=kOutput, calls=%fused_computation.57 | convolution fusion | flops 1209532416 | bytes 7471109 | tf_op jit(solution)/shard_map/dot_general | solution.py:123
  214.9 5.3 %collective-permute-start.9 = (bf16[1024,768]{1,0:T(8,128)(2,1)}, bf16[1024,768]{1,0:T(8,128)(2,1)}, u32[]{:S(2)}, u32[]{:S(2)}) collective-permute-start(bf16[1024,768]{1,0:T(8,128)(2,1)} %get-tuple-element.31), channel_id=1, source_target_pairs={{1,0},{3,2},{5,4},{7,6},{9,8},{11,10},{13,12},{15,14},{17,16},{19,... | collective-permute-start | bytes 4718600 | tf_op jit(solution)/shard_map/ppermute | solution.py:227
  220.2 23.9 %collective-permute-done.10 = bf16[768,1024]{1,0:T(8,128)(2,1)} collective-permute-done((bf16[768,1024]{1,0:T(8,128)(2,1)}, bf16[768,1024]{1,0:T(8,128)(2,1)}, u32[]{:S(2)}, u32[]{:S(2)}) %collective-permute-start.10) | collective-permute-done | bytes 1572896 | tf_op jit(solution)/shard_map/ppermute | solution.py:114
  244.1 4.5 %broadcast_select_fusion = (bf16[768,1024]{1,0:T(8,128)(2,1)}, bf16[768,1024]{1,0:T(8,128)(2,1)}) fusion(bf16[768,1024]{1,0:T(8,128)(2,1)} %collective-permute-done.10, pred[]{:T(512)S(6)} %eq.126, bf16[768,768]{1,0:T(8,128)(2,1)S(1)} %copy-done.25, bf16[768,2048]{1,0:T(8,128)(2,1)S(1)} %copy-done.4, s32[]{:T(128)S(6)} %select_n.154), kind=kOutput, calls=%fused_computation.55 | convolution fusion | flops 1209532416 | bytes 7471109 | tf_op jit(solution)/shard_map/dot_general | solution.py:123
  248.6 4.5 %collective-permute-start.11 = (bf16[768,1024]{1,0:T(8,128)(2,1)}, bf16[768,1024]{1,0:T(8,128)(2,1)}, u32[]{:S(2)}, u32[]{:S(2)}) collective-permute-start(bf16[768,1024]{1,0:T(8,128)(2,1)} %get-tuple-element.33), channel_id=1, source_target_pairs={{1,0},{3,2},{5,4},{7,6},{9,8},{11,10},{13,12},{15,14},{17,16},{19,... | collective-permute-start | bytes 4718600 | tf_op jit(solution)/shard_map/ppermute | solution.py:227
  253.0 2.9 fusion.38
  256.0 4.0 %fusion.22 = bf16[256,2048]{1,0:T(8,128)(2,1)} fusion(f32[256,2048]{1,0:T(8,128)S(1)} %fusion.38, bf16[768,2048]{1,0:T(8,128)(2,1)} %bitcast.18, bf16[512,768]{1,0:T(8,128)(2,1)S(1)} %get-tuple-element.11), kind=kOutput, calls=%fused_computation.31 | convolution fusion | flops 806354944 | bytes 6684672 | tf_op jit(solution)/shard_map/dot_general | solution.py:123
  259.9 2.5 fusion.55
  262.4 2.5 fusion.52
  265.1 3.1 convolution_convert_fusion.1
  268.2 2.5 convolution_add_fusion.2
  270.7 2.6 fusion.47
  273.3 2.7 collective-permute-start.4
  276.1 4.6 %fusion.2 = f32[1,1024,768]{2,1,0:T(8,128)} fusion(bf16[1024,768]{1,0:T(8,128)(2,1)} %collective-permute-done.6, bf16[1024,768]{1,0:T(8,128)(2,1)S(1)} %copy-done.14, bf16[1024,768]{1,0:T(8,128)(2,1)} %collective-permute-done.7, pred[]{:T(512)S(6)} %and.12, pred[]{:T(512)S(6)} %eq.127, pred[]{:T(512)S(6)} %eq.126), kind=kLoop, calls=%fused_computation.10 | loop fusion | flops 7077888 | bytes 7864323 | tf_op jit(solution)/shard_map/broadcast_in_dim | solution.py:236
  280.7 4.5 %fusion.6 = f32[1,1024,768]{2,1,0:T(8,128)} fusion(bf16[1024,768]{1,0:T(8,128)(2,1)} %collective-permute-done.8, bf16[1024,768]{1,0:T(8,128)(2,1)S(1)} %copy-done.15, bf16[1024,768]{1,0:T(8,128)(2,1)} %collective-permute-done.9, pred[]{:T(512)S(6)} %and.12, pred[]{:T(512)S(6)} %eq.127, pred[]{:T(512)S(6)} %eq.126), kind=kLoop, calls=%fused_computation.14 | loop fusion | flops 7077888 | bytes 7864323 | tf_op jit(solution)/shard_map/broadcast_in_dim | solution.py:236
  285.1 6.6 %collective-permute-done.2 = bf16[256,2048]{1,0:T(8,128)(2,1)} collective-permute-done((bf16[256,2048]{1,0:T(8,128)(2,1)}, bf16[256,2048]{1,0:T(8,128)(2,1)}, u32[]{:S(2)}, u32[]{:S(2)}) %collective-permute-start.2) | collective-permute-done | bytes 1048608 | tf_op jit(solution)/shard_map/ppermute | solution.py:119
  291.7 1.5 convert_element_type.138
  293.2 2.7 fusion.33
  296.0 4.6 %fusion.10 = f32[1,768,1024]{2,1,0:T(8,128)} fusion(bf16[768,1024]{1,0:T(8,128)(2,1)} %collective-permute-done.10, bf16[768,1024]{1,0:T(8,128)(2,1)S(1)} %copy-done.13, bf16[768,1024]{1,0:T(8,128)(2,1)} %collective-permute-done.11, pred[]{:T(512)S(6)} %and.12, pred[]{:T(512)S(6)} %eq.127, pred[]{:T(512)S(6)} %eq.126), kind=kLoop, calls=%fused_computation.18 | loop fusion | flops 7077888 | bytes 7864323 | tf_op jit(solution)/shard_map/broadcast_in_dim | solution.py:236
  300.6 11.8 %collective-permute-done.4 = bf16[256,2048]{1,0:T(8,128)(2,1)S(1)} collective-permute-done((bf16[256,2048]{1,0:T(8,128)(2,1)S(1)}, bf16[256,2048]{1,0:T(8,128)(2,1)S(1)}, u32[]{:S(2)}, u32[]{:S(2)}) %collective-permute-start.4) | collective-permute-done | bytes 1048608 | tf_op jit(solution)/shard_map/ppermute | solution.py:119
  312.4 0.2 convert_element_type.147
  312.7 2.5 fusion.30
  315.3 1.0 fusion.35
  316.3 12.3 %collective-permute-done.5 = bf16[128,2048]{1,0:T(8,128)(2,1)S(1)} collective-permute-done((bf16[128,2048]{1,0:T(8,128)(2,1)S(1)}, bf16[128,2048]{1,0:T(8,128)(2,1)S(1)}, u32[]{:S(2)}, u32[]{:S(2)}) %collective-permute-start.5) | collective-permute-done | bytes 524320 | tf_op jit(solution)/shard_map/ppermute | solution.py:114
  328.6 1.0 fusion.32
  (88 shorter events, 0.8 us)
Async XLA Ops:
  0.6 117.7 %copy-start = (bf16[1,768,2048]{2,1,0:T(8,128)(2,1)S(1)}, bf16[1,768,2048]{2,1,0:T(8,128)(2,1)}, u32[]{:S(2)}) copy-start(bf16[1,768,2048]{2,1,0:T(8,128)(2,1)} %param.15) | copy-start | bytes 9437188
  3.4 1.0 copy-start.8
  4.4 1.0 copy-start.9
  10.1 2.7 copy-start.2
  12.8 11.9 %copy-start.17 = (s32[128,4]{0,1:T(4,128)S(1)}, s32[128,4]{0,1:T(4,128)}, u32[]{:S(2)}) copy-start(s32[128,4]{0,1:T(4,128)} %param.11) | copy-start | bytes 6148
  12.8 12.1 %copy-start.16 = (f32[128,4]{0,1:T(4,128)S(1)}, f32[128,4]{0,1:T(4,128)}, u32[]{:S(2)}) copy-start(f32[128,4]{0,1:T(4,128)} %param.10) | copy-start | bytes 6148
  12.8 84.3 %copy-start.18 = (s32[64]{0:T(128)S(1)}, s32[64]{0:T(128)}, u32[]{:S(2)}) copy-start(s32[64]{0:T(128)} %param.12) | copy-start | bytes 772
  12.8 89.9 %all-to-all-start = ((bf16[128,192,128]{2,1,0:T(8,128)(2,1)}), bf16[128,192,128]{2,1,0:T(8,128)(2,1)}, u32[]{:S(2)}, u32[]{:S(2)}) async-start(bf16[128,192,128]{2,1,0:T(8,128)(2,1)} %bitcast.76), calls=%async_computation | async-start | bytes 12582912 | tf_op jit(solution)/shard_map/all_to_all | solution.py:149
  25.0 70.3 %collective-permute-start = (f32[128,13]{0,1:T(8,128)S(1)}, f32[128,13]{0,1:T(8,128)S(1)}, u32[]{:S(2)}, u32[]{:S(2)}) collective-permute-start(f32[128,13]{0,1:T(8,128)S(1)} %pad_maximum_fusion.3), channel_id=1, source_target_pairs={{0,64},{64,0},{1,65},{65,1},{2,66},{66,2},{3,67},{67,3},{4,68},{68... | collective-permute-start | bytes 19976 | tf_op jit(solution)/shard_map/ppermute | solution.py:114
  95.2 4.3 %collective-permute-start.1 = (f32[256,13]{0,1:T(8,128)S(1)}, f32[256,13]{0,1:T(8,128)S(1)}, u32[]{:S(2)}, u32[]{:S(2)}) collective-permute-start(f32[256,13]{0,1:T(8,128)S(1)} %pad_maximum_fusion.1), channel_id=1, source_target_pairs={{0,96},{32,64},{64,32},{96,0},{1,97},{33,65},{65,33},{97,1},{2,98}... | collective-permute-start | bytes 39944 | tf_op jit(solution)/shard_map/ppermute | solution.py:119
  107.3 8.1 %copy-start.5 = (bf16[768,2048]{1,0:T(8,128)(2,1)}, bf16[768,2048]{1,0:T(8,128)(2,1)S(1)}, u32[]{:S(2)}) copy-start(bf16[768,2048]{1,0:T(8,128)(2,1)S(1)} %shard_map.120) | copy-start | bytes 9437188
  107.3 5.4 %copy-start.19 = (bf16[1,2048,768]{2,1,0:T(8,128)(2,1)S(1)}, bf16[1,2048,768]{2,1,0:T(8,128)(2,1)}, u32[]{:S(2)}) copy-start(bf16[1,2048,768]{2,1,0:T(8,128)(2,1)} %param.13) | copy-start | bytes 9437188
  112.7 5.7 %copy-start.3 = (bf16[768,2048]{1,0:T(8,128)(2,1)}, bf16[768,2048]{1,0:T(8,128)(2,1)S(1)}, u32[]{:S(2)}) copy-start(bf16[768,2048]{1,0:T(8,128)(2,1)S(1)} %shard_map.121) | copy-start | bytes 9437188
  112.7 3.0 copy-start.21
  123.1 4.0 %copy-start.23 = (bf16[768,768]{1,0:T(8,128)(2,1)}, bf16[768,768]{1,0:T(8,128)(2,1)S(1)}, u32[]{:S(2)}) copy-start(bf16[768,768]{1,0:T(8,128)(2,1)S(1)} %get-tuple-element.9) | copy-start | bytes 3538948
  127.1 9.8 %copy-start.6 = (bf16[768,2048]{1,0:T(8,128)(2,1)S(1)}, bf16[768,2048]{1,0:T(8,128)(2,1)}, u32[]{:S(2)}) copy-start(bf16[768,2048]{1,0:T(8,128)(2,1)} %copy-done.5) | copy-start | bytes 9437188
  127.1 49.6 %all-to-all-start.1 = ((bf16[32,24,2048]{2,1,0:T(8,128)(2,1)}), bf16[32,24,2048]{2,1,0:T(8,128)(2,1)}, u32[]{:S(2)}, u32[]{:S(2)}) async-start(bf16[32,24,2048]{2,1,0:T(8,128)(2,1)} %bitcast.78), calls=%async_computation.1 | async-start | bytes 6291456 | tf_op jit(solution)/shard_map/all_to_all | solution.py:194
  136.9 4.0 %copy-start.26 = (bf16[768,768]{1,0:T(8,128)(2,1)S(1)}, bf16[768,768]{1,0:T(8,128)(2,1)}, u32[]{:S(2)}) copy-start(bf16[768,768]{1,0:T(8,128)(2,1)} %get-tuple-element.7) | copy-start | bytes 3538948
  140.8 43.8 %collective-permute-start.6 = (bf16[1024,768]{1,0:T(8,128)(2,1)}, bf16[1024,768]{1,0:T(8,128)(2,1)}, u32[]{:S(2)}, u32[]{:S(2)}) collective-permute-start(bf16[1024,768]{1,0:T(8,128)(2,1)} %convolution_convert_fusion.6), channel_id=1, source_target_pairs={{0,64},{64,0},{1,65},{65,1},{2,66},{66,2},{3,67},{67,3},{4,68},{68... | collective-permute-start | bytes 4718600 | tf_op jit(solution)/shard_map/ppermute | solution.py:114
  140.8 4.1 %copy-start.20 = (bf16[1,2048,768]{2,1,0:T(8,128)(2,1)S(1)}, bf16[1,2048,768]{2,1,0:T(8,128)(2,1)}, u32[]{:S(2)}) copy-start(bf16[1,2048,768]{2,1,0:T(8,128)(2,1)} %param.13) | copy-start | bytes 9437188
  140.8 4.1 %copy-start.28 = (bf16[768,768]{1,0:T(8,128)(2,1)S(1)}, bf16[768,768]{1,0:T(8,128)(2,1)}, u32[]{:S(2)}) copy-start(bf16[768,768]{1,0:T(8,128)(2,1)} %get-tuple-element.8) | copy-start | bytes 3538948
  143.5 4.1 %copy-start.4 = (bf16[768,2048]{1,0:T(8,128)(2,1)S(1)}, bf16[768,2048]{1,0:T(8,128)(2,1)}, u32[]{:S(2)}) copy-start(bf16[768,2048]{1,0:T(8,128)(2,1)} %copy-done.3) | copy-start | bytes 9437188
  143.5 4.1 %copy-start.24 = (bf16[768,768]{1,0:T(8,128)(2,1)S(1)}, bf16[768,768]{1,0:T(8,128)(2,1)}, u32[]{:S(2)}) copy-start(bf16[768,768]{1,0:T(8,128)(2,1)} %copy-done.23) | copy-start | bytes 3538948
  143.5 66.9 %collective-permute-start.8 = (bf16[1024,768]{1,0:T(8,128)(2,1)}, bf16[1024,768]{1,0:T(8,128)(2,1)}, u32[]{:S(2)}, u32[]{:S(2)}) collective-permute-start(bf16[1024,768]{1,0:T(8,128)(2,1)} %convolution_convert_fusion.4), channel_id=1, source_target_pairs={{0,64},{64,0},{1,65},{65,1},{2,66},{66,2},{3,67},{67,3},{4,68},{68... | collective-permute-start | bytes 4718600 | tf_op jit(solution)/shard_map/ppermute | solution.py:114
  147.6 2.7 copy-start.22
  150.3 93.8 %collective-permute-start.10 = (bf16[768,1024]{1,0:T(8,128)(2,1)}, bf16[768,1024]{1,0:T(8,128)(2,1)}, u32[]{:S(2)}, u32[]{:S(2)}) collective-permute-start(bf16[768,1024]{1,0:T(8,128)(2,1)} %convolution_convert_fusion.2), channel_id=1, source_target_pairs={{0,64},{64,0},{1,65},{65,1},{2,66},{66,2},{3,67},{67,3},{4,68},{68... | collective-permute-start | bytes 4718600 | tf_op jit(solution)/shard_map/ppermute | solution.py:114
  176.6 88.4 %all-to-all-start.2 = ((bf16[32,24,2048]{2,1,0:T(8,128)(2,1)}), bf16[32,24,2048]{2,1,0:T(8,128)(2,1)}, u32[]{:S(2)}, u32[]{:S(2)}) async-start(bf16[32,24,2048]{2,1,0:T(8,128)(2,1)} %bitcast.77), calls=%async_computation.2 | async-start | bytes 6291456 | tf_op jit(solution)/shard_map/all_to_all | solution.py:194
  181.6 3.0 copy-start.29
  184.6 71.4 %copy-start.10 = (bf16[512,768]{1,0:T(8,128)(2,1)}, bf16[512,768]{1,0:T(8,128)(2,1)S(1)}, u32[]{:S(2)}) copy-start(bf16[512,768]{1,0:T(8,128)(2,1)S(1)} %get-tuple-element.11) | copy-start | bytes 2359300
  184.6 25.8 %copy-start.7 = (bf16[768,2048]{1,0:T(8,128)(2,1)S(1)}, bf16[768,2048]{1,0:T(8,128)(2,1)}, u32[]{:S(2)}) copy-start(bf16[768,2048]{1,0:T(8,128)(2,1)} %copy-done.5) | copy-start | bytes 9437188
  184.6 25.8 %copy-start.27 = (bf16[768,768]{1,0:T(8,128)(2,1)S(1)}, bf16[768,768]{1,0:T(8,128)(2,1)}, u32[]{:S(2)}) copy-start(bf16[768,768]{1,0:T(8,128)(2,1)} %get-tuple-element.7) | copy-start | bytes 3538948
  189.9 54.1 %copy-start.25 = (bf16[768,768]{1,0:T(8,128)(2,1)S(1)}, bf16[768,768]{1,0:T(8,128)(2,1)}, u32[]{:S(2)}) copy-start(bf16[768,768]{1,0:T(8,128)(2,1)} %copy-done.23) | copy-start | bytes 3538948
  189.9 86.1 %collective-permute-start.7 = (bf16[1024,768]{1,0:T(8,128)(2,1)}, bf16[1024,768]{1,0:T(8,128)(2,1)}, u32[]{:S(2)}, u32[]{:S(2)}) collective-permute-start(bf16[1024,768]{1,0:T(8,128)(2,1)} %get-tuple-element.29), channel_id=1, source_target_pairs={{1,0},{3,2},{5,4},{7,6},{9,8},{11,10},{13,12},{15,14},{17,16},{19,... | collective-permute-start | bytes 4718600 | tf_op jit(solution)/shard_map/ppermute | solution.py:227
  214.9 65.8 %collective-permute-start.9 = (bf16[1024,768]{1,0:T(8,128)(2,1)}, bf16[1024,768]{1,0:T(8,128)(2,1)}, u32[]{:S(2)}, u32[]{:S(2)}) collective-permute-start(bf16[1024,768]{1,0:T(8,128)(2,1)} %get-tuple-element.31), channel_id=1, source_target_pairs={{1,0},{3,2},{5,4},{7,6},{9,8},{11,10},{13,12},{15,14},{17,16},{19,... | collective-permute-start | bytes 4718600 | tf_op jit(solution)/shard_map/ppermute | solution.py:227
  248.6 47.4 %collective-permute-start.11 = (bf16[768,1024]{1,0:T(8,128)(2,1)}, bf16[768,1024]{1,0:T(8,128)(2,1)}, u32[]{:S(2)}, u32[]{:S(2)}) collective-permute-start(bf16[768,1024]{1,0:T(8,128)(2,1)} %get-tuple-element.33), channel_id=1, source_target_pairs={{1,0},{3,2},{5,4},{7,6},{9,8},{11,10},{13,12},{15,14},{17,16},{19,... | collective-permute-start | bytes 4718600 | tf_op jit(solution)/shard_map/ppermute | solution.py:227
  265.0 26.7 %collective-permute-start.2 = (bf16[256,2048]{1,0:T(8,128)(2,1)}, bf16[256,2048]{1,0:T(8,128)(2,1)}, u32[]{:S(2)}, u32[]{:S(2)}) collective-permute-start(bf16[256,2048]{1,0:T(8,128)(2,1)} %fusion.22), channel_id=1, source_target_pairs={{0,96},{32,64},{64,32},{96,0},{1,97},{33,65},{65,33},{97,1},{2,98}... | collective-permute-start | bytes 3145736 | tf_op jit(solution)/shard_map/ppermute | solution.py:119
  265.1 3.1 copy-start.11
  268.2 2.6 copy-start.12
  270.7 5.4 %copy-start.14 = (bf16[1024,768]{1,0:T(8,128)(2,1)S(1)}, bf16[1024,768]{1,0:T(8,128)(2,1)}, u32[]{:S(2)}) copy-start(bf16[1024,768]{1,0:T(8,128)(2,1)} %get-tuple-element.30) | copy-start | bytes 4718596
  273.3 39.1 %collective-permute-start.4 = (bf16[256,2048]{1,0:T(8,128)(2,1)S(1)}, bf16[256,2048]{1,0:T(8,128)(2,1)S(1)}, u32[]{:S(2)}, u32[]{:S(2)}) collective-permute-start(bf16[256,2048]{1,0:T(8,128)(2,1)S(1)} %convolution_convert_fusion.1), channel_id=1, source_target_pairs={{0,96},{32,64},{64,32},{96,0},{1,97},{33,65},{65,33},{97,1},{2,98}... | collective-permute-start | bytes 3145736 | tf_op jit(solution)/shard_map/ppermute | solution.py:119
  276.1 4.6 %copy-start.15 = (bf16[1024,768]{1,0:T(8,128)(2,1)S(1)}, bf16[1024,768]{1,0:T(8,128)(2,1)}, u32[]{:S(2)}) copy-start(bf16[1024,768]{1,0:T(8,128)(2,1)} %get-tuple-element.32) | copy-start | bytes 4718596
  293.2 2.8 copy-start.13
  295.8 19.5 %collective-permute-start.3 = (bf16[128,2048]{1,0:T(8,128)(2,1)S(1)}, bf16[128,2048]{1,0:T(8,128)(2,1)S(1)}, u32[]{:S(2)}, u32[]{:S(2)}) collective-permute-start(bf16[128,2048]{1,0:T(8,128)(2,1)S(1)} %fusion.33), channel_id=1, source_target_pairs={{0,64},{64,0},{1,65},{65,1},{2,66},{66,2},{3,67},{67,3},{4,68},{68... | collective-permute-start | bytes 1572872 | tf_op jit(solution)/shard_map/ppermute | solution.py:114
  315.2 13.4 %collective-permute-start.5 = (bf16[128,2048]{1,0:T(8,128)(2,1)S(1)}, bf16[128,2048]{1,0:T(8,128)(2,1)S(1)}, u32[]{:S(2)}, u32[]{:S(2)}) collective-permute-start(bf16[128,2048]{1,0:T(8,128)(2,1)S(1)} %fusion.30), channel_id=1, source_target_pairs={{0,64},{64,0},{1,65},{65,1},{2,66},{66,2},{3,67},{67,3},{4,68},{68... | collective-permute-start | bytes 1572872 | tf_op jit(solution)/shard_map/ppermute | solution.py:114
  315.3 14.3 %copy-start.1 = (bf16[1,768,2048]{2,1,0:T(8,128)(2,1)S(1)}, bf16[1,768,2048]{2,1,0:T(8,128)(2,1)}, u32[]{:S(2)}) copy-start(bf16[1,768,2048]{2,1,0:T(8,128)(2,1)} %param.15) | copy-start | bytes 9437188

commit v2 on v1

v2 whole, which is shorter than its diff:
```python
import functools

import jax
import jax.numpy as jnp
from jax import lax
from jax.experimental import pallas as pl
from jax.experimental.pallas import tpu as pltpu
from jax.sharding import Mesh, PartitionSpec as P

AXES = ("xlo", "xhi", "y", "z", "core")
PLANE = ("y", "z", "core")
LANES = 128
MIB = 1 << 20


def pack_kernel(pair_rows, route_ref, weight_ref, tok_ref, cot_ref, out_ref, rank_ref, place):
    top, tokens = route_ref.shape
    targets, _, tall, _ = out_ref.shape
    slots = targets * pl.num_programs(0)
    rows = targets * pair_rows
    parts = tall // pair_rows
    step = pl.program_id(0)

    @pl.when(step == 0)
    def _():
        across = lax.broadcasted_iota(jnp.int32, (tokens, tokens), 1)
        down = lax.broadcasted_iota(jnp.int32, (tokens, tokens), 0)
        earlier = (down < across).astype(jnp.bfloat16)
        slot = lax.broadcasted_iota(jnp.int32, (slots, tokens), 0)
        before = jnp.zeros((slots, 1), jnp.float32)
        for k in range(top):
            mine = slot == route_ref[k : k + 1, :]
            marks = mine.astype(jnp.float32)
            ahead = jnp.dot(
                marks.astype(jnp.bfloat16), earlier, preferred_element_type=jnp.float32
            )
            rank = jnp.sum(jnp.where(mine, ahead + before, 0.0), axis=0, keepdims=True)
            before = before + jnp.sum(marks, axis=1, keepdims=True)
            rank_ref[k : k + 1, :] = rank.astype(jnp.int32)
            place[k : k + 1, :] = route_ref[k : k + 1, :] * pair_rows + rank.astype(jnp.int32)

    row = lax.broadcasted_iota(jnp.int32, (rows, tokens), 0) + step * rows
    chosen = jnp.zeros((rows, tokens), jnp.float32)
    weight = jnp.zeros((rows, tokens), jnp.float32)
    for k in range(top):
        hit = row == place[k : k + 1, :]
        chosen = jnp.where(hit, 1.0, chosen)
        weight = jnp.where(hit, weight_ref[k : k + 1, :], weight)
    weight = jnp.sum(weight, axis=1, keepdims=True)
    chosen = chosen.astype(jnp.bfloat16)
    tok = jnp.dot(chosen, tok_ref[...], preferred_element_type=jnp.float32)
    out_ref[:, 0] = tok.reshape(targets, tall, LANES).astype(out_ref.dtype)
    cot = jnp.dot(chosen, cot_ref[...], preferred_element_type=jnp.float32) * weight
    out_ref[:, 1] = cot.reshape(targets, tall, LANES).astype(out_ref.dtype)


def pack(route, weight, tokens, cotangent, slots, pair_rows):
    count, width = tokens.shape
    tall = pair_rows * width // LANES
    block = 16
    whole = lambda i: (0, 0)
    return pl.pallas_call(
        functools.partial(pack_kernel, pair_rows),
        grid=(slots // block,),
        out_shape=(
            pltpu.HBM((slots, 2, tall, LANES), jnp.bfloat16),
            jax.ShapeDtypeStruct(route.shape, jnp.int32),
        ),
        in_specs=[
            pl.BlockSpec(route.shape, whole),
            pl.BlockSpec(weight.shape, whole),
            pl.BlockSpec(tokens.shape, whole),
            pl.BlockSpec(cotangent.shape, whole),
        ],
        out_specs=(
            pl.BlockSpec((block, 2, tall, LANES), lambda i: (i, 0, 0, 0)),
            pl.BlockSpec(route.shape, whole),
        ),
        scratch_shapes=[pltpu.VMEM(route.shape, jnp.int32)],
        compiler_params=pltpu.CompilerParams(vmem_limit_bytes=24 * MIB),
        cost_estimate=cheap(),
    )(route, weight, tokens, cotangent)


def unpack_kernel(in_ref, tok_ref, cot_ref):
    rings, members, _, tall, _ = in_ref.shape
    rows, width = tok_ref.shape
    parts = width // LANES
    for which, out_ref in enumerate((tok_ref, cot_ref)):
        value = in_ref[:, :, which].astype(jnp.float32)
        value = value.reshape(rings, members, tall // parts, parts, LANES)
        out_ref[...] = jnp.swapaxes(value, 0, 1).reshape(rows, width).astype(out_ref.dtype)


def unpack(arrived, width):
    rings, plane, _, tall, _ = arrived.shape
    rows = rings * plane * tall * LANES // width
    block = 8
    step = rows * block // plane
    return pl.pallas_call(
        unpack_kernel,
        grid=(plane // block,),
        out_shape=(jax.ShapeDtypeStruct((rows, width), jnp.bfloat16),) * 2,
        in_specs=[
            pl.BlockSpec((rings, block, 2, tall, LANES), lambda i: (0, i, 0, 0, 0)),
        ],
        out_specs=(pl.BlockSpec((step, width), lambda i: (i, 0)),) * 2,
        compiler_params=pltpu.CompilerParams(vmem_limit_bytes=24 * MIB),
        cost_estimate=cheap(),
    )(arrived)


def dot(a, b, over_a=1, over_b=0):
    return lax.dot_general(
        a, b, (((over_a,), (over_b,)), ((), ())), preferred_element_type=jnp.float32
    )


def cheap(flops=0):
    return pl.CostEstimate(flops=flops, bytes_accessed=0, transcendentals=0)


def fixed(shape, at=(0, 0)):
    return pl.BlockSpec(shape, lambda n, g: at, pipeline_mode=pl.Buffered(1))


def away(shape):
    return pl.BlockSpec(shape, lambda n, g: (0, 1 - g[0]), pipeline_mode=pl.Buffered(1))


def here(shape):
    return pl.BlockSpec(shape, lambda n, g: (0, g[0]), pipeline_mode=pl.Buffered(1))


def down(shape):
    return pl.BlockSpec(shape, lambda n, g: (n, 0))


def across(shape):
    return pl.BlockSpec(shape, lambda n, g: (0, n))


def call(kernel, group, steps, ins, outs, *operands):
    return pl.pallas_call(
        kernel,
        grid_spec=pltpu.PrefetchScalarGridSpec(
            num_scalar_prefetch=1,
            grid=(steps,),
            in_specs=ins,
            out_specs=tuple(spec for spec, _, _ in outs),
        ),
        out_shape=tuple(pltpu.HBM(shape, kind) for _, shape, kind in outs),
        compiler_params=pltpu.CompilerParams(vmem_limit_bytes=40 * MIB),
        cost_estimate=cheap(),
    )(group, *operands)


def first_kernel(group, x_ref, c_ref, gate_w, up_w, gate_ref, up_ref, hidden_ref, send_ref):
    gate = dot(x_ref[...], gate_w[...])
    up = dot(x_ref[...], up_w[...])
    gate_ref[...] = gate
    up_ref[...] = up
    hidden = (gate * jax.nn.sigmoid(gate) * up).astype(jnp.bfloat16)
    hidden_ref[...] = hidden
    send_ref[...] = dot(hidden, c_ref[...], 0, 0).astype(jnp.bfloat16)


def first(group, inputs, cot_in, gate_w, up_w):
    rows, width = inputs.shape
    inner = gate_w.shape[1]
    block, half = 256, width // 2
    f32, b16 = jnp.float32, jnp.bfloat16
    return call(
        first_kernel,
        group,
        inner // block,
        [fixed((rows, width)), away((rows, half)), across((width, block)), across((width, block))],
        [
            (across((rows, block)), (rows, inner), f32),
            (across((rows, block)), (rows, inner), f32),
            (across((rows, block)), (rows, inner), b16),
            (down((block, half)), (inner, half), b16),
        ],
        inputs,
        cot_in,
        gate_w,
        up_w,
    )


def expert_kernel(group, hidden_ref, down_w, out_ref):
    out_ref[...] = dot(hidden_ref[...], down_w[...]).astype(jnp.bfloat16)


def expert(group, hidden, down_w):
    rows, inner = hidden.shape
    width, block = down_w.shape[1], 512
    return call(
        expert_kernel,
        group,
        width // block,
        [fixed((rows, inner)), across((inner, block))],
        [(across((rows, block)), (rows, width), jnp.bfloat16)],
        hidden,
        down_w,
    )[0]


def second_kernel(group, x_ref, c_ref, down_w, gate_ref, up_ref, dg_ref, du_ref, send_g, send_u):
    back = dot(c_ref[...], down_w[...], 1, 1)
    gate, up = gate_ref[...], up_ref[...]
    sigma = jax.nn.sigmoid(gate)
    d_gate = (back * up * sigma * (1.0 + gate * (1.0 - sigma))).astype(jnp.bfloat16)
    d_up = (back * (gate * sigma)).astype(jnp.bfloat16)
    dg_ref[...] = d_gate
    du_ref[...] = d_up
    send_g[...] = dot(x_ref[...], d_gate, 0, 0).astype(jnp.bfloat16)
    send_u[...] = dot(x_ref[...], d_up, 0, 0).astype(jnp.bfloat16)


def second(group, inputs, cot_in, down_w, gate, up):
    rows, width = inputs.shape
    inner = gate.shape[1]
    block, half = 256, width // 2
    b16 = jnp.bfloat16
    return call(
        second_kernel,
        group,
        inner // block,
        [
            away((rows, half)),
            fixed((rows, width)),
            down((block, width)),
            across((rows, block)),
            across((rows, block)),
        ],
        [
            (across((rows, block)), (rows, inner), b16),
            (across((rows, block)), (rows, inner), b16),
            (across((half, block)), (half, inner), b16),
            (across((half, block)), (half, inner), b16),
        ],
        inputs,
        cot_in,
        down_w,
        gate,
        up,
    )


def rows_kernel(group, dg_ref, du_ref, gate_w, up_w, out_ref):
    out_ref[...] = (dot(dg_ref[...], gate_w[...], 1, 1) + dot(du_ref[...], up_w[...], 1, 1)).astype(
        jnp.bfloat16
    )


def row_gradient(group, d_gate, d_up, gate_w, up_w):
    rows, inner = d_gate.shape
    width, block = gate_w.shape[0], 512
    return call(
        rows_kernel,
        group,
        width // block,
        [fixed((rows, inner)), fixed((rows, inner)), down((block, inner)), down((block, inner))],
        [(across((rows, block)), (rows, width), jnp.bfloat16)],
        d_gate,
        d_up,
        gate_w,
        up_w,
    )[0]


def keep_kernel(group, x_ref, c_ref, hidden_ref, dg_ref, du_ref, keep_d, keep_g, keep_u):
    keep_d[...] = dot(hidden_ref[...], c_ref[...], 0, 0).astype(jnp.bfloat16)
    keep_g[...] = dot(x_ref[...], dg_ref[...], 0, 0).astype(jnp.bfloat16)
    keep_u[...] = dot(x_ref[...], du_ref[...], 0, 0).astype(jnp.bfloat16)


def keep_half(group, inputs, cot_in, hidden, d_gate, d_up):
    rows, width = inputs.shape
    inner = hidden.shape[1]
    block, half = 256, width // 2
    b16 = jnp.bfloat16
    return call(
        keep_kernel,
        group,
        inner // block,
        [here((rows, half)), here((rows, half))] + [across((rows, block))] * 3,
        [
            (down((block, half)), (inner, half), b16),
            (across((half, block)), (half, inner), b16),
            (across((half, block)), (half, inner), b16),
        ],
        inputs,
        cot_in,
        hidden,
        d_gate,
        d_up,
    )


def sums_kernel(group, *refs):
    *weights, rows_ref, far_ref, near_ref = refs
    total = sum(dot(w[...], rows_ref[...], 0, 0) for w in weights)
    count = far_ref.shape[0]
    far_ref[...] = total[:count].astype(jnp.bfloat16)
    near_ref[...] = total[count:]


def sums(group, rows, *weights):
    count, targets = weights[0].shape
    width, block = rows.shape[1], 512
    part = targets // 2
    return call(
        sums_kernel,
        group,
        width // block,
        [fixed((count, targets)) for _ in weights] + [across((count, block))],
        [
            (across((part, block)), (part, width), jnp.bfloat16),
            (across((part, block)), (part, width), jnp.float32),
        ],
        *weights,
        rows,
    )


def over(axes, sizes, move):
    pairs = []
    total = 1
    for n in sizes:
        total *= n
    for i in range(total):
        at, rest = [], i
        for n in reversed(sizes):
            at.append(rest % n)
            rest //= n
        to = move(tuple(reversed(at)))
        if to is not None:
            j = 0
            for n, c in zip(sizes, to, strict=True):
                j = j * n + c
            pairs.append((i, j))
    return pairs


def swap_low(block):
    return lax.ppermute(block, "xlo", [(0, 1), (1, 0)])


def swap_high(block):
    route = over(("xlo", "xhi"), (2, 2), lambda c: (1 - c[0], 1 - c[1]))
    return lax.ppermute(block, ("xlo", "xhi"), route)


def after(value, *others):
    return lax.optimization_barrier((value,) + others)[0]


def on_device(tokens, cotangent, combine, route, anchors, w_gate, w_up, w_down):
    token_count, width = tokens.shape
    top = route.shape[1]
    rings = lax.axis_size(("xlo", "xhi"))
    plane = lax.axis_size(PLANE)
    slots = rings * plane
    pair_rows = 3 * token_count * top // (2 * slots)
    half = width // 2
    group = lax.axis_index("xlo")
    high = lax.axis_index("xhi")
    ring_at = lax.axis_index(("xlo", "xhi"))
    ep_index = lax.axis_index(("xhi",) + PLANE)
    ep_count = lax.axis_size(("xhi",) + PLANE)

    weight = jnp.transpose(combine)
    target = jnp.transpose(route)
    packed, rank = pack(target, weight, tokens, cotangent, slots, pair_rows)
    arrived = lax.all_to_all(packed.reshape(slots, -1, LANES), AXES, 0, 0, tiled=True).reshape(
        rings, plane, 2, -1, LANES
    )

    facts = jnp.concatenate([target.astype(jnp.float32), rank.astype(jnp.float32), weight, weight])
    def weights_of(facts):
        near = jnp.concatenate([facts, swap_low(facts)])
        facts = jnp.concatenate([swap_high(near), near]).reshape(rings, 4, top, token_count)
        ring_of = jnp.stack(
            [
                (1 - group) * 2 + 1 - high,
                group * 2 + 1 - high,
                group * 2 + high,
                (1 - group) * 2 + high,
            ]
        )[:, None, None]
        slot_of = facts[:, 0].astype(jnp.int32) - ring_at * plane
        rank_of = facts[:, 1].astype(jnp.int32)
        inside = (slot_of >= 0) & (slot_of < plane)
        column = jnp.where(inside, (slot_of * rings + ring_of) * pair_rows + rank_of, -1)
        places = jnp.arange(slots * pair_rows, dtype=jnp.int32)[:, None, None]
        coarse_of = lax.reduce_precision(facts[:, 2], 8, 7)
        fine_of = facts[:, 2] - coarse_of
        ones, coarse, fine = 0.0, 0.0, 0.0
        for k in range(top):
            hit = column[None, :, k] == places
            ones = ones + jnp.where(hit, 1.0, 0.0)
            coarse = coarse + jnp.where(hit, coarse_of[None, :, k], 0.0)
            fine = fine + jnp.where(hit, fine_of[None, :, k], 0.0)
        return [
            w.astype(jnp.bfloat16).reshape(slots * pair_rows, rings * token_count)
            for w in (coarse, fine, ones)
        ]

    def to_plane(rows):
        chunks = rows.reshape(plane, rings * pair_rows, width)
        return lax.all_to_all(chunks, PLANE, 0, 0, tiled=True).reshape(slots * pair_rows, width)

    gate_weight, up_weight, down_weight = w_gate[0], w_up[0], w_down[0]
    at = group.astype(jnp.int32).reshape(1)
    inputs, cot_in = unpack(arrived, width)
    gate, up_proj, hidden, send_down = first(at, inputs, cot_in, gate_weight, up_weight)
    got_down = swap_low(send_down)
    expert_out = expert(at, hidden, down_weight)
    out_rows = to_plane(expert_out)
    d_gate, d_up, send_gate, send_up = second(
        at, inputs, after(cot_in, expert_out), down_weight, gate, up_proj
    )
    got_gate, got_up = swap_low(send_gate), swap_low(send_up)
    row_grad = row_gradient(at, d_gate, d_up, gate_weight, up_weight)
    grad_rows = to_plane(after(row_grad, got_down))
    kept = keep_half(at, inputs, cot_in, after(hidden, row_grad), d_gate, d_up)
    coarse, fine, ones = weights_of(after(facts, send_up))
    out_rows = after(out_rows, coarse, fine, ones)

    is_anchor = anchors[ep_index] == ep_index
    beside = jnp.minimum(ep_index + 1, ep_count - 1)
    joins = (ep_index + 1 < ep_count) & (anchors[beside] == ep_index)

    def joined(keep, got):
        passed = lax.ppermute(jnp.where(group == 0, got, keep), "core", [(1, 0)]).astype(jnp.float32)
        keep, got = keep.astype(jnp.float32), got.astype(jnp.float32)
        one = jnp.where(group == 0, keep, got)
        two = jnp.where(group == 0, got, keep)
        return one + jnp.where(is_anchor, two, 0.0) + jnp.where(joins, passed, 0.0)

    out_far, out_near = sums(at, out_rows, coarse, fine)
    out_came = swap_high(out_far)
    got_down = after(got_down, out_far)
    grad_down = joined(kept[0], got_down)
    out_near = after(out_near, got_gate) + out_came.astype(jnp.float32)
    out_others = out_near[token_count:].astype(jnp.bfloat16)
    out_last = swap_low(out_others)
    grad_gate = joined(kept[1], got_gate)
    row_far, row_near = sums(at, after(grad_rows, out_others, got_up), ones)
    row_came = swap_high(row_far)
    got_up = after(got_up, row_far)
    grad_up = joined(kept[2], got_up)
    out_last = after(out_last, row_far)
    mixed = (out_near[:token_count] + out_last.astype(jnp.float32)).astype(jnp.bfloat16)
    row_near = row_near + row_came.astype(jnp.float32)
    row_others = row_near[token_count:].astype(jnp.bfloat16)
    row_last = swap_low(row_others).astype(jnp.float32)
    input_grad = (row_near[:token_count] + row_last).astype(jnp.bfloat16)
    return (mixed, input_grad, grad_gate[None], grad_up[None], grad_down[None])


def solution(mesh):
    fine = Mesh(mesh.devices.reshape(2, 2, 4, 4, 2), AXES)
    rows = P(AXES, None)
    slot = P(AXES, None, None)
    experts = ("xhi",) + PLANE
    return jax.shard_map(
        on_device,
        mesh=fine,
        in_specs=(rows, rows, rows, rows, P(), slot, slot, slot),
        out_specs=(
            rows,
            rows,
            P(experts, "xlo", None),
            P(experts, "xlo", None),
            P(experts, None, "xlo"),
        ),
        check_vma=False,
    )
```

time: 331 us -> 280 us (0.85); the launches traced: 330 us -> 275 us
  matrix products: 69.5 us -> 0 us
  waiting for transfers between devices: 166 us -> 112 us
  Pallas kernels: 14.5 us -> 60.7 us
  local copies, waits for them, and re-layouts: 8.22 us -> 25.6 us
  other arithmetic: 20.9 us -> 28 us
    ppermute x6, waiting for transfers between devices: 122 us -> 23.8 us  [swap_low(): return lax.ppermute(block, 'xlo', [(0, 1), (1, 0)])]
    all_to_all x1, waiting for transfers between devices: 3.1 us -> 78 us  [on_device(): lax.all_to_all(packed.reshape(slots, -1, LANES), AXES, 0, 0, tiled=True)]
    dot_general x21 -> x0, matrix products: 69.5 us -> none  [dot(): lax.dot_general(a, b, (((over_a,), (over_b,)), ((), ())), preferred_eleme...]
    pallas_call x3 -> x9, Pallas kernels: 14.5 us -> 60.7 us  [the longest x7 48.6 us: call(): pl.pallas_call(kernel, grid_spec=pltpu.PrefetchScalarGridSpec(num_scalar_...]
    all_to_all x2, waiting for transfers between devices: 22.3 us -> 0.01 us  [to_plane(): lax.all_to_all(chunks, PLANE, 0, 0, tiled=True)]
    unnamed x63 -> x62, local copies, waits for them, and re-layouts: 6.98 us -> 24.8 us
    ppermute x3, waiting for transfers between devices: 18.9 us -> 10 us  [swap_high(): return lax.ppermute(block, ('xlo', 'xhi'), route)]
    select_n x1 -> x4, other arithmetic: 0.02 us -> 7.52 us  [the longest x3 7.44 us: joined(): jnp.where(group == 0, got, keep)]
  transfers between devices with their start and end apart: 15 -> 15, of which waited for: 9 -> 4; matrix products, arithmetic and copies ran while one was open for 23% -> 10% of each run, Pallas kernels for 0% -> 13%
where the time goes in v2:
time: 280 us; the launch traced here: 275 us
  waiting for transfers between devices  112 us (40%)
  Pallas kernels  60.7 us (22%)
  starting transfers between devices  46.5 us (17%)
  other arithmetic  28 us (10%)
  local copies, waits for them, and re-layouts  25.6 us (9%)
    all_to_all x1, waiting for transfers between devices, on_device(): lax.all_to_all(packed.reshape(slots, -1, LANES), AXES, 0, 0, tiled=True)  78 us
    pallas_call x7, Pallas kernels, call(): pl.pallas_call(kernel, grid_spec=pltpu.PrefetchScalarGridSpec(num_scalar_...  48.6 us
    unnamed x62, local copies, waits for them, and re-layouts  24.8 us
    ppermute x6, waiting for transfers between devices, swap_low(): return lax.ppermute(block, 'xlo', [(0, 1), (1, 0)])  23.8 us
    all_to_all x2, starting transfers between devices, to_plane(): lax.all_to_all(chunks, PLANE, 0, 0, tiled=True)  18.5 us
    broadcast_in_dim x3, other arithmetic, on_device(): return (mixed, input_grad, grad_gate[None], grad_up[None], grad_down[None])  13.1 us
    all_to_all x1, starting transfers between devices, on_device(): lax.all_to_all(packed.reshape(slots, -1, LANES), AXES, 0, 0, tiled=True)  11.9 us
    ppermute x3, starting transfers between devices, joined(): lax.ppermute(jnp.where(group == 0, got, keep), 'core', [(1, 0)])  10.9 us
  transfers between devices with their start and end apart: 15, of which 4 were waited for; matrix products, arithmetic and copies ran while one was open for 10% of the time, Pallas kernels for 13%

profile of v2, /device:TPU:1, one launch (start us, length us, event | category | flops | bytes accessed | tf_op | source)
XLA Modules:
  0.0 275.0 jit_solution(11500987394276653257)
XLA Ops:
  0.6 1.0 copy-done.18
  1.7 1.0 copy-done.19
  2.7 0.7 copy-done.20
  3.4 0.7 copy-done.22
  4.1 6.5 %shard_map.119 = (bf16[128,2,96,128]{3,2,1,0:T(8,128)(2,1)}, s32[4,128]{1,0:T(4,128)S(1)}) custom-call(s32[4,128]{1,0:T(4,128)S(1)} %bitcast.76, f32[4,128]{1,0:T(4,128)S(1)} %bitcast.74, bf16[128,2048]{1,0:T(8,128)(2,1)S(1)} %copy-done.18, bf16[128,2048]{1,0:T(8,128)(2,1)S(1)} %copy-done.19), custom_call_target="tpu_custom_call" | custom-call | tf_op jit(solution)/shard_map/pallas_call | solution.py:62
  10.6 11.9 %all-to-all-start = ((bf16[128,192,128]{2,1,0:T(8,128)(2,1)}), bf16[128,192,128]{2,1,0:T(8,128)(2,1)}, u32[]{:S(2)}, u32[]{:S(2)}) async-start(bf16[128,192,128]{2,1,0:T(8,128)(2,1)} %bitcast.79), calls=%async_computation | async-start | bytes 12582912 | tf_op jit(solution)/shard_map/all_to_all | solution.py:377
  22.5 78.0 %all-to-all-done = bf16[128,192,128]{2,1,0:T(8,128)(2,1)} async-done(((bf16[128,192,128]{2,1,0:T(8,128)(2,1)}), bf16[128,192,128]{2,1,0:T(8,128)(2,1)}, u32[]{:S(2)}, u32[]{:S(2)}) %all-to-all-start) | async-done | bytes 6291488 | tf_op jit(solution)/shard_map/all_to_all | solution.py:377
  100.5 5.6 %shard_map.120 = (bf16[768,2048]{1,0:T(8,128)(2,1)S(1)}, bf16[768,2048]{1,0:T(8,128)(2,1)S(1)}) custom-call(bf16[4,32,2,96,128]{4,3,2,1,0:T(8,128)(2,1)} %bitcast.4.in_ref), custom_call_target="tpu_custom_call" | custom-call | tf_op jit(solution)/shard_map/pallas_call | solution.py:100
  106.1 0.0 copy-start
  106.1 0.0 copy-start.3
  106.2 8.4 %shard_map.121 = (f32[768,768]{1,0:T(8,128)}, f32[768,768]{1,0:T(8,128)}, bf16[768,768]{1,0:T(8,128)(2,1)}, bf16[768,1024]{1,0:T(8,128)(2,1)}) custom-call(s32[1]{0:T(128)} %bitcast.group, bf16[768,2048]{1,0:T(8,128)(2,1)S(1)} %get-tuple-element.36.x_ref, bf16[768,2048]{1,0:T(8,128)(2,1)S(1)} %get-tuple-element.39.c_ref, bf16[2048,768]{1,0:T(8,128)(2,1)S(1)} %bitcast.70, ...), custom_call_target="tpu_custom_call" | custom-call | tf_op jit(solution)/shard_map/pallas_call | solution.py:144
  114.6 1.3 copy-done.13
  115.8 4.3 %shard_map.122 = bf16[768,2048]{1,0:T(8,128)(2,1)} custom-call(s32[1]{0:T(128)} %bitcast.group, bf16[768,768]{1,0:T(8,128)(2,1)S(1)} %copy-done.13, bf16[768,2048]{1,0:T(8,128)(2,1)S(1)} %bitcast.68), custom_call_target="tpu_custom_call" | custom-call | tf_op jit(solution)/shard_map/pallas_call | solution.py:144
  120.1 9.6 %all-to-all-start.1 = ((bf16[32,24,2048]{2,1,0:T(8,128)(2,1)}), bf16[32,24,2048]{2,1,0:T(8,128)(2,1)}, u32[]{:S(2)}, u32[]{:S(2)}) async-start(bf16[32,24,2048]{2,1,0:T(8,128)(2,1)} %bitcast.78), calls=%async_computation.1 | async-start | bytes 6291456 | tf_op jit(solution)/shard_map/all_to_all | solution.py:413
  129.8 0.1 collective-permute-start.5
  129.9 1.9 copy-done.1
  131.8 1.9 copy-done.4
  133.7 1.7 copy-done.16
  135.4 1.7 copy-done.17
  137.0 11.9 %shard_map.123 = (bf16[768,768]{1,0:T(8,128)(2,1)}, bf16[768,768]{1,0:T(8,128)(2,1)}, bf16[1024,768]{1,0:T(8,128)(2,1)}, bf16[1024,768]{1,0:T(8,128)(2,1)}) custom-call(s32[1]{0:T(128)} %bitcast.group, bf16[768,2048]{1,0:T(8,128)(2,1)S(1)} %get-tuple-element.36.x_ref, bf16[768,2048]{1,0:T(8,128)(2,1)S(1)} %copy-done.1, bf16[768,2048]{1,0:T(8,128)(2,1)S(1)} %bitcast.69, ...), custom_call_target="tpu_custom_call" | custom-call | tf_op jit(solution)/shard_map/pallas_call | solution.py:144
  148.9 1.4 collective-permute-start
  150.3 0.0 collective-permute-start.2
  150.3 15.7 %collective-permute-done = f32[16,128]{1,0:T(8,128)S(1)} collective-permute-done((f32[16,128]{1,0:T(8,128)S(1)}, f32[16,128]{1,0:T(8,128)S(1)}, u32[]{:S(2)}, u32[]{:S(2)}) %collective-permute-start) | collective-permute-done | bytes 8224 | tf_op jit(solution)/shard_map/ppermute | solution.py:348
  166.0 0.1 pad_add_fusion
  166.1 1.9 copy-done.6
  168.0 1.9 copy-done.8
  169.9 1.3 copy-done.9
  171.2 1.3 copy-done.11
  172.4 6.6 %shard_map.125 = bf16[768,2048]{1,0:T(8,128)(2,1)} custom-call(s32[1]{0:T(128)} %bitcast.group, bf16[768,768]{1,0:T(8,128)(2,1)S(1)} %copy-done.9, bf16[768,768]{1,0:T(8,128)(2,1)S(1)} %copy-done.11, bf16[2048,768]{1,0:T(8,128)(2,1)S(1)} %bitcast.71, bf16[2048,768]{1,0:T(8,128)(2,1)S(1)} %bitcast.73), custom_call_target="tpu_custom_call" | custom-call | tf_op jit(solution)/shard_map/pallas_call | solution.py:144
  179.0 8.9 %all-to-all-start.2 = ((bf16[32,24,2048]{2,1,0:T(8,128)(2,1)}), bf16[32,24,2048]{2,1,0:T(8,128)(2,1)}, u32[]{:S(2)}, u32[]{:S(2)}) async-start(bf16[32,24,2048]{2,1,0:T(8,128)(2,1)} %bitcast.77), calls=%async_computation.2 | async-start | bytes 6291456 | tf_op jit(solution)/shard_map/all_to_all | solution.py:413
  187.9 0.1 fusion.16
  188.1 2.6 add_convert_fusion
  190.6 6.4 %shard_map.124 = (bf16[256,2048]{1,0:T(8,128)(2,1)}, f32[256,2048]{1,0:T(8,128)}) custom-call(s32[1]{0:T(128)} %bitcast.group, bf16[768,512]{1,0:T(8,128)(2,1)S(1)} %get-tuple-element.67.refs_0_, bf16[768,512]{1,0:T(8,128)(2,1)S(1)} %get-tuple-element.66.refs_1_, bf16[768,2048]{1,0:T(8,128)(2,1)} %bitcast.30.refs_2_), custom_call_target="tpu_custom_call" | custom-call | tf_op jit(solution)/shard_map/pallas_call | solution.py:144
  197.0 3.0 %collective-permute-start.3 = (bf16[256,2048]{1,0:T(8,128)(2,1)}, bf16[256,2048]{1,0:T(8,128)(2,1)}, u32[]{:S(2)}, u32[]{:S(2)}) collective-permute-start(bf16[256,2048]{1,0:T(8,128)(2,1)} %get-tuple-element.48), channel_id=1, source_target_pairs={{0,96},{32,64},{64,32},{96,0},{1,97},{33,65},{65,33},{97,1},{2,98}... | collective-permute-start | bytes 3145736 | tf_op jit(solution)/shard_map/ppermute | solution.py:353
  200.0 1.9 copy-done.2
  201.9 1.3 copy-done.10
  203.2 1.3 copy-done.12
  204.4 1.3 copy-done.14
  205.7 5.8 %shard_map.127 = (bf16[768,1024]{1,0:T(8,128)(2,1)}, bf16[1024,768]{1,0:T(8,128)(2,1)}, bf16[1024,768]{1,0:T(8,128)(2,1)}) custom-call(s32[1]{0:T(128)} %bitcast.group, bf16[768,2048]{1,0:T(8,128)(2,1)S(1)} %get-tuple-element.36.x_ref, bf16[768,2048]{1,0:T(8,128)(2,1)S(1)} %copy-done.2, bf16[768,768]{1,0:T(8,128)(2,1)S(1)} %copy-done.14, ...), custom_call_target="tpu_custom_call" | custom-call | tf_op jit(solution)/shard_map/pallas_call | solution.py:144
  211.5 2.8 %broadcast_select_fusion.1 = bf16[1024,768]{1,0:T(8,128)(2,1)} fusion(bf16[1024,768]{1,0:T(8,128)(2,1)} %collective-permute-done.2, bf16[1024,768]{1,0:T(8,128)(2,1)} %get-tuple-element.58, pred[]{:T(512)S(6)} %eq.105), kind=kLoop, calls=%fused_computation.28 | loop fusion | flops 786432 | bytes 4718593 | tf_op jit(solution)/shard_map/jit(_where)/select_n | solution.py:437
  214.4 3.8 %collective-permute-start.9 = (bf16[1024,768]{1,0:T(8,128)(2,1)}, bf16[1024,768]{1,0:T(8,128)(2,1)}, u32[]{:S(2)}, u32[]{:S(2)}) collective-permute-start(bf16[1024,768]{1,0:T(8,128)(2,1)} %broadcast_select_fusion.1), channel_id=1, source_target_pairs={{1,0},{3,2},{5,4},{7,6},{9,8},{11,10},{13,12},{15,14},{17,16},{19,... | collective-permute-start | bytes 4718600 | tf_op jit(solution)/shard_map/ppermute | solution.py:437
  218.2 0.6 fusion.25
  220.1 0.0 copy-start.28
  220.1 2.9 %broadcast_select_fusion = bf16[768,1024]{1,0:T(8,128)(2,1)} fusion(bf16[768,1024]{1,0:T(8,128)(2,1)} %collective-permute-done.5, bf16[768,1024]{1,0:T(8,128)(2,1)S(1)} %copy-done.25, pred[]{:T(512)S(6)} %eq.105), kind=kLoop, calls=%fused_computation.27 | loop fusion | flops 786432 | bytes 4718593 | tf_op jit(solution)/shard_map/jit(_where)/select_n | solution.py:437
  223.0 2.5 collective-permute-start.11
  225.6 1.5 convert_add_fusion.1
  227.1 0.1 slice.128
  227.2 0.3 collective-permute-start.4
  227.4 8.0 %collective-permute-done.6 = bf16[1024,768]{1,0:T(8,128)(2,1)} collective-permute-done((bf16[1024,768]{1,0:T(8,128)(2,1)}, bf16[1024,768]{1,0:T(8,128)(2,1)}, u32[]{:S(2)}, u32[]{:S(2)}) %collective-permute-start.6) | collective-permute-done | bytes 1572896 | tf_op jit(solution)/shard_map/ppermute | solution.py:348
  235.5 5.3 %shard_map.126 = (bf16[256,2048]{1,0:T(8,128)(2,1)}, f32[256,2048]{1,0:T(8,128)}) custom-call(s32[1]{0:T(128)} %bitcast.group, bf16[768,512]{1,0:T(8,128)(2,1)S(1)} %copy-done.15, bf16[768,2048]{1,0:T(8,128)(2,1)} %bitcast.32.refs_1_), custom_call_target="tpu_custom_call" | custom-call | tf_op jit(solution)/shard_map/pallas_call | solution.py:144
  240.8 0.3 collective-permute-start.7
  241.1 1.7 broadcast_select_fusion.2
  242.8 4.6 %collective-permute-start.10 = (bf16[1024,768]{1,0:T(8,128)(2,1)S(1)}, bf16[1024,768]{1,0:T(8,128)(2,1)S(1)}, u32[]{:S(2)}, u32[]{:S(2)}) collective-permute-start(bf16[1024,768]{1,0:T(8,128)(2,1)S(1)} %broadcast_select_fusion.2), channel_id=1, source_target_pairs={{1,0},{3,2},{5,4},{7,6},{9,8},{11,10},{13,12},{15,14},{17,16},{19,... | collective-permute-start | bytes 4718600 | tf_op jit(solution)/shard_map/ppermute | solution.py:437
  247.4 4.5 %fusion.2 = f32[1,1024,768]{2,1,0:T(8,128)} fusion(bf16[1024,768]{1,0:T(8,128)(2,1)} %collective-permute-done.2, bf16[1024,768]{1,0:T(8,128)(2,1)S(1)} %copy-done.27, bf16[1024,768]{1,0:T(8,128)(2,1)} %collective-permute-done.9, pred[]{:T(512)S(6)} %and.16, pred[]{:T(512)S(6)} %eq.106, pred[]{:T(512)S(6)} %eq.105), kind=kLoop, calls=%fused_computation.8 | loop fusion | flops 7077888 | bytes 7864323 | tf_op jit(solution)/shard_map/broadcast_in_dim | solution.py:461
  251.9 2.1 fusion.13
  254.0 10.0 %collective-permute-done.7 = bf16[256,2048]{1,0:T(8,128)(2,1)S(1)} collective-permute-done((bf16[256,2048]{1,0:T(8,128)(2,1)}, bf16[256,2048]{1,0:T(8,128)(2,1)S(1)}, u32[]{:S(2)}, u32[]{:S(2)}) %collective-permute-start.7) | collective-permute-done | bytes 1048608 | tf_op jit(solution)/shard_map/ppermute | solution.py:353
  264.0 0.3 convert_add_fusion
  264.3 0.1 slice.127
  264.4 0.1 collective-permute-start.8
  264.5 0.9 copy-done.26
  265.4 4.6 %fusion.10 = f32[1,768,1024]{2,1,0:T(8,128)} fusion(bf16[768,1024]{1,0:T(8,128)(2,1)} %collective-permute-done.5, bf16[768,1024]{1,0:T(8,128)(2,1)S(1)} %copy-done.26, bf16[768,1024]{1,0:T(8,128)(2,1)} %collective-permute-done.11, pred[]{:T(512)S(6)} %and.16, pred[]{:T(512)S(6)} %eq.106, pred[]{:T(512)S(6)} %eq.105), kind=kLoop, calls=%fused_computation.16 | loop fusion | flops 7077888 | bytes 7864323 | tf_op jit(solution)/shard_map/broadcast_in_dim | solution.py:461
  270.0 4.0 %fusion.6 = f32[1,1024,768]{2,1,0:T(8,128)} fusion(bf16[1024,768]{1,0:T(8,128)(2,1)} %collective-permute-done.6, bf16[1024,768]{1,0:T(8,128)(2,1)S(1)} %copy-done.24, bf16[1024,768]{1,0:T(8,128)(2,1)S(1)} %collective-permute-done.10, pred[]{:T(512)S(6)} %and.16, pred[]{:T(512)S(6)} %eq.106, pred[]{:T(512)S(6)} %eq.105), kind=kLoop, calls=%fused_computation.12 | loop fusion | flops 7077888 | bytes 7864323 | tf_op jit(solution)/shard_map/broadcast_in_dim | solution.py:461
  274.0 0.0 collective-permute-done.8
  274.1 0.9 fusion.12
  (61 shorter events, 0.2 us)
Async XLA Ops:
  0.6 1.0 copy-start.18
  1.7 1.0 copy-start.19
  2.7 0.7 copy-start.20
  3.4 0.7 copy-start.22
  10.6 89.9 %all-to-all-start = ((bf16[128,192,128]{2,1,0:T(8,128)(2,1)}), bf16[128,192,128]{2,1,0:T(8,128)(2,1)}, u32[]{:S(2)}, u32[]{:S(2)}) async-start(bf16[128,192,128]{2,1,0:T(8,128)(2,1)} %bitcast.79), calls=%async_computation | async-start | bytes 12582912 | tf_op jit(solution)/shard_map/all_to_all | solution.py:377
  100.5 5.6 %copy-start.5 = (bf16[1,2048,768]{2,1,0:T(8,128)(2,1)S(1)}, bf16[1,2048,768]{2,1,0:T(8,128)(2,1)}, u32[]{:S(2)}) copy-start(bf16[1,2048,768]{2,1,0:T(8,128)(2,1)} %param.13) | copy-start | bytes 9437188
  100.5 5.6 %copy-start.7 = (bf16[1,2048,768]{2,1,0:T(8,128)(2,1)S(1)}, bf16[1,2048,768]{2,1,0:T(8,128)(2,1)}, u32[]{:S(2)}) copy-start(bf16[1,2048,768]{2,1,0:T(8,128)(2,1)} %param.14) | copy-start | bytes 9437188
  106.1 8.5 %copy-start = (bf16[768,2048]{1,0:T(8,128)(2,1)}, bf16[768,2048]{1,0:T(8,128)(2,1)S(1)}, u32[]{:S(2)}) copy-start(bf16[768,2048]{1,0:T(8,128)(2,1)S(1)} %get-tuple-element.39.c_ref) | copy-start | bytes 9437188
  106.1 8.4 %copy-start.3 = (bf16[1,768,2048]{2,1,0:T(8,128)(2,1)S(1)}, bf16[1,768,2048]{2,1,0:T(8,128)(2,1)}, u32[]{:S(2)}) copy-start(bf16[1,768,2048]{2,1,0:T(8,128)(2,1)} %param.15) | copy-start | bytes 9437188
  114.6 1.3 copy-start.13
  120.1 9.7 %copy-start.23 = (s32[128,4]{0,1:T(4,128)S(1)}, s32[128,4]{0,1:T(4,128)}, u32[]{:S(2)}) copy-start(s32[128,4]{0,1:T(4,128)} %param.11) | copy-start | bytes 6148
  120.1 9.8 %copy-start.21 = (f32[128,4]{0,1:T(4,128)S(1)}, f32[128,4]{0,1:T(4,128)}, u32[]{:S(2)}) copy-start(f32[128,4]{0,1:T(4,128)} %param.10) | copy-start | bytes 6148
  120.1 58.9 %all-to-all-start.1 = ((bf16[32,24,2048]{2,1,0:T(8,128)(2,1)}), bf16[32,24,2048]{2,1,0:T(8,128)(2,1)}, u32[]{:S(2)}, u32[]{:S(2)}) async-start(bf16[32,24,2048]{2,1,0:T(8,128)(2,1)} %bitcast.78), calls=%async_computation.1 | async-start | bytes 6291456 | tf_op jit(solution)/shard_map/all_to_all | solution.py:413
  129.8 49.3 %collective-permute-start.5 = (bf16[768,1024]{1,0:T(8,128)(2,1)}, bf16[768,1024]{1,0:T(8,128)(2,1)}, u32[]{:S(2)}, u32[]{:S(2)}) collective-permute-start(bf16[768,1024]{1,0:T(8,128)(2,1)} %get-tuple-element.51), channel_id=1, source_target_pairs={{0,64},{64,0},{1,65},{65,1},{2,66},{66,2},{3,67},{67,3},{4,68},{68... | collective-permute-start | bytes 4718600 | tf_op jit(solution)/shard_map/ppermute | solution.py:348
  129.9 1.9 copy-start.1
  131.8 1.9 copy-start.4
  133.7 1.7 copy-start.16
  135.4 1.7 copy-start.17
  148.9 17.1 %collective-permute-start = (f32[16,128]{1,0:T(8,128)S(1)}, f32[16,128]{1,0:T(8,128)S(1)}, u32[]{:S(2)}, u32[]{:S(2)}) collective-permute-start(f32[16,128]{1,0:T(8,128)S(1)} %pad_maximum_fusion.2), channel_id=1, source_target_pairs={{0,64},{64,0},{1,65},{65,1},{2,66},{66,2},{3,67},{67,3},{4,68},{68... | collective-permute-start | bytes 24584 | tf_op jit(solution)/shard_map/ppermute | solution.py:348
  150.3 61.2 %collective-permute-start.2 = (bf16[1024,768]{1,0:T(8,128)(2,1)}, bf16[1024,768]{1,0:T(8,128)(2,1)}, u32[]{:S(2)}, u32[]{:S(2)}) collective-permute-start(bf16[1024,768]{1,0:T(8,128)(2,1)} %get-tuple-element.46), channel_id=1, source_target_pairs={{0,64},{64,0},{1,65},{65,1},{2,66},{66,2},{3,67},{67,3},{4,68},{68... | collective-permute-start | bytes 4718600 | tf_op jit(solution)/shard_map/ppermute | solution.py:348
  166.0 21.9 %collective-permute-start.1 = (f32[32,128]{1,0:T(8,128)S(1)}, f32[32,128]{1,0:T(8,128)S(1)}, u32[]{:S(2)}, u32[]{:S(2)}) collective-permute-start(f32[32,128]{1,0:T(8,128)S(1)} %pad_maximum_fusion.1), channel_id=1, source_target_pairs={{0,96},{32,64},{64,32},{96,0},{1,97},{33,65},{65,33},{97,1},{2,98}... | collective-permute-start | bytes 49160 | tf_op jit(solution)/shard_map/ppermute | solution.py:353
  166.1 1.9 copy-start.6
  168.0 1.9 copy-start.8
  169.9 1.3 copy-start.9
  171.2 1.3 copy-start.11
  179.0 56.5 %all-to-all-start.2 = ((bf16[32,24,2048]{2,1,0:T(8,128)(2,1)}), bf16[32,24,2048]{2,1,0:T(8,128)(2,1)}, u32[]{:S(2)}, u32[]{:S(2)}) async-start(bf16[32,24,2048]{2,1,0:T(8,128)(2,1)} %bitcast.77), calls=%async_computation.2 | async-start | bytes 6291456 | tf_op jit(solution)/shard_map/all_to_all | solution.py:413
  197.0 28.5 %collective-permute-start.3 = (bf16[256,2048]{1,0:T(8,128)(2,1)}, bf16[256,2048]{1,0:T(8,128)(2,1)}, u32[]{:S(2)}, u32[]{:S(2)}) collective-permute-start(bf16[256,2048]{1,0:T(8,128)(2,1)} %get-tuple-element.48), channel_id=1, source_target_pairs={{0,96},{32,64},{64,32},{96,0},{1,97},{33,65},{65,33},{97,1},{2,98}... | collective-permute-start | bytes 3145736 | tf_op jit(solution)/shard_map/ppermute | solution.py:353
  200.0 35.5 %collective-permute-start.6 = (bf16[1024,768]{1,0:T(8,128)(2,1)}, bf16[1024,768]{1,0:T(8,128)(2,1)}, u32[]{:S(2)}, u32[]{:S(2)}) collective-permute-start(bf16[1024,768]{1,0:T(8,128)(2,1)} %get-tuple-element.42), channel_id=1, source_target_pairs={{0,64},{64,0},{1,65},{65,1},{2,66},{66,2},{3,67},{67,3},{4,68},{68... | collective-permute-start | bytes 4718600 | tf_op jit(solution)/shard_map/ppermute | solution.py:348
  200.0 1.9 copy-start.2
  201.9 1.3 copy-start.10
  203.2 1.3 copy-start.12
  204.4 1.3 copy-start.14
  211.5 6.7 %copy-start.30 = (s32[64]{0:T(128)S(1)}, s32[64]{0:T(128)}, u32[]{:S(2)}) copy-start(s32[64]{0:T(128)} %param.12) | copy-start | bytes 772
  211.5 8.6 %copy-start.25 = (bf16[768,1024]{1,0:T(8,128)(2,1)S(1)}, bf16[768,1024]{1,0:T(8,128)(2,1)}, u32[]{:S(2)}) copy-start(bf16[768,1024]{1,0:T(8,128)(2,1)} %get-tuple-element.61) | copy-start | bytes 4718596
  214.4 33.0 %collective-permute-start.9 = (bf16[1024,768]{1,0:T(8,128)(2,1)}, bf16[1024,768]{1,0:T(8,128)(2,1)}, u32[]{:S(2)}, u32[]{:S(2)}) collective-permute-start(bf16[1024,768]{1,0:T(8,128)(2,1)} %broadcast_select_fusion.1), channel_id=1, source_target_pairs={{1,0},{3,2},{5,4},{7,6},{9,8},{11,10},{13,12},{15,14},{17,16},{19,... | collective-permute-start | bytes 4718600 | tf_op jit(solution)/shard_map/ppermute | solution.py:437
  220.1 5.4 %copy-start.28 = (f32[256,2048]{1,0:T(8,128)S(1)}, f32[256,2048]{1,0:T(8,128)}, u32[]{:S(2)}) copy-start(f32[256,2048]{1,0:T(8,128)} %get-tuple-element.47) | copy-start | bytes 6291460
  223.0 41.4 %collective-permute-start.11 = (bf16[768,1024]{1,0:T(8,128)(2,1)}, bf16[768,1024]{1,0:T(8,128)(2,1)}, u32[]{:S(2)}, u32[]{:S(2)}) collective-permute-start(bf16[768,1024]{1,0:T(8,128)(2,1)} %broadcast_select_fusion), channel_id=1, source_target_pairs={{1,0},{3,2},{5,4},{7,6},{9,8},{11,10},{13,12},{15,14},{17,16},{19,... | collective-permute-start | bytes 4718600 | tf_op jit(solution)/shard_map/ppermute | solution.py:437
  227.1 8.4 %copy-start.15 = (bf16[768,512]{1,0:T(8,128)(2,1)S(1)}, bf16[768,512]{1,0:T(8,128)(2,1)}, u32[]{:S(2)}) copy-start(bf16[768,512]{1,0:T(8,128)(2,1)} %get-tuple-element.65.refs_0_) | copy-start | bytes 2359300
  227.2 24.7 %collective-permute-start.4 = (bf16[128,2048]{1,0:T(8,128)(2,1)S(1)}, bf16[128,2048]{1,0:T(8,128)(2,1)}, u32[]{:S(2)}, u32[]{:S(2)}) collective-permute-start(bf16[128,2048]{1,0:T(8,128)(2,1)S(1)} %slice.128), channel_id=1, source_target_pairs={{0,64},{64,0},{1,65},{65,1},{2,66},{66,2},{3,67},{67,3},{4,68},{68... | collective-permute-start | bytes 1572872 | tf_op jit(solution)/shard_map/ppermute | solution.py:348
  235.5 5.6 %copy-start.24 = (bf16[1024,768]{1,0:T(8,128)(2,1)S(1)}, bf16[1024,768]{1,0:T(8,128)(2,1)}, u32[]{:S(2)}) copy-start(bf16[1024,768]{1,0:T(8,128)(2,1)} %get-tuple-element.59) | copy-start | bytes 4718596
  240.8 23.2 %collective-permute-start.7 = (bf16[256,2048]{1,0:T(8,128)(2,1)}, bf16[256,2048]{1,0:T(8,128)(2,1)S(1)}, u32[]{:S(2)}, u32[]{:S(2)}) collective-permute-start(bf16[256,2048]{1,0:T(8,128)(2,1)} %get-tuple-element.54), channel_id=1, source_target_pairs={{0,96},{32,64},{64,32},{96,0},{1,97},{33,65},{65,33},{97,1},{2,98}... | collective-permute-start | bytes 3145736 | tf_op jit(solution)/shard_map/ppermute | solution.py:353
  241.1 6.3 %copy-start.27 = (bf16[1024,768]{1,0:T(8,128)(2,1)S(1)}, bf16[1024,768]{1,0:T(8,128)(2,1)}, u32[]{:S(2)}) copy-start(bf16[1024,768]{1,0:T(8,128)(2,1)} %get-tuple-element.58) | copy-start | bytes 4718596
  242.8 27.2 %collective-permute-start.10 = (bf16[1024,768]{1,0:T(8,128)(2,1)S(1)}, bf16[1024,768]{1,0:T(8,128)(2,1)S(1)}, u32[]{:S(2)}, u32[]{:S(2)}) collective-permute-start(bf16[1024,768]{1,0:T(8,128)(2,1)S(1)} %broadcast_select_fusion.2), channel_id=1, source_target_pairs={{1,0},{3,2},{5,4},{7,6},{9,8},{11,10},{13,12},{15,14},{17,16},{19,... | collective-permute-start | bytes 4718600 | tf_op jit(solution)/shard_map/ppermute | solution.py:437
  251.9 12.1 %copy-start.29 = (f32[256,2048]{1,0:T(8,128)S(1)}, f32[256,2048]{1,0:T(8,128)}, u32[]{:S(2)}) copy-start(f32[256,2048]{1,0:T(8,128)} %get-tuple-element.56) | copy-start | bytes 6291460
  264.0 1.4 copy-start.26
  264.4 9.7 %collective-permute-start.8 = (bf16[128,2048]{1,0:T(8,128)(2,1)S(1)}, bf16[128,2048]{1,0:T(8,128)(2,1)S(1)}, u32[]{:S(2)}, u32[]{:S(2)}) collective-permute-start(bf16[128,2048]{1,0:T(8,128)(2,1)S(1)} %slice.127), channel_id=1, source_target_pairs={{0,64},{64,0},{1,65},{65,1},{2,66},{66,2},{3,67},{67,3},{4,68},{68... | collective-permute-start | bytes 1572872 | tf_op jit(solution)/shard_map/ppermute | solution.py:348

commit v3 on v2

--- a/solution.py
+++ b/solution.py
@@ -77,37 +77,9 @@
             pl.BlockSpec(route.shape, whole),
         ),
         scratch_shapes=[pltpu.VMEM(route.shape, jnp.int32)],
-        compiler_params=pltpu.CompilerParams(vmem_limit_bytes=24 * MIB),
+        compiler_params=pltpu.CompilerParams(vmem_limit_bytes=60 * MIB),
         cost_estimate=cheap(),
     )(route, weight, tokens, cotangent)
-
-
-def unpack_kernel(in_ref, tok_ref, cot_ref):
-    rings, members, _, tall, _ = in_ref.shape
-    rows, width = tok_ref.shape
-    parts = width // LANES
-    for which, out_ref in enumerate((tok_ref, cot_ref)):
-        value = in_ref[:, :, which].astype(jnp.float32)
-        value = value.reshape(rings, members, tall // parts, parts, LANES)
-        out_ref[...] = jnp.swapaxes(value, 0, 1).reshape(rows, width).astype(out_ref.dtype)
-
-
-def unpack(arrived, width):
-    rings, plane, _, tall, _ = arrived.shape
-    rows = rings * plane * tall * LANES // width
-    block = 8
-    step = rows * block // plane
-    return pl.pallas_call(
-        unpack_kernel,
-        grid=(plane // block,),
-        out_shape=(jax.ShapeDtypeStruct((rows, width), jnp.bfloat16),) * 2,
-        in_specs=[
-            pl.BlockSpec((rings, block, 2, tall, LANES), lambda i: (0, i, 0, 0, 0)),
-        ],
-        out_specs=(pl.BlockSpec((step, width), lambda i: (i, 0)),) * 2,
-        compiler_params=pltpu.CompilerParams(vmem_limit_bytes=24 * MIB),
-        cost_estimate=cheap(),
-    )(arrived)
 
 
 def dot(a, b, over_a=1, over_b=0):
@@ -124,14 +96,6 @@
     return pl.BlockSpec(shape, lambda n, g: at, pipeline_mode=pl.Buffered(1))
 
 
-def away(shape):
-    return pl.BlockSpec(shape, lambda n, g: (0, 1 - g[0]), pipeline_mode=pl.Buffered(1))
-
-
-def here(shape):
-    return pl.BlockSpec(shape, lambda n, g: (0, g[0]), pipeline_mode=pl.Buffered(1))
-
-
 def down(shape):
     return pl.BlockSpec(shape, lambda n, g: (n, 0))
 
@@ -140,7 +104,7 @@
     return pl.BlockSpec(shape, lambda n, g: (0, n))
 
 
-def call(kernel, group, steps, ins, outs, *operands):
+def call(kernel, group, steps, ins, outs, *operands, scratch=(), vmem=56 * MIB):
     return pl.pallas_call(
         kernel,
         grid_spec=pltpu.PrefetchScalarGridSpec(
@@ -148,88 +112,166 @@
             grid=(steps,),
             in_specs=ins,
             out_specs=tuple(spec for spec, _, _ in outs),
+            scratch_shapes=list(scratch),
         ),
         out_shape=tuple(pltpu.HBM(shape, kind) for _, shape, kind in outs),
-        compiler_params=pltpu.CompilerParams(vmem_limit_bytes=40 * MIB),
+        compiler_params=pltpu.CompilerParams(vmem_limit_bytes=vmem),
         cost_estimate=cheap(),
     )(group, *operands)
 
 
-def first_kernel(group, x_ref, c_ref, gate_w, up_w, gate_ref, up_ref, hidden_ref, send_ref):
-    gate = dot(x_ref[...], gate_w[...])
-    up = dot(x_ref[...], up_w[...])
-    gate_ref[...] = gate
-    up_ref[...] = up
-    hidden = (gate * jax.nn.sigmoid(gate) * up).astype(jnp.bfloat16)
-    hidden_ref[...] = hidden
-    send_ref[...] = dot(hidden, c_ref[...], 0, 0).astype(jnp.bfloat16)
-
-
-def first(group, inputs, cot_in, gate_w, up_w):
-    rows, width = inputs.shape
-    inner = gate_w.shape[1]
-    block, half = 256, width // 2
+def front_kernel(
+    group,
+    arrived,
+    gate_in,
+    up_in,
+    down_in,
+    x_out,
+    c_out,
+    gate_out,
+    up_out,
+    hidden_out,
+    down_out,
+    expert_out,
+    landed,
+    gate_w,
+    up_w,
+    down_w,
+    x_all,
+    c_all,
+    gate_all,
+    up_all,
+    hidden,
+    send_down,
+    expert_all,
+    in_sems,
+    w_sems,
+    out_sems,
+):
+    rings, plane, _, tall, _ = arrived.shape
+    steps, _, members = landed.shape[:3]
+    _, rows, half = x_all.shape
+    width = 2 * half
+    parts = width // LANES
+    inner = hidden.shape[1]
+    block, wide = 256, 512
+    some = rows // steps
+    mine = 1 - group[0]
+    fetches = [
+        pltpu.make_async_copy(
+            arrived.at[:, pl.ds(i * members, members)], landed.at[i], in_sems.at[i]
+        )
+        for i in range(steps)
+    ]
+    loads = [
+        pltpu.make_async_copy(source, target, w_sems.at[i])
+        for i, (source, target) in enumerate(
+            ((gate_in, gate_w), (up_in, up_w), (down_in, down_w))
+        )
+    ]
+    for copy in fetches + loads:
+        copy.start()
+    sent = []
+
+    def put(source, target):
+        copy = pltpu.make_async_copy(source, target, out_sems.at[len(sent)])
+        copy.start()
+        sent.append(copy)
+
+    for i in range(steps):
+        fetches[i].wait()
+        for which, out in enumerate((x_all, c_all)):
+            value = landed[i, :, :, which].astype(jnp.float32)
+            value = value.reshape(rings, members, tall // parts, parts, LANES)
+            value = jnp.swapaxes(value, 0, 1).reshape(some, width).astype(jnp.bfloat16)
+            out[0, i * some : (i + 1) * some, :] = value[:, :half]
+            out[1, i * some : (i + 1) * some, :] = value[:, half:]
+    loads[0].wait()
+    loads[1].wait()
+    for n in range(inner // block):
+        cols = slice(n * block, (n + 1) * block)
+        gate = dot(x_all[0], gate_w[:half, cols]) + dot(x_all[1], gate_w[half:, cols])
+        up = dot(x_all[0], up_w[:half, cols]) + dot(x_all[1], up_w[half:, cols])
+        gate_all[:, cols] = gate
+        up_all[:, cols] = up
+        hidden[:, cols] = (gate * jax.nn.sigmoid(gate) * up).astype(jnp.bfloat16)
+        send_down[cols, :] = dot(hidden[:, cols], c_all[mine], 0, 0).astype(jnp.bfloat16)
+    put(send_down, down_out)
+    loads[2].wait()
+    for n in range(width // wide):
+        cols = slice(n * wide, (n + 1) * wide)
+        expert_all[:, cols] = dot(hidden[...], down_w[:, cols]).astype(jnp.bfloat16)
+    put(expert_all, expert_out)
+    put(x_all, x_out)
+    put(c_all, c_out)
+    put(gate_all, gate_out)
+    put(up_all, up_out)
+    put(hidden, hidden_out)
+    for copy in sent:
+        copy.wait()
+
+
+def front(group, arrived, gate_w, up_w, down_w):
+    rings, plane, _, tall, _ = arrived.shape
+    width, inner = gate_w.shape
+    rows = rings * plane * tall * LANES // width
+    half, members = width // 2, 8
+    steps = plane // members
     f32, b16 = jnp.float32, jnp.bfloat16
-    return call(
-        first_kernel,
-        group,
-        inner // block,
-        [fixed((rows, width)), away((rows, half)), across((width, block)), across((width, block))],
-        [
-            (across((rows, block)), (rows, inner), f32),
-            (across((rows, block)), (rows, inner), f32),
-            (across((rows, block)), (rows, inner), b16),
-            (down((block, half)), (inner, half), b16),
-        ],
-        inputs,
-        cot_in,
-        gate_w,
-        up_w,
-    )
-
-
-def expert_kernel(group, hidden_ref, down_w, out_ref):
-    out_ref[...] = dot(hidden_ref[...], down_w[...]).astype(jnp.bfloat16)
-
-
-def expert(group, hidden, down_w):
-    rows, inner = hidden.shape
-    width, block = down_w.shape[1], 512
-    return call(
-        expert_kernel,
-        group,
-        width // block,
-        [fixed((rows, inner)), across((inner, block))],
-        [(across((rows, block)), (rows, width), jnp.bfloat16)],
-        hidden,
-        down_w,
-    )[0]
-
-
-def second_kernel(group, x_ref, c_ref, down_w, gate_ref, up_ref, dg_ref, du_ref, send_g, send_u):
-    back = dot(c_ref[...], down_w[...], 1, 1)
+    shapes = [
+        ((2, rows, half), b16),
+        ((2, rows, half), b16),
+        ((rows, inner), f32),
+        ((rows, inner), f32),
+        ((rows, inner), b16),
+        ((inner, half), b16),
+        ((rows, width), b16),
+    ]
+    weights = [((width, inner), b16), ((width, inner), b16), ((inner, width), b16)]
+    return pl.pallas_call(
+        front_kernel,
+        out_shape=tuple(pltpu.HBM(*shape) for shape in shapes),
+        in_specs=[pl.BlockSpec(memory_space=pltpu.SMEM)]
+        + [pl.BlockSpec(memory_space=pl.ANY)] * 4,
+        out_specs=tuple(pl.BlockSpec(memory_space=pl.ANY) for _ in shapes),
+        scratch_shapes=[pltpu.VMEM((steps, rings, members, 2, tall, LANES), b16)]
+        + [pltpu.VMEM(*shape) for shape in weights + shapes]
+        + [pltpu.SemaphoreType.DMA((n,)) for n in (steps, len(weights), len(shapes))],
+        compiler_params=pltpu.CompilerParams(vmem_limit_bytes=56 * MIB),
+        cost_estimate=cheap(),
+    )(group, arrived, gate_w, up_w, down_w)
+
+
+def second_kernel(group, x_ref, c_ref, down_w, gate_ref, up_ref, dg_ref, du_ref, send_ref, turned):
+    @pl.when(pl.program_id(0) == 0)
+    def _():
+        turned[...] = jnp.transpose(x_ref[0])
+
+    half = x_ref.shape[2]
+    back = dot(c_ref[0], down_w[:, :half], 1, 1) + dot(c_ref[1], down_w[:, half:], 1, 1)
     gate, up = gate_ref[...], up_ref[...]
     sigma = jax.nn.sigmoid(gate)
     d_gate = (back * up * sigma * (1.0 + gate * (1.0 - sigma))).astype(jnp.bfloat16)
     d_up = (back * (gate * sigma)).astype(jnp.bfloat16)
     dg_ref[...] = d_gate
     du_ref[...] = d_up
-    send_g[...] = dot(x_ref[...], d_gate, 0, 0).astype(jnp.bfloat16)
-    send_u[...] = dot(x_ref[...], d_up, 0, 0).astype(jnp.bfloat16)
+    send_ref[0] = dot(turned[...], d_gate).astype(jnp.bfloat16)
+    send_ref[1] = dot(turned[...], d_up).astype(jnp.bfloat16)
 
 
 def second(group, inputs, cot_in, down_w, gate, up):
-    rows, width = inputs.shape
+    _, rows, half = inputs.shape
     inner = gate.shape[1]
-    block, half = 256, width // 2
+    block, width = 256, 2 * half
     b16 = jnp.bfloat16
+    away = pl.BlockSpec((1, rows, half), lambda n, g: (1 - g[0], 0, 0), pipeline_mode=pl.Buffered(1))
     return call(
         second_kernel,
         group,
         inner // block,
         [
-            away((rows, half)),
-            fixed((rows, width)),
+            away,
+            fixed((2, rows, half), (0, 0, 0)),
             down((block, width)),
             across((rows, block)),
             across((rows, block)),
@@ -237,14 +279,14 @@
         [
             (across((rows, block)), (rows, inner), b16),
             (across((rows, block)), (rows, inner), b16),
-            (across((half, block)), (half, inner), b16),
-            (across((half, block)), (half, inner), b16),
+            (pl.BlockSpec((2, half, block), lambda n, g: (0, 0, n)), (2, half, inner), b16),
         ],
         inputs,
         cot_in,
         down_w,
         gate,
         up,
+        scratch=[pltpu.VMEM((half, rows), b16)],
     )
 
 
@@ -254,14 +296,16 @@
     )
 
 
-def row_gradient(group, d_gate, d_up, gate_w, up_w):
+def row_gradient(group, which, d_gate, d_up, gate_w, up_w):
     rows, inner = d_gate.shape
-    width, block = gate_w.shape[0], 512
+    width, block = gate_w.shape[0] // 2, 512
+    steps = width // block
+    part = pl.BlockSpec((block, inner), lambda n, g: (n + which * steps, 0))
     return call(
         rows_kernel,
         group,
-        width // block,
-        [fixed((rows, inner)), fixed((rows, inner)), down((block, inner)), down((block, inner))],
+        steps,
+        [fixed((rows, inner)), fixed((rows, inner)), part, part],
         [(across((rows, block)), (rows, width), jnp.bfloat16)],
         d_gate,
         d_up,
@@ -271,21 +315,23 @@
 
 
 def keep_kernel(group, x_ref, c_ref, hidden_ref, dg_ref, du_ref, keep_d, keep_g, keep_u):
-    keep_d[...] = dot(hidden_ref[...], c_ref[...], 0, 0).astype(jnp.bfloat16)
-    keep_g[...] = dot(x_ref[...], dg_ref[...], 0, 0).astype(jnp.bfloat16)
-    keep_u[...] = dot(x_ref[...], du_ref[...], 0, 0).astype(jnp.bfloat16)
+    keep_d[...] = dot(hidden_ref[...], c_ref[0], 0, 0).astype(jnp.bfloat16)
+    turned = jnp.transpose(x_ref[0])
+    keep_g[...] = dot(turned, dg_ref[...]).astype(jnp.bfloat16)
+    keep_u[...] = dot(turned, du_ref[...]).astype(jnp.bfloat16)
 
 
 def keep_half(group, inputs, cot_in, hidden, d_gate, d_up):
-    rows, width = inputs.shape
+    _, rows, half = inputs.shape
     inner = hidden.shape[1]
-    block, half = 256, width // 2
+    block = 384
     b16 = jnp.bfloat16
+    here = pl.BlockSpec((1, rows, half), lambda n, g: (g[0], 0, 0), pipeline_mode=pl.Buffered(1))
     return call(
         keep_kernel,
         group,
         inner // block,
-        [here((rows, half)), here((rows, half))] + [across((rows, block))] * 3,
+        [here, here] + [across((rows, block))] * 3,
         [
             (down((block, half)), (inner, half), b16),
             (across((half, block)), (half, inner), b16),
@@ -379,9 +425,12 @@
     )
 
     facts = jnp.concatenate([target.astype(jnp.float32), rank.astype(jnp.float32), weight, weight])
+    opposite = lax.ppermute(facts, "xhi", [(0, 1), (1, 0)])
+    facts = [swap_high(facts), opposite, facts, swap_low(facts)]
+    arrived, *facts = lax.optimization_barrier((arrived, *facts))
+
     def weights_of(facts):
-        near = jnp.concatenate([facts, swap_low(facts)])
-        facts = jnp.concatenate([swap_high(near), near]).reshape(rings, 4, top, token_count)
+        facts = jnp.stack(facts).reshape(rings, 4, top, token_count)
         ring_of = jnp.stack(
             [
                 (1 - group) * 2 + 1 - high,
@@ -409,25 +458,26 @@
         ]
 
     def to_plane(rows):
-        chunks = rows.reshape(plane, rings * pair_rows, width)
-        return lax.all_to_all(chunks, PLANE, 0, 0, tiled=True).reshape(slots * pair_rows, width)
+        chunks = rows.reshape(plane, rings * pair_rows, -1)
+        return lax.all_to_all(chunks, PLANE, 0, 0, tiled=True).reshape(slots * pair_rows, -1)
 
     gate_weight, up_weight, down_weight = w_gate[0], w_up[0], w_down[0]
     at = group.astype(jnp.int32).reshape(1)
-    inputs, cot_in = unpack(arrived, width)
-    gate, up_proj, hidden, send_down = first(at, inputs, cot_in, gate_weight, up_weight)
+    inputs, cot_in, gate, up_proj, hidden, send_down, expert_out = front(
+        at, arrived, gate_weight, up_weight, down_weight
+    )
     got_down = swap_low(send_down)
-    expert_out = expert(at, hidden, down_weight)
     out_rows = to_plane(expert_out)
-    d_gate, d_up, send_gate, send_up = second(
-        at, inputs, after(cot_in, expert_out), down_weight, gate, up_proj
-    )
-    got_gate, got_up = swap_low(send_gate), swap_low(send_up)
-    row_grad = row_gradient(at, d_gate, d_up, gate_weight, up_weight)
-    grad_rows = to_plane(after(row_grad, got_down))
-    kept = keep_half(at, inputs, cot_in, after(hidden, row_grad), d_gate, d_up)
-    coarse, fine, ones = weights_of(after(facts, send_up))
+    d_gate, d_up, send_both = second(at, inputs, cot_in, down_weight, gate, up_proj)
+    got_both = swap_low(send_both)
+    row_left = row_gradient(at, 0, d_gate, d_up, gate_weight, up_weight)
+    left_rows = to_plane(after(row_left, got_down))
+    row_right = row_gradient(at, 1, after(d_gate, row_left), d_up, gate_weight, up_weight)
+    right_rows = to_plane(row_right)
+    coarse, fine, ones = weights_of(lax.optimization_barrier((*facts, row_right))[:-1])
     out_rows = after(out_rows, coarse, fine, ones)
+    out_far, out_near = sums(at, out_rows, coarse, fine)
+    kept = keep_half(at, inputs, cot_in, after(hidden, out_far), d_gate, d_up)
 
     is_anchor = anchors[ep_index] == ep_index
     beside = jnp.minimum(ep_index + 1, ep_count - 1)
@@ -440,24 +490,26 @@
         two = jnp.where(group == 0, got, keep)
         return one + jnp.where(is_anchor, two, 0.0) + jnp.where(joins, passed, 0.0)
 
-    out_far, out_near = sums(at, out_rows, coarse, fine)
+    grad_down = joined(kept[0], after(got_down, out_far))
     out_came = swap_high(out_far)
-    got_down = after(got_down, out_far)
-    grad_down = joined(kept[0], got_down)
-    out_near = after(out_near, got_gate) + out_came.astype(jnp.float32)
+    out_near = out_near + out_came.astype(jnp.float32)
     out_others = out_near[token_count:].astype(jnp.bfloat16)
     out_last = swap_low(out_others)
-    grad_gate = joined(kept[1], got_gate)
-    row_far, row_near = sums(at, after(grad_rows, out_others, got_up), ones)
-    row_came = swap_high(row_far)
-    got_up = after(got_up, row_far)
-    grad_up = joined(kept[2], got_up)
-    out_last = after(out_last, row_far)
+    left_far, left_near = sums(at, after(left_rows, out_others), ones)
+    left_came = swap_high(left_far)
+    right_far, right_near = sums(at, after(right_rows, left_far, got_both), ones)
+    right_came = swap_high(right_far)
+    got_both = after(got_both, right_far)
+    grad_gate = joined(kept[1], got_both[0])
+    grad_up = joined(kept[2], got_both[1])
+    out_last = after(out_last, right_far)
     mixed = (out_near[:token_count] + out_last.astype(jnp.float32)).astype(jnp.bfloat16)
-    row_near = row_near + row_came.astype(jnp.float32)
-    row_others = row_near[token_count:].astype(jnp.bfloat16)
-    row_last = swap_low(row_others).astype(jnp.float32)
-    input_grad = (row_near[:token_count] + row_last).astype(jnp.bfloat16)
+    ends = []
+    for near, came in ((left_near, left_came), (right_near, right_came)):
+        near = near + came.astype(jnp.float32)
+        last = swap_low(near[token_count:].astype(jnp.bfloat16)).astype(jnp.float32)
+        ends.append((near[:token_count] + last).astype(jnp.bfloat16))
+    input_grad = jnp.concatenate(ends, axis=1)
     return (mixed, input_grad, grad_gate[None], grad_up[None], grad_down[None])
 
 

time: 280 us -> 264 us (0.943)
  local copies, waits for them, and re-layouts: 25.6 us -> 3.07 us
  Pallas kernels: 60.7 us -> 77.5 us
  other arithmetic: 28 us -> 21.7 us
  waiting for transfers between devices: 112 us -> 109 us
    all_to_all x1, waiting for transfers between devices: 78 us -> 5.76 us  [on_device(): lax.all_to_all(packed.reshape(slots, -1, LANES), AXES, 0, 0, tiled=True)]
    ppermute x6, waiting for transfers between devices: 23.8 us -> 80.3 us  [swap_low(): return lax.ppermute(block, 'xlo', [(0, 1), (1, 0)])]
    unnamed x62 -> x24, local copies, waits for them, and re-layouts: 24.8 us -> 2.33 us
    all_to_all x2 -> x3, waiting for transfers between devices: 0.01 us -> 16.6 us  [to_plane(): lax.all_to_all(chunks, PLANE, 0, 0, tiled=True)]
    pallas_call x1, Pallas kernels: 5.56 us -> 19.9 us  [front(): pl.pallas_call(front_kernel, out_shape=tuple((pltpu.HBM(*shape) for shape...]
    ppermute x3 -> x4, waiting for transfers between devices: 10 us -> 5.11 us  [swap_high(): return lax.ppermute(block, ('xlo', 'xhi'), route)]
    broadcast_in_dim x3 -> x2, other arithmetic: 13.1 us -> 9.61 us  [on_device(): return (mixed, input_grad, grad_gate[None], grad_up[None], grad_down[None])]
    ppermute x3 -> x4, starting transfers between devices: 3.27 us -> 0.42 us  [swap_high(): return lax.ppermute(block, ('xlo', 'xhi'), route)]
  transfers between devices with their start and end apart: 15 -> 18, of which waited for: 4 -> 11; matrix products, arithmetic and copies ran while one was open for 10% -> 7% of each run, Pallas kernels for 13% -> 19%
where the time goes in v3:
time: 264 us; the launch traced here: 262 us
  waiting for transfers between devices  109 us (41%)
  Pallas kernels  77.5 us (29%)
  starting transfers between devices  47.6 us (18%)
  other arithmetic  21.7 us (8%)
  local copies, waits for them, and re-layouts  3.07 us (1%)
    ppermute x6, waiting for transfers between devices, swap_low(): return lax.ppermute(block, 'xlo', [(0, 1), (1, 0)])  80.3 us
    pallas_call x7, Pallas kernels, call(): pl.pallas_call(kernel, grid_spec=pltpu.PrefetchScalarGridSpec(num_scalar_...  49.8 us
    pallas_call x1, Pallas kernels, front(): pl.pallas_call(front_kernel, out_shape=tuple((pltpu.HBM(*shape) for shape...  19.9 us
    all_to_all x3, starting transfers between devices, to_plane(): lax.all_to_all(chunks, PLANE, 0, 0, tiled=True)  19.9 us
    all_to_all x3, waiting for transfers between devices, to_plane(): lax.all_to_all(chunks, PLANE, 0, 0, tiled=True)  16.6 us
    all_to_all x1, starting transfers between devices, on_device(): lax.all_to_all(packed.reshape(slots, -1, LANES), AXES, 0, 0, tiled=True)  11.9 us
    broadcast_in_dim x2, other arithmetic, on_device(): return (mixed, input_grad, grad_gate[None], grad_up[None], grad_down[None])  9.61 us
    ppermute x3, starting transfers between devices, joined(): lax.ppermute(jnp.where(group == 0, got, keep), 'core', [(1, 0)])  9.12 us
  transfers between devices with their start and end apart: 18, of which 11 were waited for; matrix products, arithmetic and copies ran while one was open for 7% of the time, Pallas kernels for 19%

profile of v3, /device:TPU:1, one launch (start us, length us, event | category | flops | bytes accessed | tf_op | source)
XLA Modules:
  0.0 261.6 jit_solution(4921133355426227961)
XLA Ops:
  0.6 7.8 %shard_map.119 = (bf16[128,2,96,128]{3,2,1,0:T(8,128)(2,1)}, s32[4,128]{1,0:T(4,128)}) custom-call(s32[4,128]{1,0:T(4,128)} %bitcast.96, f32[4,128]{1,0:T(4,128)} %bitcast.94, bf16[128,2048]{1,0:T(8,128)(2,1)} %tok_ref.1, bf16[128,2048]{1,0:T(8,128)(2,1)} %cot_ref.1), custom_call_target="tpu_custom_call" | custom-call | tf_op jit(solution)/shard_map/pallas_call | solution.py:62
  8.4 11.9 %all-to-all-start = ((bf16[128,192,128]{2,1,0:T(8,128)(2,1)}), bf16[128,192,128]{2,1,0:T(8,128)(2,1)}, u32[]{:S(2)}, u32[]{:S(2)}) async-start(bf16[128,192,128]{2,1,0:T(8,128)(2,1)} %bitcast.83), calls=%async_computation | async-start | bytes 12582912 | tf_op jit(solution)/shard_map/all_to_all | solution.py:423
  20.4 1.5 collective-permute-start.2
  21.9 2.4 collective-permute-start.1
  24.3 0.1 collective-permute-start
  24.4 66.5 %collective-permute-done.2 = f32[16,128]{1,0:T(8,128)S(1)} collective-permute-done((f32[16,128]{1,0:T(8,128)S(1)}, f32[16,128]{1,0:T(8,128)S(1)}, u32[]{:S(2)}, u32[]{:S(2)}) %collective-permute-start.2) | collective-permute-done | bytes 8224 | tf_op jit(solution)/shard_map/ppermute | solution.py:394
  90.9 1.7 collective-permute-done.1
  92.6 0.0 collective-permute-done
  92.6 5.8 %all-to-all-done = bf16[128,192,128]{2,1,0:T(8,128)(2,1)} async-done(((bf16[128,192,128]{2,1,0:T(8,128)(2,1)}), bf16[128,192,128]{2,1,0:T(8,128)(2,1)}, u32[]{:S(2)}, u32[]{:S(2)}) %all-to-all-start) | async-done | bytes 6291488 | tf_op jit(solution)/shard_map/all_to_all | solution.py:423
  98.3 19.9 %shard_map.120 = (bf16[2,768,1024]{2,1,0:T(8,128)(2,1)}, bf16[2,768,1024]{2,1,0:T(8,128)(2,1)}, f32[768,768]{1,0:T(8,128)}, f32[768,768]{1,0:T(8,128)}, bf16[768...) custom-call(s32[1]{0:T(128)} %bitcast.group, bf16[4,32,2,96,128]{4,3,2,1,0:T(8,128)(2,1)} %bitcast.4.arrived, ...), custom_call_target="tpu_custom_call" | custom-call | tf_op jit(solution)/shard_map/pallas_call | solution.py:231
  118.3 9.4 %all-to-all-start.1 = ((bf16[32,24,2048]{2,1,0:T(8,128)(2,1)}), bf16[32,24,2048]{2,1,0:T(8,128)(2,1)S(1)}, u32[]{:S(2)}, u32[]{:S(2)}) async-start(bf16[32,24,2048]{2,1,0:T(8,128)(2,1)} %bitcast.85), calls=%async_computation.1 | async-start | bytes 6291456 | tf_op jit(solution)/shard_map/all_to_all | solution.py:462
  127.7 0.3 collective-permute-start.5
  128.0 0.1 pad_add_fusion
  128.1 15.4 %shard_map.121 = (bf16[768,768]{1,0:T(8,128)(2,1)}, bf16[768,768]{1,0:T(8,128)(2,1)}, bf16[2,1024,768]{2,1,0:T(8,128)(2,1)}) custom-call(s32[1]{0:T(128)} %bitcast.group, bf16[2,768,1024]{2,1,0:T(8,128)(2,1)} %get-tuple-element.51.x_ref, bf16[2,768,1024]{2,1,0:T(8,128)(2,1)} %get-tuple-element.52.c_ref, bf16[768,2048]{1,0:T(8,128)(2,1)} %bitcast.82, ...), custom_call_target="tpu_custom_call" | custom-call | tf_op jit(solution)/shard_map/pallas_call | solution.py:108
  143.5 5.9 %shard_map.122 = bf16[768,1024]{1,0:T(8,128)(2,1)} custom-call(s32[1]{0:T(128)} %bitcast.group, bf16[768,768]{1,0:T(8,128)(2,1)} %get-tuple-element.57.dg_ref, bf16[768,768]{1,0:T(8,128)(2,1)} %get-tuple-element.56.du_ref, bf16[2048,768]{1,0:T(8,128)(2,1)} %bitcast.75, bf16[2048,768]{1,0:T(8,128)(2,1)} %bitcast.78), custom_call_target="tpu_custom_call" | custom-call | tf_op jit(solution)/shard_map/pallas_call | solution.py:108
  149.4 5.9 %shard_map.123 = bf16[768,1024]{1,0:T(8,128)(2,1)} custom-call(s32[1]{0:T(128)} %bitcast.group, bf16[768,768]{1,0:T(8,128)(2,1)} %get-tuple-element.57.dg_ref, bf16[768,768]{1,0:T(8,128)(2,1)} %get-tuple-element.56.du_ref, bf16[2048,768]{1,0:T(8,128)(2,1)} %bitcast.76, bf16[2048,768]{1,0:T(8,128)(2,1)} %bitcast.79), custom_call_target="tpu_custom_call" | custom-call | tf_op jit(solution)/shard_map/pallas_call | solution.py:108
  155.3 1.4 collective-permute-start.6
  156.8 7.3 %collective-permute-done.5 = bf16[768,1024]{1,0:T(8,128)(2,1)} collective-permute-done((bf16[768,1024]{1,0:T(8,128)(2,1)}, bf16[768,1024]{1,0:T(8,128)(2,1)}, u32[]{:S(2)}, u32[]{:S(2)}) %collective-permute-start.5) | collective-permute-done | bytes 1572896 | tf_op jit(solution)/shard_map/ppermute | solution.py:394
  164.1 3.4 %all-to-all-done.1 = bf16[32,24,2048]{2,1,0:T(8,128)(2,1)S(1)} async-done(((bf16[32,24,2048]{2,1,0:T(8,128)(2,1)}), bf16[32,24,2048]{2,1,0:T(8,128)(2,1)S(1)}, u32[]{:S(2)}, u32[]{:S(2)}) %all-to-all-start.1) | async-done | bytes 3145760 | tf_op jit(solution)/shard_map/all_to_all | solution.py:462
  167.5 1.7 copy-done
  169.1 5.5 %all-to-all-start.3 = ((bf16[32,24,1024]{2,1,0:T(8,128)(2,1)}), bf16[32,24,1024]{2,1,0:T(8,128)(2,1)}, u32[]{:S(2)}, u32[]{:S(2)}) async-start(bf16[32,24,1024]{2,1,0:T(8,128)(2,1)} %bitcast.84), calls=%async_computation.3 | async-start | bytes 3145728 | tf_op jit(solution)/shard_map/all_to_all | solution.py:462
  174.6 0.1 fusion.18
  174.8 3.3 %add_convert_fusion = (bf16[768,512]{1,0:T(8,128)(2,1)}, bf16[768,512]{1,0:T(8,128)(2,1)}, bf16[768,512]{1,0:T(8,128)(2,1)}) fusion(s32[512]{0:T(512)S(1)} %bitcast.102, s32[512]{0:T(512)S(1)} %bitcast.103, s32[512]{0:T(512)S(1)} %bitcast.104, s32[512]{0:T(512)S(1)} %bitcast.101, f32[512]{0:T(512)S(1)} %bitcast.98, f32[512]{0:T(512)S(1)} %bitcast.99, ...), kind=kLoop, calls=%fused_computation.21 | loop fusion | flops 11010048 | bytes 2383872 | tf_op jit(solution)/shard_map/convert_element_type | solution.py:456
  178.1 7.0 %shard_map.124 = (bf16[256,2048]{1,0:T(8,128)(2,1)}, f32[256,2048]{1,0:T(8,128)}) custom-call(s32[1]{0:T(128)} %bitcast.group, bf16[768,512]{1,0:T(8,128)(2,1)} %get-tuple-element.91.refs_0_, bf16[768,512]{1,0:T(8,128)(2,1)} %get-tuple-element.90.refs_1_, bf16[768,2048]{1,0:T(8,128)(2,1)} %bitcast.80), custom_call_target="tpu_custom_call" | custom-call | tf_op jit(solution)/shard_map/pallas_call | solution.py:108
  185.1 0.0 collective-permute-start.3
  185.1 12.3 %all-to-all-done.3 = bf16[32,24,1024]{2,1,0:T(8,128)(2,1)} async-done(((bf16[32,24,1024]{2,1,0:T(8,128)(2,1)}), bf16[32,24,1024]{2,1,0:T(8,128)(2,1)}, u32[]{:S(2)}, u32[]{:S(2)}) %all-to-all-start.3) | async-done | bytes 1572896 | tf_op jit(solution)/shard_map/all_to_all | solution.py:462
  197.4 5.0 %all-to-all-start.2 = ((bf16[32,24,1024]{2,1,0:T(8,128)(2,1)}), bf16[32,24,1024]{2,1,0:T(8,128)(2,1)}, u32[]{:S(2)}, u32[]{:S(2)}) async-start(bf16[32,24,1024]{2,1,0:T(8,128)(2,1)} %bitcast.34), calls=%async_computation.2 | async-start | bytes 3145728 | tf_op jit(solution)/shard_map/all_to_all | solution.py:462
  202.4 8.6 %shard_map.127 = (bf16[768,1024]{1,0:T(8,128)(2,1)}, bf16[1024,768]{1,0:T(8,128)(2,1)}, bf16[1024,768]{1,0:T(8,128)(2,1)}) custom-call(s32[1]{0:T(128)} %bitcast.group, bf16[2,768,1024]{2,1,0:T(8,128)(2,1)} %get-tuple-element.51.x_ref, bf16[2,768,1024]{2,1,0:T(8,128)(2,1)} %get-tuple-element.52.c_ref, bf16[768,768]{1,0:T(8,128)(2,1)} %get-tuple-element.77.hidden_ref, ...), custom_call_target="tpu_custom_call" | custom-call | tf_op jit(solution)/shard_map/pallas_call | solution.py:108
  210.9 0.1 collective-permute-done.3
  211.1 0.2 convert_add_fusion
  211.3 0.0 copy-start.3
  211.3 0.1 slice.130
  211.4 3.6 %shard_map.125 = (bf16[256,1024]{1,0:T(8,128)(2,1)}, f32[256,1024]{1,0:T(8,128)}) custom-call(s32[1]{0:T(128)} %bitcast.group, bf16[768,512]{1,0:T(8,128)(2,1)} %get-tuple-element.89.refs_0_, bf16[768,1024]{1,0:T(8,128)(2,1)} %bitcast.37.refs_1_), custom_call_target="tpu_custom_call" | custom-call | tf_op jit(solution)/shard_map/pallas_call | solution.py:108
  215.0 0.3 collective-permute-start.7
  215.3 2.7 %broadcast_select_fusion = bf16[768,1024]{1,0:T(8,128)(2,1)} fusion(bf16[768,1024]{1,0:T(8,128)(2,1)} %collective-permute-done.5, bf16[768,1024]{1,0:T(8,128)(2,1)S(1)} %copy-done.3, pred[]{:T(512)S(6)} %eq.105), kind=kLoop, calls=%fused_computation.28 | loop fusion | flops 786432 | bytes 4718593 | tf_op jit(solution)/shard_map/jit(_where)/select_n | solution.py:487
  218.0 4.0 %collective-permute-start.13 = (bf16[768,1024]{1,0:T(8,128)(2,1)}, bf16[768,1024]{1,0:T(8,128)(2,1)}, u32[]{:S(2)}, u32[]{:S(2)}) collective-permute-start(bf16[768,1024]{1,0:T(8,128)(2,1)} %broadcast_select_fusion), channel_id=1, source_target_pairs={{1,0},{3,2},{5,4},{7,6},{9,8},{11,10},{13,12},{15,14},{17,16},{19,... | collective-permute-start | bytes 4718600 | tf_op jit(solution)/shard_map/ppermute | solution.py:487
  222.1 0.6 fusion.26
  224.0 0.3 collective-permute-start.4
  224.3 0.9 all-to-all-done.2
  225.2 6.3 %collective-permute-done.6 = bf16[2,1024,768]{2,1,0:T(8,128)(2,1)} collective-permute-done((bf16[2,1024,768]{2,1,0:T(8,128)(2,1)}, bf16[2,1024,768]{2,1,0:T(8,128)(2,1)}, u32[]{:S(2)}, u32[]{:S(2)}) %collective-permute-start.6) | collective-permute-done | bytes 3145760 | tf_op jit(solution)/shard_map/ppermute | solution.py:394
  231.5 3.4 %shard_map.126 = (bf16[256,1024]{1,0:T(8,128)(2,1)}, f32[256,1024]{1,0:T(8,128)}) custom-call(s32[1]{0:T(128)} %bitcast.group, bf16[768,512]{1,0:T(8,128)(2,1)} %get-tuple-element.89.refs_0_, bf16[768,1024]{1,0:T(8,128)(2,1)} %bitcast.35.refs_1_), custom_call_target="tpu_custom_call" | custom-call | tf_op jit(solution)/shard_map/pallas_call | solution.py:108
  234.9 0.0 collective-permute-start.9
  234.9 2.3 bitcast_select_fusion
  237.2 3.7 %collective-permute-start.12 = (bf16[1024,768]{1,0:T(8,128)(2,1)S(1)}, bf16[1024,768]{1,0:T(8,128)(2,1)S(1)}, u32[]{:S(2)}, u32[]{:S(2)}) collective-permute-start(bf16[1024,768]{1,0:T(8,128)(2,1)S(1)} %get-tuple-element.87), channel_id=1, source_target_pairs={{1,0},{3,2},{5,4},{7,6},{9,8},{11,10},{13,12},{15,14},{17,16},{19,... | collective-permute-start | bytes 4718600 | tf_op jit(solution)/shard_map/ppermute | solution.py:487
  240.9 1.4 collective-permute-start.11
  242.3 0.0 copy-start.7
  242.3 0.2 convert_add_fusion.2
  242.5 0.2 collective-permute-done.4
  242.7 0.3 collective-permute-start.8
  243.0 5.0 %collective-permute-done.9 = bf16[256,1024]{1,0:T(8,128)(2,1)S(1)} collective-permute-done((bf16[256,1024]{1,0:T(8,128)(2,1)}, bf16[256,1024]{1,0:T(8,128)(2,1)S(1)}, u32[]{:S(2)}, u32[]{:S(2)}) %collective-permute-start.9) | collective-permute-done | bytes 524320 | tf_op jit(solution)/shard_map/ppermute | solution.py:399
  248.0 0.2 convert_add_fusion.1
  248.2 0.0 copy-start.4
  248.2 0.1 collective-permute-start.10
  248.3 2.0 fusion.12
  250.4 4.6 %fusion.10 = f32[1,768,1024]{2,1,0:T(8,128)} fusion(bf16[768,1024]{1,0:T(8,128)(2,1)} %collective-permute-done.5, bf16[768,1024]{1,0:T(8,128)(2,1)S(1)} %copy-done.4, bf16[768,1024]{1,0:T(8,128)(2,1)} %collective-permute-done.13, pred[]{:T(512)S(6)} %and.16, pred[]{:T(512)S(6)} %eq.106, pred[]{:T(512)S(6)} %eq.105), kind=kLoop, calls=%fused_computation.16 | loop fusion | flops 7077888 | bytes 7864323 | tf_op jit(solution)/shard_map/broadcast_in_dim | solution.py:513
  255.0 0.0 collective-permute-done.8
  255.0 0.1 fusion.14
  255.1 0.0 collective-permute-done.10
  255.1 0.1 fusion.13
  255.2 0.8 pad_maximum_fusion
  256.0 0.0 collective-permute-done.12
  256.0 0.0 collective-permute-done.11
  256.0 0.6 copy-done.2
  256.6 5.0 %fusion.6 = (f32[1,1024,768]{2,1,0:T(8,128)}, f32[1,1024,768]{2,1,0:T(8,128)}) fusion(bf16[1024,768]{1,0:T(8,128)(2,1)S(1)} %copy-done.2, bf16[1024,768]{1,0:T(8,128)(2,1)S(1)} %collective-permute-done.12, pred[]{:T(512)S(6)} %and.16, pred[]{:T(512)S(6)} %eq.106, pred[]{:T(512)S(6)} %eq.105, bf16[2,1024,768]{2,1,0:T(8,128)(2,1)} %collective-permute-done.6, ...), kind=kLoop, calls=%fused_computation.12 | loop fusion | flops 14155776 | bytes 15728643 | tf_op jit(solution)/shard_map/broadcast_in_dim | solution.py:513
  (31 shorter events, 0.2 us)
Async XLA Ops:
  8.4 11.9 %copy-start.11 = (s32[4,128]{1,0:T(4,128)S(1)}, s32[4,128]{1,0:T(4,128)}, u32[]{:S(2)}) copy-start(s32[4,128]{1,0:T(4,128)} %get-tuple-element.45) | copy-start | bytes 6148
  8.4 11.9 %copy-start.9 = (s32[128,4]{0,1:T(4,128)S(1)}, s32[128,4]{0,1:T(4,128)}, u32[]{:S(2)}) copy-start(s32[128,4]{0,1:T(4,128)} %param.11) | copy-start | bytes 6148
  8.4 12.0 %copy-start.8 = (f32[128,4]{0,1:T(4,128)S(1)}, f32[128,4]{0,1:T(4,128)}, u32[]{:S(2)}) copy-start(f32[128,4]{0,1:T(4,128)} %param.10) | copy-start | bytes 6148
  8.4 89.9 %all-to-all-start = ((bf16[128,192,128]{2,1,0:T(8,128)(2,1)}), bf16[128,192,128]{2,1,0:T(8,128)(2,1)}, u32[]{:S(2)}, u32[]{:S(2)}) async-start(bf16[128,192,128]{2,1,0:T(8,128)(2,1)} %bitcast.83), calls=%async_computation | async-start | bytes 12582912 | tf_op jit(solution)/shard_map/all_to_all | solution.py:423
  20.4 70.5 %collective-permute-start.2 = (f32[16,128]{1,0:T(8,128)S(1)}, f32[16,128]{1,0:T(8,128)S(1)}, u32[]{:S(2)}, u32[]{:S(2)}) collective-permute-start(f32[16,128]{1,0:T(8,128)S(1)} %pad_maximum_fusion.4), channel_id=1, source_target_pairs={{0,64},{64,0},{1,65},{65,1},{2,66},{66,2},{3,67},{67,3},{4,68},{68... | collective-permute-start | bytes 24584 | tf_op jit(solution)/shard_map/ppermute | solution.py:394
  21.9 70.7 %collective-permute-start.1 = (f32[16,128]{1,0:T(8,128)S(1)}, f32[16,128]{1,0:T(8,128)S(1)}, u32[]{:S(2)}, u32[]{:S(2)}) collective-permute-start(f32[16,128]{1,0:T(8,128)S(1)} %pad_maximum_fusion.4), channel_id=1, source_target_pairs={{0,32},{32,0},{1,33},{33,1},{2,34},{34,2},{3,35},{35,3},{4,36},{36... | collective-permute-start | bytes 24584 | tf_op jit(solution)/shard_map/ppermute | solution.py:428
  24.3 68.3 %collective-permute-start = (f32[16,128]{1,0:T(8,128)S(1)}, f32[16,128]{1,0:T(8,128)S(1)}, u32[]{:S(2)}, u32[]{:S(2)}) collective-permute-start(f32[16,128]{1,0:T(8,128)S(1)} %pad_maximum_fusion.4), channel_id=1, source_target_pairs={{0,96},{32,64},{64,32},{96,0},{1,97},{33,65},{65,33},{97,1},{2,98}... | collective-permute-start | bytes 24584 | tf_op jit(solution)/shard_map/ppermute | solution.py:399
  118.3 49.2 %all-to-all-start.1 = ((bf16[32,24,2048]{2,1,0:T(8,128)(2,1)}), bf16[32,24,2048]{2,1,0:T(8,128)(2,1)S(1)}, u32[]{:S(2)}, u32[]{:S(2)}) async-start(bf16[32,24,2048]{2,1,0:T(8,128)(2,1)} %bitcast.85), calls=%async_computation.1 | async-start | bytes 6291456 | tf_op jit(solution)/shard_map/all_to_all | solution.py:462
  127.7 36.3 %collective-permute-start.5 = (bf16[768,1024]{1,0:T(8,128)(2,1)}, bf16[768,1024]{1,0:T(8,128)(2,1)}, u32[]{:S(2)}, u32[]{:S(2)}) collective-permute-start(bf16[768,1024]{1,0:T(8,128)(2,1)} %get-tuple-element.66), channel_id=1, source_target_pairs={{0,64},{64,0},{1,65},{65,1},{2,66},{66,2},{3,67},{67,3},{4,68},{68... | collective-permute-start | bytes 4718600 | tf_op jit(solution)/shard_map/ppermute | solution.py:394
  155.3 76.2 %collective-permute-start.6 = (bf16[2,1024,768]{2,1,0:T(8,128)(2,1)}, bf16[2,1024,768]{2,1,0:T(8,128)(2,1)}, u32[]{:S(2)}, u32[]{:S(2)}) collective-permute-start(bf16[2,1024,768]{2,1,0:T(8,128)(2,1)} %get-tuple-element.70), channel_id=1, source_target_pairs={{0,64},{64,0},{1,65},{65,1},{2,66},{66,2},{3,67},{67,3},{4,68},{68... | collective-permute-start | bytes 9437192 | tf_op jit(solution)/shard_map/ppermute | solution.py:394
  167.5 1.7 copy-start
  169.1 28.2 %all-to-all-start.3 = ((bf16[32,24,1024]{2,1,0:T(8,128)(2,1)}), bf16[32,24,1024]{2,1,0:T(8,128)(2,1)}, u32[]{:S(2)}, u32[]{:S(2)}) async-start(bf16[32,24,1024]{2,1,0:T(8,128)(2,1)} %bitcast.84), calls=%async_computation.3 | async-start | bytes 3145728 | tf_op jit(solution)/shard_map/all_to_all | solution.py:462
  185.1 26.0 %collective-permute-start.3 = (bf16[256,2048]{1,0:T(8,128)(2,1)}, bf16[256,2048]{1,0:T(8,128)(2,1)S(1)}, u32[]{:S(2)}, u32[]{:S(2)}) collective-permute-start(bf16[256,2048]{1,0:T(8,128)(2,1)} %get-tuple-element.65), channel_id=1, source_target_pairs={{0,96},{32,64},{64,32},{96,0},{1,97},{33,65},{65,33},{97,1},{2,98}... | collective-permute-start | bytes 3145736 | tf_op jit(solution)/shard_map/ppermute | solution.py:399
  197.4 27.8 %all-to-all-start.2 = ((bf16[32,24,1024]{2,1,0:T(8,128)(2,1)}), bf16[32,24,1024]{2,1,0:T(8,128)(2,1)}, u32[]{:S(2)}, u32[]{:S(2)}) async-start(bf16[32,24,1024]{2,1,0:T(8,128)(2,1)} %bitcast.34), calls=%async_computation.2 | async-start | bytes 3145728 | tf_op jit(solution)/shard_map/all_to_all | solution.py:462
  202.4 8.7 %copy-start.5 = (f32[256,2048]{1,0:T(8,128)S(1)}, f32[256,2048]{1,0:T(8,128)}, u32[]{:S(2)}) copy-start(f32[256,2048]{1,0:T(8,128)} %get-tuple-element.64) | copy-start | bytes 6291460
  211.3 4.0 %copy-start.3 = (bf16[768,1024]{1,0:T(8,128)(2,1)S(1)}, bf16[768,1024]{1,0:T(8,128)(2,1)}, u32[]{:S(2)}) copy-start(bf16[768,1024]{1,0:T(8,128)(2,1)} %get-tuple-element.81) | copy-start | bytes 4718596
  215.0 25.9 %collective-permute-start.7 = (bf16[256,1024]{1,0:T(8,128)(2,1)}, bf16[256,1024]{1,0:T(8,128)(2,1)S(1)}, u32[]{:S(2)}, u32[]{:S(2)}) collective-permute-start(bf16[256,1024]{1,0:T(8,128)(2,1)} %get-tuple-element.69), channel_id=1, source_target_pairs={{0,96},{32,64},{64,32},{96,0},{1,97},{33,65},{65,33},{97,1},{2,98}... | collective-permute-start | bytes 1572872 | tf_op jit(solution)/shard_map/ppermute | solution.py:399
  215.3 6.8 %copy-start.10 = (s32[64]{0:T(128)S(1)}, s32[64]{0:T(128)}, u32[]{:S(2)}) copy-start(s32[64]{0:T(128)} %param.12) | copy-start | bytes 772
  218.0 32.3 %collective-permute-start.13 = (bf16[768,1024]{1,0:T(8,128)(2,1)}, bf16[768,1024]{1,0:T(8,128)(2,1)}, u32[]{:S(2)}, u32[]{:S(2)}) collective-permute-start(bf16[768,1024]{1,0:T(8,128)(2,1)} %broadcast_select_fusion), channel_id=1, source_target_pairs={{1,0},{3,2},{5,4},{7,6},{9,8},{11,10},{13,12},{15,14},{17,16},{19,... | collective-permute-start | bytes 4718600 | tf_op jit(solution)/shard_map/ppermute | solution.py:487
  224.0 18.7 %collective-permute-start.4 = (bf16[128,2048]{1,0:T(8,128)(2,1)S(1)}, bf16[128,2048]{1,0:T(8,128)(2,1)}, u32[]{:S(2)}, u32[]{:S(2)}) collective-permute-start(bf16[128,2048]{1,0:T(8,128)(2,1)S(1)} %slice.130), channel_id=1, source_target_pairs={{0,64},{64,0},{1,65},{65,1},{2,66},{66,2},{3,67},{67,3},{4,68},{68... | collective-permute-start | bytes 1572872 | tf_op jit(solution)/shard_map/ppermute | solution.py:394
  225.2 9.7 %copy-start.1 = (bf16[1024,768]{1,0:T(8,128)(2,1)S(1)}, bf16[1024,768]{1,0:T(8,128)(2,1)}, u32[]{:S(2)}) copy-start(bf16[1024,768]{1,0:T(8,128)(2,1)} %get-tuple-element.78) | copy-start | bytes 4718596
  234.9 13.1 %collective-permute-start.9 = (bf16[256,1024]{1,0:T(8,128)(2,1)}, bf16[256,1024]{1,0:T(8,128)(2,1)S(1)}, u32[]{:S(2)}, u32[]{:S(2)}) collective-permute-start(bf16[256,1024]{1,0:T(8,128)(2,1)} %get-tuple-element.72), channel_id=1, source_target_pairs={{0,96},{32,64},{64,32},{96,0},{1,97},{33,65},{65,33},{97,1},{2,98}... | collective-permute-start | bytes 1572872 | tf_op jit(solution)/shard_map/ppermute | solution.py:399
  234.9 7.4 %copy-start.6 = (f32[256,1024]{1,0:T(8,128)S(1)}, f32[256,1024]{1,0:T(8,128)}, u32[]{:S(2)}) copy-start(f32[256,1024]{1,0:T(8,128)} %get-tuple-element.74) | copy-start | bytes 3145732
  237.2 18.8 %collective-permute-start.12 = (bf16[1024,768]{1,0:T(8,128)(2,1)S(1)}, bf16[1024,768]{1,0:T(8,128)(2,1)S(1)}, u32[]{:S(2)}, u32[]{:S(2)}) collective-permute-start(bf16[1024,768]{1,0:T(8,128)(2,1)S(1)} %get-tuple-element.87), channel_id=1, source_target_pairs={{1,0},{3,2},{5,4},{7,6},{9,8},{11,10},{13,12},{15,14},{17,16},{19,... | collective-permute-start | bytes 4718600 | tf_op jit(solution)/shard_map/ppermute | solution.py:487
  240.9 15.1 %collective-permute-start.11 = (bf16[1024,768]{1,0:T(8,128)(2,1)S(1)}, bf16[1024,768]{1,0:T(8,128)(2,1)S(1)}, u32[]{:S(2)}, u32[]{:S(2)}) collective-permute-start(bf16[1024,768]{1,0:T(8,128)(2,1)S(1)} %get-tuple-element.88), channel_id=1, source_target_pairs={{1,0},{3,2},{5,4},{7,6},{9,8},{11,10},{13,12},{15,14},{17,16},{19,... | collective-permute-start | bytes 4718600 | tf_op jit(solution)/shard_map/ppermute | solution.py:487
  242.3 5.7 %copy-start.7 = (f32[256,1024]{1,0:T(8,128)S(1)}, f32[256,1024]{1,0:T(8,128)}, u32[]{:S(2)}) copy-start(f32[256,1024]{1,0:T(8,128)} %get-tuple-element.75) | copy-start | bytes 3145732
  242.7 12.3 %collective-permute-start.8 = (bf16[128,1024]{1,0:T(8,128)(2,1)S(1)}, bf16[128,1024]{1,0:T(8,128)(2,1)S(1)}, u32[]{:S(2)}, u32[]{:S(2)}) collective-permute-start(bf16[128,1024]{1,0:T(8,128)(2,1)S(1)} %slice.132), channel_id=1, source_target_pairs={{0,64},{64,0},{1,65},{65,1},{2,66},{66,2},{3,67},{67,3},{4,68},{68... | collective-permute-start | bytes 786440 | tf_op jit(solution)/shard_map/ppermute | solution.py:394
  248.2 2.2 copy-start.4
  248.2 6.8 %collective-permute-start.10 = (bf16[128,1024]{1,0:T(8,128)(2,1)S(1)}, bf16[128,1024]{1,0:T(8,128)(2,1)S(1)}, u32[]{:S(2)}, u32[]{:S(2)}) collective-permute-start(bf16[128,1024]{1,0:T(8,128)(2,1)S(1)} %slice.131), channel_id=1, source_target_pairs={{0,64},{64,0},{1,65},{65,1},{2,66},{66,2},{3,67},{67,3},{4,68},{68... | collective-permute-start | bytes 786440 | tf_op jit(solution)/shard_map/ppermute | solution.py:394
  255.0 1.6 copy-start.2

commit v4 on v3

--- a/solution.py
+++ b/solution.py
@@ -11,6 +11,7 @@
 PLANE = ("y", "z", "core")
 LANES = 128
 MIB = 1 << 20
+LONG = 40_000_000_000
 
 
 def pack_kernel(pair_rows, route_ref, weight_ref, tok_ref, cot_ref, out_ref, rank_ref, place):
@@ -104,7 +105,7 @@
     return pl.BlockSpec(shape, lambda n, g: (0, n))
 
 
-def call(kernel, group, steps, ins, outs, *operands, scratch=(), vmem=56 * MIB):
+def call(kernel, group, steps, ins, outs, *operands, scratch=(), vmem=56 * MIB, cost=0):
     return pl.pallas_call(
         kernel,
         grid_spec=pltpu.PrefetchScalarGridSpec(
@@ -116,7 +117,7 @@
         ),
         out_shape=tuple(pltpu.HBM(shape, kind) for _, shape, kind in outs),
         compiler_params=pltpu.CompilerParams(vmem_limit_bytes=vmem),
-        cost_estimate=cheap(),
+        cost_estimate=cheap(cost),
     )(group, *operands)
 
 
@@ -125,25 +126,21 @@
     arrived,
     gate_in,
     up_in,
-    down_in,
     x_out,
     c_out,
     gate_out,
     up_out,
     hidden_out,
     down_out,
-    expert_out,
     landed,
     gate_w,
     up_w,
-    down_w,
     x_all,
     c_all,
     gate_all,
     up_all,
     hidden,
     send_down,
-    expert_all,
     in_sems,
     w_sems,
     out_sems,
@@ -154,7 +151,7 @@
     width = 2 * half
     parts = width // LANES
     inner = hidden.shape[1]
-    block, wide = 256, 512
+    block = gate_all.shape[2]
     some = rows // steps
     mine = 1 - group[0]
     fetches = [
@@ -166,7 +163,7 @@
     loads = [
         pltpu.make_async_copy(source, target, w_sems.at[i])
         for i, (source, target) in enumerate(
-            ((gate_in, gate_w), (up_in, up_w), (down_in, down_w))
+            ((gate_in, gate_w), (up_in, up_w))
         )
     ]
     for copy in fetches + loads:
@@ -186,60 +183,73 @@
             value = jnp.swapaxes(value, 0, 1).reshape(some, width).astype(jnp.bfloat16)
             out[0, i * some : (i + 1) * some, :] = value[:, :half]
             out[1, i * some : (i + 1) * some, :] = value[:, half:]
-    loads[0].wait()
-    loads[1].wait()
+    for copy in loads:
+        copy.wait()
+    put(x_all, x_out)
+    put(c_all, c_out)
     for n in range(inner // block):
         cols = slice(n * block, (n + 1) * block)
         gate = dot(x_all[0], gate_w[:half, cols]) + dot(x_all[1], gate_w[half:, cols])
         up = dot(x_all[0], up_w[:half, cols]) + dot(x_all[1], up_w[half:, cols])
-        gate_all[:, cols] = gate
-        up_all[:, cols] = up
+        gate_all[n] = gate
+        up_all[n] = up
+        put(gate_all.at[n], gate_out.at[n])
+        put(up_all.at[n], up_out.at[n])
         hidden[:, cols] = (gate * jax.nn.sigmoid(gate) * up).astype(jnp.bfloat16)
         send_down[cols, :] = dot(hidden[:, cols], c_all[mine], 0, 0).astype(jnp.bfloat16)
-    put(send_down, down_out)
-    loads[2].wait()
-    for n in range(width // wide):
-        cols = slice(n * wide, (n + 1) * wide)
-        expert_all[:, cols] = dot(hidden[...], down_w[:, cols]).astype(jnp.bfloat16)
-    put(expert_all, expert_out)
-    put(x_all, x_out)
-    put(c_all, c_out)
-    put(gate_all, gate_out)
-    put(up_all, up_out)
+        put(send_down.at[cols], down_out.at[cols])
     put(hidden, hidden_out)
     for copy in sent:
         copy.wait()
 
 
-def front(group, arrived, gate_w, up_w, down_w):
+def front(group, arrived, gate_w, up_w):
     rings, plane, _, tall, _ = arrived.shape
     width, inner = gate_w.shape
     rows = rings * plane * tall * LANES // width
-    half, members = width // 2, 8
+    half, members, block = width // 2, 8, 256
     steps = plane // members
     f32, b16 = jnp.float32, jnp.bfloat16
     shapes = [
         ((2, rows, half), b16),
         ((2, rows, half), b16),
-        ((rows, inner), f32),
-        ((rows, inner), f32),
+        ((inner // block, rows, block), f32),
+        ((inner // block, rows, block), f32),
         ((rows, inner), b16),
         ((inner, half), b16),
-        ((rows, width), b16),
     ]
-    weights = [((width, inner), b16), ((width, inner), b16), ((inner, width), b16)]
+    weights = [((width, inner), b16)] * 2
+    sends = 3 + 3 * (inner // block)
     return pl.pallas_call(
         front_kernel,
         out_shape=tuple(pltpu.HBM(*shape) for shape in shapes),
         in_specs=[pl.BlockSpec(memory_space=pltpu.SMEM)]
-        + [pl.BlockSpec(memory_space=pl.ANY)] * 4,
+        + [pl.BlockSpec(memory_space=pl.ANY)] * 3,
         out_specs=tuple(pl.BlockSpec(memory_space=pl.ANY) for _ in shapes),
         scratch_shapes=[pltpu.VMEM((steps, rings, members, 2, tall, LANES), b16)]
         + [pltpu.VMEM(*shape) for shape in weights + shapes]
-        + [pltpu.SemaphoreType.DMA((n,)) for n in (steps, len(weights), len(shapes))],
+        + [pltpu.SemaphoreType.DMA((n,)) for n in (steps, len(weights), sends)],
         compiler_params=pltpu.CompilerParams(vmem_limit_bytes=56 * MIB),
         cost_estimate=cheap(),
-    )(group, arrived, gate_w, up_w, down_w)
+    )(group, arrived, gate_w, up_w)
+
+
+def expert_kernel(group, hidden_ref, down_w, out_ref):
+    out_ref[...] = dot(hidden_ref[...], down_w[...]).astype(jnp.bfloat16)
+
+
+def expert(group, hidden, down_w):
+    rows, inner = hidden.shape
+    width, block = down_w.shape[1], 512
+    return call(
+        expert_kernel,
+        group,
+        width // block,
+        [fixed((rows, inner)), across((inner, block))],
+        [(across((rows, block)), (rows, width), jnp.bfloat16)],
+        hidden,
+        down_w,
+    )[0]
 
 
 def second_kernel(group, x_ref, c_ref, down_w, gate_ref, up_ref, dg_ref, du_ref, send_ref, turned):
@@ -249,7 +259,7 @@
 
     half = x_ref.shape[2]
     back = dot(c_ref[0], down_w[:, :half], 1, 1) + dot(c_ref[1], down_w[:, half:], 1, 1)
-    gate, up = gate_ref[...], up_ref[...]
+    gate, up = gate_ref[0], up_ref[0]
     sigma = jax.nn.sigmoid(gate)
     d_gate = (back * up * sigma * (1.0 + gate * (1.0 - sigma))).astype(jnp.bfloat16)
     d_up = (back * (gate * sigma)).astype(jnp.bfloat16)
@@ -261,8 +271,9 @@
 
 def second(group, inputs, cot_in, down_w, gate, up):
     _, rows, half = inputs.shape
-    inner = gate.shape[1]
-    block, width = 256, 2 * half
+    chunks, _, block = gate.shape
+    inner, width = chunks * block, 2 * half
+    chunk = pl.BlockSpec((1, rows, block), lambda n, g: (n, 0, 0))
     b16 = jnp.bfloat16
     away = pl.BlockSpec((1, rows, half), lambda n, g: (1 - g[0], 0, 0), pipeline_mode=pl.Buffered(1))
     return call(
@@ -273,8 +284,8 @@
             away,
             fixed((2, rows, half), (0, 0, 0)),
             down((block, width)),
-            across((rows, block)),
-            across((rows, block)),
+            chunk,
+            chunk,
         ],
         [
             (across((rows, block)), (rows, inner), b16),
@@ -296,21 +307,20 @@
     )
 
 
-def row_gradient(group, which, d_gate, d_up, gate_w, up_w):
+def row_gradient(group, first, steps, block, cost, d_gate, d_up, gate_w, up_w):
     rows, inner = d_gate.shape
-    width, block = gate_w.shape[0] // 2, 512
-    steps = width // block
-    part = pl.BlockSpec((block, inner), lambda n, g: (n + which * steps, 0))
+    part = pl.BlockSpec((block, inner), lambda n, g: (n + first, 0))
     return call(
         rows_kernel,
         group,
         steps,
         [fixed((rows, inner)), fixed((rows, inner)), part, part],
-        [(across((rows, block)), (rows, width), jnp.bfloat16)],
+        [(across((rows, block)), (rows, steps * block), jnp.bfloat16)],
         d_gate,
         d_up,
         gate_w,
         up_w,
+        cost=cost,
     )[0]
 
 
@@ -355,7 +365,7 @@
 
 def sums(group, rows, *weights):
     count, targets = weights[0].shape
-    width, block = rows.shape[1], 512
+    width, block = rows.shape[1], 256
     part = targets // 2
     return call(
         sums_kernel,
@@ -463,20 +473,19 @@
 
     gate_weight, up_weight, down_weight = w_gate[0], w_up[0], w_down[0]
     at = group.astype(jnp.int32).reshape(1)
-    inputs, cot_in, gate, up_proj, hidden, send_down, expert_out = front(
-        at, arrived, gate_weight, up_weight, down_weight
-    )
+    inputs, cot_in, gate, up_proj, hidden, send_down = front(at, arrived, gate_weight, up_weight)
     got_down = swap_low(send_down)
-    out_rows = to_plane(expert_out)
+    out_rows = to_plane(expert(at, hidden, down_weight))
     d_gate, d_up, send_both = second(at, inputs, cot_in, down_weight, gate, up_proj)
     got_both = swap_low(send_both)
-    row_left = row_gradient(at, 0, d_gate, d_up, gate_weight, up_weight)
-    left_rows = to_plane(after(row_left, got_down))
-    row_right = row_gradient(at, 1, after(d_gate, row_left), d_up, gate_weight, up_weight)
-    right_rows = to_plane(row_right)
+    row_left = row_gradient(at, 0, 5, 256, 0, d_gate, d_up, gate_weight, up_weight)
+    tied = lax.optimization_barrier((d_gate, row_left, got_down))
+    d_gate, got_down = tied[0], tied[2]
+    row_right = row_gradient(at, 5, 3, 256, LONG, d_gate, d_up, gate_weight, up_weight)
     coarse, fine, ones = weights_of(lax.optimization_barrier((*facts, row_right))[:-1])
-    out_rows = after(out_rows, coarse, fine, ones)
+    left_rows = to_plane(after(row_left, row_right, coarse, fine, ones))
     out_far, out_near = sums(at, out_rows, coarse, fine)
+    right_rows = to_plane(after(row_right, out_far))
     kept = keep_half(at, inputs, cot_in, after(hidden, out_far), d_gate, d_up)
 
     is_anchor = anchors[ep_index] == ep_index
@@ -490,25 +499,32 @@
         two = jnp.where(group == 0, got, keep)
         return one + jnp.where(is_anchor, two, 0.0) + jnp.where(joins, passed, 0.0)
 
-    grad_down = joined(kept[0], after(got_down, out_far))
     out_came = swap_high(out_far)
-    out_near = out_near + out_came.astype(jnp.float32)
+    left_far, left_near = sums(at, after(left_rows, out_far), ones)
+    out_near = out_near + after(out_came, left_far).astype(jnp.float32)
     out_others = out_near[token_count:].astype(jnp.bfloat16)
     out_last = swap_low(out_others)
-    left_far, left_near = sums(at, after(left_rows, out_others), ones)
+    got_both = after(got_both, left_far, out_others)
+    grad_down = joined(kept[0], after(got_down, left_far, out_others))
     left_came = swap_high(left_far)
-    right_far, right_near = sums(at, after(right_rows, left_far, got_both), ones)
+    right_far, right_near = sums(at, after(right_rows, left_far, got_both, out_others), ones)
     right_came = swap_high(right_far)
-    got_both = after(got_both, right_far)
     grad_gate = joined(kept[1], got_both[0])
     grad_up = joined(kept[2], got_both[1])
     out_last = after(out_last, right_far)
     mixed = (out_near[:token_count] + out_last.astype(jnp.float32)).astype(jnp.bfloat16)
-    ends = []
-    for near, came in ((left_near, left_came), (right_near, right_came)):
-        near = near + came.astype(jnp.float32)
-        last = swap_low(near[token_count:].astype(jnp.bfloat16)).astype(jnp.float32)
-        ends.append((near[:token_count] + last).astype(jnp.bfloat16))
+    left_near = left_near + after(left_came, right_far).astype(jnp.float32)
+    left_others = left_near[token_count:].astype(jnp.bfloat16)
+    left_last = swap_low(left_others)
+    right_came, left_last, grad_down = lax.optimization_barrier((right_came, left_last, grad_down))
+    right_near = right_near + right_came.astype(jnp.float32)
+    right_last = swap_low(right_near[token_count:].astype(jnp.bfloat16))
+    tied = (left_last, right_last, mixed, grad_down, grad_gate, grad_up)
+    left_last, right_last, mixed, grad_down, grad_gate, grad_up = lax.optimization_barrier(tied)
+    ends = [
+        (near[:token_count] + last.astype(jnp.float32)).astype(jnp.bfloat16)
+        for near, last in ((left_near, left_last), (right_near, right_last))
+    ]
     input_grad = jnp.concatenate(ends, axis=1)
     return (mixed, input_grad, grad_gate[None], grad_up[None], grad_down[None])
 

time: 264 us -> 258 us (0.977)
  waiting for transfers between devices: 109 us -> 90.1 us
  other arithmetic: 21.7 us -> 26.3 us
  Pallas kernels: 77.5 us -> 82.1 us
  starting transfers between devices: 47.6 us -> 51 us
    ppermute x6, waiting for transfers between devices: 80.3 us -> 0.02 us  [swap_low(): return lax.ppermute(block, 'xlo', [(0, 1), (1, 0)])]
    ppermute x4, waiting for transfers between devices: 5.11 us -> 67.2 us  [swap_high(): return lax.ppermute(block, ('xlo', 'xhi'), route)]
    add x3 -> x5, other arithmetic: 0.59 us -> 13.1 us  [the longest x2 10.3 us: joined(): return one + jnp.where(is_anchor, two, 0.0) + jnp.where(joins, passed, 0.0)]
    pallas_call x7 -> x8, Pallas kernels: 49.8 us -> 61.7 us  [call(): pl.pallas_call(kernel, grid_spec=pltpu.PrefetchScalarGridSpec(num_scalar_...]
    broadcast_in_dim x2 -> x0, other arithmetic: 9.61 us -> none  [on_device(): return (mixed, input_grad, grad_gate[None], grad_up[None], grad_down[None])]
    pallas_call x1, Pallas kernels: 19.9 us -> 12.7 us  [front(): pl.pallas_call(front_kernel, out_shape=tuple((pltpu.HBM(*shape) for shape...]
    ppermute x4, starting transfers between devices: 0.42 us -> 7.49 us  [swap_high(): return lax.ppermute(block, ('xlo', 'xhi'), route)]
  transfers between devices with their start and end apart: 18 -> 18, of which waited for: 11 -> 5; matrix products, arithmetic and copies ran while one was open for 7% -> 10% of each run, Pallas kernels for 19% -> 24%
where the time goes in v4:
time: 258 us; the launch traced here: 257 us
  waiting for transfers between devices  90.1 us (35%)
  Pallas kernels  82.1 us (32%)
  starting transfers between devices  51 us (20%)
  other arithmetic  26.3 us (10%)
  local copies, waits for them, and re-layouts  5.31 us (2%)
    ppermute x4, waiting for transfers between devices, swap_high(): return lax.ppermute(block, ('xlo', 'xhi'), route)  67.2 us
    pallas_call x8, Pallas kernels, call(): pl.pallas_call(kernel, grid_spec=pltpu.PrefetchScalarGridSpec(num_scalar_...  61.7 us
    all_to_all x3, starting transfers between devices, to_plane(): lax.all_to_all(chunks, PLANE, 0, 0, tiled=True)  18.9 us
    all_to_all x3, waiting for transfers between devices, to_plane(): lax.all_to_all(chunks, PLANE, 0, 0, tiled=True)  15.5 us
    pallas_call x1, Pallas kernels, front(): pl.pallas_call(front_kernel, out_shape=tuple((pltpu.HBM(*shape) for shape...  12.7 us
    all_to_all x1, starting transfers between devices, on_device(): lax.all_to_all(packed.reshape(slots, -1, LANES), AXES, 0, 0, tiled=True)  11.9 us
    add x2, other arithmetic, joined(): return one + jnp.where(is_anchor, two, 0.0) + jnp.where(joins, passed, 0.0)  10.3 us
    ppermute x3, starting transfers between devices, joined(): lax.ppermute(jnp.where(group == 0, got, keep), 'core', [(1, 0)])  8.61 us
  transfers between devices with their start and end apart: 18, of which 5 were waited for; matrix products, arithmetic and copies ran while one was open for 10% of the time, Pallas kernels for 24%

profile of v4, /device:TPU:1, one launch (start us, length us, event | category | flops | bytes accessed | tf_op | source)
XLA Modules:
  0.0 257.0 jit_solution(11745959083360369286)
XLA Ops:
  0.6 7.7 %shard_map.119 = (bf16[128,2,96,128]{3,2,1,0:T(8,128)(2,1)}, s32[4,128]{1,0:T(4,128)}) custom-call(s32[4,128]{1,0:T(4,128)} %bitcast.97, f32[4,128]{1,0:T(4,128)} %bitcast.95, bf16[128,2048]{1,0:T(8,128)(2,1)} %tok_ref.1, bf16[128,2048]{1,0:T(8,128)(2,1)} %cot_ref.1), custom_call_target="tpu_custom_call" | custom-call | tf_op jit(solution)/shard_map/pallas_call | solution.py:63
  8.3 11.9 %all-to-all-start = ((bf16[128,192,128]{2,1,0:T(8,128)(2,1)}), bf16[128,192,128]{2,1,0:T(8,128)(2,1)}, u32[]{:S(2)}, u32[]{:S(2)}) async-start(bf16[128,192,128]{2,1,0:T(8,128)(2,1)} %bitcast.82), calls=%async_computation | async-start | bytes 12582912 | tf_op jit(solution)/shard_map/all_to_all | solution.py:433
  20.3 2.7 %collective-permute-start = (f32[16,128]{1,0:T(8,128)S(1)}, f32[16,128]{1,0:T(8,128)S(1)}, u32[]{:S(2)}, u32[]{:S(2)}) collective-permute-start(f32[16,128]{1,0:T(8,128)S(1)} %pad_maximum_fusion.4), channel_id=1, source_target_pairs={{0,96},{32,64},{64,32},{96,0},{1,97},{33,65},{65,33},{97,1},{2,98}... | collective-permute-start | bytes 24584 | tf_op jit(solution)/shard_map/ppermute | solution.py:409
  23.0 0.6 collective-permute-start.1
  23.5 0.1 collective-permute-start.2
  23.6 67.2 %collective-permute-done = f32[16,128]{1,0:T(8,128)S(1)} collective-permute-done((f32[16,128]{1,0:T(8,128)S(1)}, f32[16,128]{1,0:T(8,128)S(1)}, u32[]{:S(2)}, u32[]{:S(2)}) %collective-permute-start) | collective-permute-done | bytes 8224 | tf_op jit(solution)/shard_map/ppermute | solution.py:409
  90.8 1.4 collective-permute-done.1
  92.3 0.0 collective-permute-done.2
  92.3 5.9 %all-to-all-done = bf16[128,192,128]{2,1,0:T(8,128)(2,1)} async-done(((bf16[128,192,128]{2,1,0:T(8,128)(2,1)}), bf16[128,192,128]{2,1,0:T(8,128)(2,1)}, u32[]{:S(2)}, u32[]{:S(2)}) %all-to-all-start) | async-done | bytes 6291488 | tf_op jit(solution)/shard_map/all_to_all | solution.py:433
  98.2 12.7 %shard_map.120 = (bf16[2,768,1024]{2,1,0:T(8,128)(2,1)}, bf16[2,768,1024]{2,1,0:T(8,128)(2,1)}, f32[3,768,256]{2,1,0:T(8,128)}, f32[3,768,256]{2,1,0:T(8,128)}, ...) custom-call(s32[1]{0:T(128)} %bitcast.group, bf16[4,32,2,96,128]{4,3,2,1,0:T(8,128)(2,1)} %bitcast.4.arrived, ...), custom_call_target="tpu_custom_call" | custom-call | tf_op jit(solution)/shard_map/pallas_call | solution.py:223
  110.9 0.1 collective-permute-start.3
  111.0 0.1 pad_add_fusion
  111.1 6.2 %shard_map.124 = bf16[768,2048]{1,0:T(8,128)(2,1)} custom-call(s32[1]{0:T(128)} %bitcast.group, bf16[768,768]{1,0:T(8,128)(2,1)} %get-tuple-element.88.hidden_ref, bf16[768,2048]{1,0:T(8,128)(2,1)} %bitcast.73), custom_call_target="tpu_custom_call" | custom-call | tf_op jit(solution)/shard_map/pallas_call | solution.py:109
  117.4 9.4 %all-to-all-start.1 = ((bf16[32,24,2048]{2,1,0:T(8,128)(2,1)}), bf16[32,24,2048]{2,1,0:T(8,128)(2,1)S(1)}, u32[]{:S(2)}, u32[]{:S(2)}) async-start(bf16[32,24,2048]{2,1,0:T(8,128)(2,1)} %bitcast.72), calls=%async_computation.1 | async-start | bytes 6291456 | tf_op jit(solution)/shard_map/all_to_all | solution.py:472
  126.8 15.4 %shard_map.121 = (bf16[768,768]{1,0:T(8,128)(2,1)}, bf16[768,768]{1,0:T(8,128)(2,1)}, bf16[2,1024,768]{2,1,0:T(8,128)(2,1)}) custom-call(s32[1]{0:T(128)} %bitcast.group, bf16[2,768,1024]{2,1,0:T(8,128)(2,1)} %get-tuple-element.62.x_ref, bf16[2,768,1024]{2,1,0:T(8,128)(2,1)} %get-tuple-element.63.c_ref, bf16[768,2048]{1,0:T(8,128)(2,1)} %bitcast.74, ...), custom_call_target="tpu_custom_call" | custom-call | tf_op jit(solution)/shard_map/pallas_call | solution.py:109
  142.2 1.7 collective-permute-start.4
  143.9 7.7 %shard_map.122 = bf16[768,1280]{1,0:T(8,128)(2,1)} custom-call(s32[1]{0:T(128)} %bitcast.group, bf16[768,768]{1,0:T(8,128)(2,1)} %get-tuple-element.69.dg_ref, bf16[768,768]{1,0:T(8,128)(2,1)} %get-tuple-element.67.du_ref, bf16[2048,768]{1,0:T(8,128)(2,1)} %bitcast.76, bf16[2048,768]{1,0:T(8,128)(2,1)} %bitcast.79), custom_call_target="tpu_custom_call" | custom-call | tf_op jit(solution)/shard_map/pallas_call | solution.py:109
  151.6 0.0 collective-permute-done.3
  151.6 5.6 %shard_map.123 = bf16[768,768]{1,0:T(8,128)(2,1)} custom-call(s32[1]{0:T(128)} %bitcast.group, bf16[768,768]{1,0:T(8,128)(2,1)} %get-tuple-element.69.dg_ref, bf16[768,768]{1,0:T(8,128)(2,1)} %get-tuple-element.67.du_ref, bf16[2048,768]{1,0:T(8,128)(2,1)} %bitcast.77, bf16[2048,768]{1,0:T(8,128)(2,1)} %bitcast.80), custom_call_target="tpu_custom_call" | custom-call | flops 40000000000 | tf_op jit(solution)/shard_map/pallas_call | solution.py:109
  157.2 0.1 fusion.15
  157.3 3.3 %add_convert_fusion = (bf16[768,512]{1,0:T(8,128)(2,1)}, bf16[768,512]{1,0:T(8,128)(2,1)}, bf16[768,512]{1,0:T(8,128)(2,1)}) fusion(f32[512]{0:T(512)S(1)} %bitcast.99, f32[512]{0:T(512)S(1)} %bitcast.100, f32[512]{0:T(512)S(1)} %bitcast.101, f32[512]{0:T(512)S(1)} %bitcast.98, s32[512]{0:T(512)S(1)} %bitcast.103, s32[512]{0:T(512)S(1)} %bitcast.104, ...), kind=kLoop, calls=%fused_computation.18 | loop fusion | flops 11010048 | bytes 2383872 | tf_op jit(solution)/shard_map/convert_element_type | solution.py:466
  160.6 5.9 %all-to-all-done.1 = bf16[32,24,2048]{2,1,0:T(8,128)(2,1)S(1)} async-done(((bf16[32,24,2048]{2,1,0:T(8,128)(2,1)}), bf16[32,24,2048]{2,1,0:T(8,128)(2,1)S(1)}, u32[]{:S(2)}, u32[]{:S(2)}) %all-to-all-start.1) | async-done | bytes 3145760 | tf_op jit(solution)/shard_map/all_to_all | solution.py:472
  166.6 1.7 copy-done
  168.2 5.0 %all-to-all-start.3 = ((bf16[32,24,1280]{2,1,0:T(8,128)(2,1)}), bf16[32,24,1280]{2,1,0:T(8,128)(2,1)}, u32[]{:S(2)}, u32[]{:S(2)}) async-start(bf16[32,24,1280]{2,1,0:T(8,128)(2,1)} %bitcast.81), calls=%async_computation.3 | async-start | bytes 3932160 | tf_op jit(solution)/shard_map/all_to_all | solution.py:472
  173.3 8.8 %shard_map.125 = (bf16[256,2048]{1,0:T(8,128)(2,1)}, f32[256,2048]{1,0:T(8,128)}) custom-call(s32[1]{0:T(128)} %bitcast.group, bf16[768,512]{1,0:T(8,128)(2,1)} %get-tuple-element.112.refs_0_, bf16[768,512]{1,0:T(8,128)(2,1)} %get-tuple-element.111.refs_1_, bf16[768,2048]{1,0:T(8,128)(2,1)} %bitcast.71), custom_call_target="tpu_custom_call" | custom-call | tf_op jit(solution)/shard_map/pallas_call | solution.py:109
  182.1 0.1 collective-permute-start.5
  182.1 8.5 %shard_map.128 = (bf16[768,1024]{1,0:T(8,128)(2,1)}, bf16[1024,768]{1,0:T(8,128)(2,1)}, bf16[1024,768]{1,0:T(8,128)(2,1)}) custom-call(s32[1]{0:T(128)} %bitcast.group, bf16[2,768,1024]{2,1,0:T(8,128)(2,1)} %get-tuple-element.62.x_ref, bf16[2,768,1024]{2,1,0:T(8,128)(2,1)} %get-tuple-element.63.c_ref, bf16[768,768]{1,0:T(8,128)(2,1)} %get-tuple-element.88.hidden_ref, ...), custom_call_target="tpu_custom_call" | custom-call | tf_op jit(solution)/shard_map/pallas_call | solution.py:109
  190.6 9.6 %all-to-all-done.3 = bf16[32,24,1280]{2,1,0:T(8,128)(2,1)} async-done(((bf16[32,24,1280]{2,1,0:T(8,128)(2,1)}), bf16[32,24,1280]{2,1,0:T(8,128)(2,1)}, u32[]{:S(2)}, u32[]{:S(2)}) %all-to-all-start.3) | async-done | bytes 1966112 | tf_op jit(solution)/shard_map/all_to_all | solution.py:472
  200.2 4.4 %all-to-all-start.2 = ((bf16[32,24,768]{2,1,0:T(8,128)(2,1)}), bf16[32,24,768]{2,1,0:T(8,128)(2,1)S(1)}, u32[]{:S(2)}, u32[]{:S(2)}) async-start(bf16[32,24,768]{2,1,0:T(8,128)(2,1)} %bitcast.34), calls=%async_computation.2 | async-start | bytes 2359296 | tf_op jit(solution)/shard_map/all_to_all | solution.py:472
  204.6 5.6 %shard_map.126 = (bf16[256,1280]{1,0:T(8,128)(2,1)}, f32[256,1280]{1,0:T(8,128)}) custom-call(s32[1]{0:T(128)} %bitcast.group, bf16[768,512]{1,0:T(8,128)(2,1)} %get-tuple-element.113.refs_0_, bf16[768,1280]{1,0:T(8,128)(2,1)} %bitcast.37.refs_1_), custom_call_target="tpu_custom_call" | custom-call | tf_op jit(solution)/shard_map/pallas_call | solution.py:109
  210.3 0.1 collective-permute-start.7
  210.4 0.0 collective-permute-done.5
  210.4 1.0 copy-done.8
  211.4 1.6 convert_add_fusion
  213.0 0.9 slice.130
  213.8 2.8 %broadcast_select_fusion = bf16[768,1024]{1,0:T(8,128)(2,1)} fusion(bf16[768,1024]{1,0:T(8,128)(2,1)} %collective-permute-done.3, bf16[768,1024]{1,0:T(8,128)(2,1)S(1)} %copy-done.3, pred[]{:T(512)S(6)} %eq.105), kind=kLoop, calls=%fused_computation.25 | loop fusion | flops 786432 | bytes 4718593 | tf_op jit(solution)/shard_map/jit(_where)/select_n | solution.py:496
  216.6 3.7 %collective-permute-start.9 = (bf16[768,1024]{1,0:T(8,128)(2,1)}, bf16[768,1024]{1,0:T(8,128)(2,1)}, u32[]{:S(2)}, u32[]{:S(2)}) collective-permute-start(bf16[768,1024]{1,0:T(8,128)(2,1)} %broadcast_select_fusion), channel_id=1, source_target_pairs={{1,0},{3,2},{5,4},{7,6},{9,8},{11,10},{13,12},{15,14},{17,16},{19,... | collective-permute-start | bytes 4718600 | tf_op jit(solution)/shard_map/ppermute | solution.py:496
  220.3 0.6 fusion.23
  222.2 0.1 collective-permute-start.11
  222.3 0.0 collective-permute-done.4
  222.3 3.9 %bitcast_select_fusion = (bf16[1024,768]{1,0:T(8,128)(2,1)}, bf16[1024,768]{1,0:T(8,128)(2,1)}) fusion(bf16[1024,768]{1,0:T(8,128)(2,1)} %get-tuple-element.98, pred[]{:T(512)S(6)} %eq.105, bf16[2,1024,768]{2,1,0:T(8,128)(2,1)} %collective-permute-done.4, bf16[1024,768]{1,0:T(8,128)(2,1)} %get-tuple-element.97), kind=kLoop, calls=%fused_computation.16 | loop fusion | flops 1572864 | bytes 9437185 | tf_op jit(solution)/shard_map/jit(_where)/select_n | solution.py:496
  226.2 2.5 collective-permute-start.13
  228.7 2.4 collective-permute-start.12
  231.2 0.0 all-to-all-done.2
  231.2 1.0 copy-done.5
  232.2 4.0 %shard_map.127 = (bf16[256,768]{1,0:T(8,128)(2,1)}, f32[256,768]{1,0:T(8,128)}) custom-call(s32[1]{0:T(128)} %bitcast.group, bf16[768,512]{1,0:T(8,128)(2,1)} %get-tuple-element.113.refs_0_, bf16[768,768]{1,0:T(8,128)(2,1)} %bitcast.83), custom_call_target="tpu_custom_call" | custom-call | tf_op jit(solution)/shard_map/pallas_call | solution.py:109
  236.2 0.0 collective-permute-done.7
  236.2 4.6 %collective-permute-start.6 = (bf16[256,768]{1,0:T(8,128)(2,1)}, bf16[256,768]{1,0:T(8,128)(2,1)S(1)}, u32[]{:S(2)}, u32[]{:S(2)}) collective-permute-start(bf16[256,768]{1,0:T(8,128)(2,1)} %get-tuple-element.85), channel_id=1, source_target_pairs={{0,96},{32,64},{64,32},{96,0},{1,97},{33,65},{65,33},{97,1},{2,98}... | collective-permute-start | bytes 1179656 | tf_op jit(solution)/shard_map/ppermute | solution.py:409
  240.8 1.2 convert_add_fusion.1
  242.0 0.0 copy-start.4
  242.0 0.0 collective-permute-done.11
  242.1 0.1 collective-permute-start.8
  242.1 2.0 fusion.9
  244.2 0.0 collective-permute-done.9
  244.2 4.8 %fusion.1 = f32[768,1024]{1,0:T(8,128)} fusion(bf16[768,1024]{1,0:T(8,128)(2,1)} %collective-permute-done.3, bf16[768,1024]{1,0:T(8,128)(2,1)S(1)} %copy-done.4, bf16[768,1024]{1,0:T(8,128)(2,1)} %collective-permute-done.9, pred[]{:T(512)S(6)} %and.16, pred[]{:T(512)S(6)} %eq.106, pred[]{:T(512)S(6)} %eq.105), kind=kLoop, calls=%fused_computation.7 | loop fusion | flops 7077888 | bytes 7864323 | tf_op jit(solution)/shard_map/add | solution.py:500
  249.0 0.0 collective-permute-done.8
  249.0 0.0 collective-permute-done.6
  249.0 0.1 convert_add_fusion.2
  249.1 1.4 collective-permute-start.10
  250.6 0.0 collective-permute-done.13
  250.6 0.0 collective-permute-done.12
  250.6 5.5 %fusion.7 = (f32[1024,768]{1,0:T(8,128)}, f32[1024,768]{1,0:T(8,128)}) fusion(bf16[1024,768]{1,0:T(8,128)(2,1)S(1)} %copy-done.2, bf16[1024,768]{1,0:T(8,128)(2,1)} %collective-permute-done.13, pred[]{:T(512)S(6)} %and.16, pred[]{:T(512)S(6)} %eq.106, pred[]{:T(512)S(6)} %eq.105, bf16[2,1024,768]{2,1,0:T(8,128)(2,1)} %collective-permute-done.4, ...), kind=kLoop, calls=%fused_computation.13 | loop fusion | flops 14155776 | bytes 15728643 | tf_op jit(solution)/shard_map/add | solution.py:500
  256.1 0.1 fusion.10
  256.2 0.8 pad_maximum_fusion
  (36 shorter events, 0.2 us)
Async XLA Ops:
  8.3 11.9 %copy-start.13 = (s32[4,128]{1,0:T(4,128)S(1)}, s32[4,128]{1,0:T(4,128)}, u32[]{:S(2)}) copy-start(s32[4,128]{1,0:T(4,128)} %get-tuple-element.56) | copy-start | bytes 6148
  8.3 11.9 %copy-start.11 = (s32[128,4]{0,1:T(4,128)S(1)}, s32[128,4]{0,1:T(4,128)}, u32[]{:S(2)}) copy-start(s32[128,4]{0,1:T(4,128)} %param.11) | copy-start | bytes 6148
  8.3 12.0 %copy-start.10 = (f32[128,4]{0,1:T(4,128)S(1)}, f32[128,4]{0,1:T(4,128)}, u32[]{:S(2)}) copy-start(f32[128,4]{0,1:T(4,128)} %param.10) | copy-start | bytes 6148
  8.3 89.9 %all-to-all-start = ((bf16[128,192,128]{2,1,0:T(8,128)(2,1)}), bf16[128,192,128]{2,1,0:T(8,128)(2,1)}, u32[]{:S(2)}, u32[]{:S(2)}) async-start(bf16[128,192,128]{2,1,0:T(8,128)(2,1)} %bitcast.82), calls=%async_computation | async-start | bytes 12582912 | tf_op jit(solution)/shard_map/all_to_all | solution.py:433
  20.3 70.6 %collective-permute-start = (f32[16,128]{1,0:T(8,128)S(1)}, f32[16,128]{1,0:T(8,128)S(1)}, u32[]{:S(2)}, u32[]{:S(2)}) collective-permute-start(f32[16,128]{1,0:T(8,128)S(1)} %pad_maximum_fusion.4), channel_id=1, source_target_pairs={{0,96},{32,64},{64,32},{96,0},{1,97},{33,65},{65,33},{97,1},{2,98}... | collective-permute-start | bytes 24584 | tf_op jit(solution)/shard_map/ppermute | solution.py:409
  23.0 69.3 %collective-permute-start.1 = (f32[16,128]{1,0:T(8,128)S(1)}, f32[16,128]{1,0:T(8,128)S(1)}, u32[]{:S(2)}, u32[]{:S(2)}) collective-permute-start(f32[16,128]{1,0:T(8,128)S(1)} %pad_maximum_fusion.4), channel_id=1, source_target_pairs={{0,32},{32,0},{1,33},{33,1},{2,34},{34,2},{3,35},{35,3},{4,36},{36... | collective-permute-start | bytes 24584 | tf_op jit(solution)/shard_map/ppermute | solution.py:438
  23.5 68.7 %collective-permute-start.2 = (f32[16,128]{1,0:T(8,128)S(1)}, f32[16,128]{1,0:T(8,128)S(1)}, u32[]{:S(2)}, u32[]{:S(2)}) collective-permute-start(f32[16,128]{1,0:T(8,128)S(1)} %pad_maximum_fusion.4), channel_id=1, source_target_pairs={{0,64},{64,0},{1,65},{65,1},{2,66},{66,2},{3,67},{67,3},{4,68},{68... | collective-permute-start | bytes 24584 | tf_op jit(solution)/shard_map/ppermute | solution.py:404
  110.9 40.6 %collective-permute-start.3 = (bf16[768,1024]{1,0:T(8,128)(2,1)}, bf16[768,1024]{1,0:T(8,128)(2,1)}, u32[]{:S(2)}, u32[]{:S(2)}) collective-permute-start(bf16[768,1024]{1,0:T(8,128)(2,1)} %get-tuple-element.68), channel_id=1, source_target_pairs={{0,64},{64,0},{1,65},{65,1},{2,66},{66,2},{3,67},{67,3},{4,68},{68... | collective-permute-start | bytes 4718600 | tf_op jit(solution)/shard_map/ppermute | solution.py:404
  117.4 49.2 %all-to-all-start.1 = ((bf16[32,24,2048]{2,1,0:T(8,128)(2,1)}), bf16[32,24,2048]{2,1,0:T(8,128)(2,1)S(1)}, u32[]{:S(2)}, u32[]{:S(2)}) async-start(bf16[32,24,2048]{2,1,0:T(8,128)(2,1)} %bitcast.72), calls=%async_computation.1 | async-start | bytes 6291456 | tf_op jit(solution)/shard_map/all_to_all | solution.py:472
  142.2 80.1 %collective-permute-start.4 = (bf16[2,1024,768]{2,1,0:T(8,128)(2,1)}, bf16[2,1024,768]{2,1,0:T(8,128)(2,1)}, u32[]{:S(2)}, u32[]{:S(2)}) collective-permute-start(bf16[2,1024,768]{2,1,0:T(8,128)(2,1)} %get-tuple-element.80), channel_id=1, source_target_pairs={{0,64},{64,0},{1,65},{65,1},{2,66},{66,2},{3,67},{67,3},{4,68},{68... | collective-permute-start | bytes 9437192 | tf_op jit(solution)/shard_map/ppermute | solution.py:404
  166.6 1.7 copy-start
  168.2 32.0 %all-to-all-start.3 = ((bf16[32,24,1280]{2,1,0:T(8,128)(2,1)}), bf16[32,24,1280]{2,1,0:T(8,128)(2,1)}, u32[]{:S(2)}, u32[]{:S(2)}) async-start(bf16[32,24,1280]{2,1,0:T(8,128)(2,1)} %bitcast.81), calls=%async_computation.3 | async-start | bytes 3932160 | tf_op jit(solution)/shard_map/all_to_all | solution.py:472
  182.1 28.3 %collective-permute-start.5 = (bf16[256,2048]{1,0:T(8,128)(2,1)}, bf16[256,2048]{1,0:T(8,128)(2,1)S(1)}, u32[]{:S(2)}, u32[]{:S(2)}) collective-permute-start(bf16[256,2048]{1,0:T(8,128)(2,1)} %get-tuple-element.75), channel_id=1, source_target_pairs={{0,96},{32,64},{64,32},{96,0},{1,97},{33,65},{65,33},{97,1},{2,98}... | collective-permute-start | bytes 3145736 | tf_op jit(solution)/shard_map/ppermute | solution.py:409
  200.2 31.0 %all-to-all-start.2 = ((bf16[32,24,768]{2,1,0:T(8,128)(2,1)}), bf16[32,24,768]{2,1,0:T(8,128)(2,1)S(1)}, u32[]{:S(2)}, u32[]{:S(2)}) async-start(bf16[32,24,768]{2,1,0:T(8,128)(2,1)} %bitcast.34), calls=%async_computation.2 | async-start | bytes 2359296 | tf_op jit(solution)/shard_map/all_to_all | solution.py:472
  204.6 6.7 %copy-start.6 = (f32[256,2048]{1,0:T(8,128)S(1)}, f32[256,2048]{1,0:T(8,128)}, u32[]{:S(2)}) copy-start(f32[256,2048]{1,0:T(8,128)} %get-tuple-element.81) | copy-start | bytes 6291460
  210.3 25.9 %collective-permute-start.7 = (bf16[256,1280]{1,0:T(8,128)(2,1)}, bf16[256,1280]{1,0:T(8,128)(2,1)}, u32[]{:S(2)}, u32[]{:S(2)}) collective-permute-start(bf16[256,1280]{1,0:T(8,128)(2,1)} %get-tuple-element.79), channel_id=1, source_target_pairs={{0,96},{32,64},{64,32},{96,0},{1,97},{33,65},{65,33},{97,1},{2,98}... | collective-permute-start | bytes 1966088 | tf_op jit(solution)/shard_map/ppermute | solution.py:409
  210.4 1.0 copy-start.8
  211.4 2.5 copy-start.3
  213.8 6.4 %copy-start.12 = (s32[64]{0:T(128)S(1)}, s32[64]{0:T(128)}, u32[]{:S(2)}) copy-start(s32[64]{0:T(128)} %param.12) | copy-start | bytes 772
  216.6 27.6 %collective-permute-start.9 = (bf16[768,1024]{1,0:T(8,128)(2,1)}, bf16[768,1024]{1,0:T(8,128)(2,1)}, u32[]{:S(2)}, u32[]{:S(2)}) collective-permute-start(bf16[768,1024]{1,0:T(8,128)(2,1)} %broadcast_select_fusion), channel_id=1, source_target_pairs={{1,0},{3,2},{5,4},{7,6},{9,8},{11,10},{13,12},{15,14},{17,16},{19,... | collective-permute-start | bytes 4718600 | tf_op jit(solution)/shard_map/ppermute | solution.py:496
  222.2 19.8 %collective-permute-start.11 = (bf16[128,2048]{1,0:T(8,128)(2,1)}, bf16[128,2048]{1,0:T(8,128)(2,1)}, u32[]{:S(2)}, u32[]{:S(2)}) collective-permute-start(bf16[128,2048]{1,0:T(8,128)(2,1)} %slice.130), channel_id=1, source_target_pairs={{0,64},{64,0},{1,65},{65,1},{2,66},{66,2},{3,67},{67,3},{4,68},{68... | collective-permute-start | bytes 1572872 | tf_op jit(solution)/shard_map/ppermute | solution.py:404
  226.2 24.4 %collective-permute-start.13 = (bf16[1024,768]{1,0:T(8,128)(2,1)}, bf16[1024,768]{1,0:T(8,128)(2,1)}, u32[]{:S(2)}, u32[]{:S(2)}) collective-permute-start(bf16[1024,768]{1,0:T(8,128)(2,1)} %get-tuple-element.109), channel_id=1, source_target_pairs={{1,0},{3,2},{5,4},{7,6},{9,8},{11,10},{13,12},{15,14},{17,16},{19,... | collective-permute-start | bytes 4718600 | tf_op jit(solution)/shard_map/ppermute | solution.py:496
  228.7 21.9 %collective-permute-start.12 = (bf16[1024,768]{1,0:T(8,128)(2,1)}, bf16[1024,768]{1,0:T(8,128)(2,1)}, u32[]{:S(2)}, u32[]{:S(2)}) collective-permute-start(bf16[1024,768]{1,0:T(8,128)(2,1)} %get-tuple-element.110), channel_id=1, source_target_pairs={{1,0},{3,2},{5,4},{7,6},{9,8},{11,10},{13,12},{15,14},{17,16},{19,... | collective-permute-start | bytes 4718600 | tf_op jit(solution)/shard_map/ppermute | solution.py:496
  231.2 1.0 copy-start.5
  231.2 9.6 %copy-start.7 = (f32[256,1280]{1,0:T(8,128)S(1)}, f32[256,1280]{1,0:T(8,128)}, u32[]{:S(2)}) copy-start(f32[256,1280]{1,0:T(8,128)} %get-tuple-element.86) | copy-start | bytes 3932164
  236.2 12.8 %collective-permute-start.6 = (bf16[256,768]{1,0:T(8,128)(2,1)}, bf16[256,768]{1,0:T(8,128)(2,1)S(1)}, u32[]{:S(2)}, u32[]{:S(2)}) collective-permute-start(bf16[256,768]{1,0:T(8,128)(2,1)} %get-tuple-element.85), channel_id=1, source_target_pairs={{0,96},{32,64},{64,32},{96,0},{1,97},{33,65},{65,33},{97,1},{2,98}... | collective-permute-start | bytes 1179656 | tf_op jit(solution)/shard_map/ppermute | solution.py:409
  242.0 2.2 copy-start.4
  242.1 6.9 %collective-permute-start.8 = (bf16[128,1280]{1,0:T(8,128)(2,1)S(1)}, bf16[128,1280]{1,0:T(8,128)(2,1)S(1)}, u32[]{:S(2)}, u32[]{:S(2)}) collective-permute-start(bf16[128,1280]{1,0:T(8,128)(2,1)S(1)} %slice.131), channel_id=1, source_target_pairs={{0,64},{64,0},{1,65},{65,1},{2,66},{66,2},{3,67},{67,3},{4,68},{68... | collective-permute-start | bytes 983048 | tf_op jit(solution)/shard_map/ppermute | solution.py:404
  244.2 4.8 %copy-start.9 = (f32[256,768]{1,0:T(8,128)S(1)}, f32[256,768]{1,0:T(8,128)}, u32[]{:S(2)}) copy-start(f32[256,768]{1,0:T(8,128)} %get-tuple-element.93) | copy-start | bytes 2359300
  244.2 6.4 %copy-start.2 = (bf16[1024,768]{1,0:T(8,128)(2,1)S(1)}, bf16[1024,768]{1,0:T(8,128)(2,1)}, u32[]{:S(2)}) copy-start(bf16[1024,768]{1,0:T(8,128)(2,1)} %get-tuple-element.98) | copy-start | bytes 4718596
  249.0 1.6 copy-start.1
  249.1 6.9 %collective-permute-start.10 = (bf16[128,768]{1,0:T(8,128)(2,1)S(1)}, bf16[128,768]{1,0:T(8,128)(2,1)S(1)}, u32[]{:S(2)}, u32[]{:S(2)}) collective-permute-start(bf16[128,768]{1,0:T(8,128)(2,1)S(1)} %slice.132), channel_id=1, source_target_pairs={{0,64},{64,0},{1,65},{65,1},{2,66},{66,2},{3,67},{67,3},{4,68},{68... | collective-permute-start | bytes 589832 | tf_op jit(solution)/shard_map/ppermute | solution.py:404

commit v5 on v4

--- a/solution.py
+++ b/solution.py
@@ -58,7 +58,7 @@
 def pack(route, weight, tokens, cotangent, slots, pair_rows):
     count, width = tokens.shape
     tall = pair_rows * width // LANES
-    block = 16
+    block = 32
     whole = lambda i: (0, 0)
     return pl.pallas_call(
         functools.partial(pack_kernel, pair_rows),
@@ -240,7 +240,7 @@
 
 def expert(group, hidden, down_w):
     rows, inner = hidden.shape
-    width, block = down_w.shape[1], 512
+    width, block = down_w.shape[1], 1024
     return call(
         expert_kernel,
         group,
@@ -365,7 +365,8 @@
 
 def sums(group, rows, *weights):
     count, targets = weights[0].shape
-    width, block = rows.shape[1], 256
+    width = rows.shape[1]
+    block = width // 2
     part = targets // 2
     return call(
         sums_kernel,

time: 258 us -> 254 us (0.984)
  Pallas kernels: 82.1 us -> 76.3 us
    pallas_call x8, Pallas kernels: 61.7 us -> 57 us  [call(): pl.pallas_call(kernel, grid_spec=pltpu.PrefetchScalarGridSpec(num_scalar_...]
  transfers between devices with their start and end apart: 18 -> 18, of which waited for: 5 -> 5; matrix products, arithmetic and copies ran while one was open for 10% -> 11% of each run, Pallas kernels for 24% -> 22%
where the time goes in v5:
time: 254 us
  waiting for transfers between devices  92.3 us (36%)
  Pallas kernels  76.3 us (30%)
  starting transfers between devices  51.2 us (20%)
  other arithmetic  26.3 us (10%)
  local copies, waits for them, and re-layouts  5.31 us (2%)
    ppermute x4, waiting for transfers between devices, swap_high(): return lax.ppermute(block, ('xlo', 'xhi'), route)  67.2 us
    pallas_call x8, Pallas kernels, call(): pl.pallas_call(kernel, grid_spec=pltpu.PrefetchScalarGridSpec(num_scalar_...  57 us
    all_to_all x3, starting transfers between devices, to_plane(): lax.all_to_all(chunks, PLANE, 0, 0, tiled=True)  18.9 us
    all_to_all x3, waiting for transfers between devices, to_plane(): lax.all_to_all(chunks, PLANE, 0, 0, tiled=True)  17.7 us
    pallas_call x1, Pallas kernels, front(): pl.pallas_call(front_kernel, out_shape=tuple((pltpu.HBM(*shape) for shape...  12.7 us
    all_to_all x1, starting transfers between devices, on_device(): lax.all_to_all(packed.reshape(slots, -1, LANES), AXES, 0, 0, tiled=True)  11.9 us
    add x2, other arithmetic, joined(): return one + jnp.where(is_anchor, two, 0.0) + jnp.where(joins, passed, 0.0)  10.3 us
    ppermute x3, starting transfers between devices, joined(): lax.ppermute(jnp.where(group == 0, got, keep), 'core', [(1, 0)])  8.61 us
  transfers between devices with their start and end apart: 18, of which 5 were waited for; matrix products, arithmetic and copies ran while one was open for 11% of the time, Pallas kernels for 22%

profile of v5, /device:TPU:1, one launch (start us, length us, event | category | flops | bytes accessed | tf_op | source)
XLA Modules:
  0.0 253.6 jit_solution(17347972249365219458)
XLA Ops:
  0.6 6.7 %shard_map.119 = (bf16[128,2,96,128]{3,2,1,0:T(8,128)(2,1)}, s32[4,128]{1,0:T(4,128)}) custom-call(s32[4,128]{1,0:T(4,128)} %bitcast.97, f32[4,128]{1,0:T(4,128)} %bitcast.95, bf16[128,2048]{1,0:T(8,128)(2,1)} %tok_ref.1, bf16[128,2048]{1,0:T(8,128)(2,1)} %cot_ref.1), custom_call_target="tpu_custom_call" | custom-call | tf_op jit(solution)/shard_map/pallas_call | solution.py:63
  7.3 11.9 %all-to-all-start = ((bf16[128,192,128]{2,1,0:T(8,128)(2,1)}), bf16[128,192,128]{2,1,0:T(8,128)(2,1)}, u32[]{:S(2)}, u32[]{:S(2)}) async-start(bf16[128,192,128]{2,1,0:T(8,128)(2,1)} %bitcast.82), calls=%async_computation | async-start | bytes 12582912 | tf_op jit(solution)/shard_map/all_to_all | solution.py:434
  19.3 2.7 %collective-permute-start = (f32[16,128]{1,0:T(8,128)S(1)}, f32[16,128]{1,0:T(8,128)S(1)}, u32[]{:S(2)}, u32[]{:S(2)}) collective-permute-start(f32[16,128]{1,0:T(8,128)S(1)} %pad_maximum_fusion.4), channel_id=1, source_target_pairs={{0,96},{32,64},{64,32},{96,0},{1,97},{33,65},{65,33},{97,1},{2,98}... | collective-permute-start | bytes 24584 | tf_op jit(solution)/shard_map/ppermute | solution.py:410
  21.9 0.6 collective-permute-start.1
  22.5 0.1 collective-permute-start.2
  22.6 67.2 %collective-permute-done = f32[16,128]{1,0:T(8,128)S(1)} collective-permute-done((f32[16,128]{1,0:T(8,128)S(1)}, f32[16,128]{1,0:T(8,128)S(1)}, u32[]{:S(2)}, u32[]{:S(2)}) %collective-permute-start) | collective-permute-done | bytes 8224 | tf_op jit(solution)/shard_map/ppermute | solution.py:410
  89.8 1.4 collective-permute-done.1
  91.3 0.0 collective-permute-done.2
  91.3 5.9 %all-to-all-done = bf16[128,192,128]{2,1,0:T(8,128)(2,1)} async-done(((bf16[128,192,128]{2,1,0:T(8,128)(2,1)}), bf16[128,192,128]{2,1,0:T(8,128)(2,1)}, u32[]{:S(2)}, u32[]{:S(2)}) %all-to-all-start) | async-done | bytes 6291488 | tf_op jit(solution)/shard_map/all_to_all | solution.py:434
  97.2 12.7 %shard_map.120 = (bf16[2,768,1024]{2,1,0:T(8,128)(2,1)}, bf16[2,768,1024]{2,1,0:T(8,128)(2,1)}, f32[3,768,256]{2,1,0:T(8,128)}, f32[3,768,256]{2,1,0:T(8,128)}, ...) custom-call(s32[1]{0:T(128)} %bitcast.group, bf16[4,32,2,96,128]{4,3,2,1,0:T(8,128)(2,1)} %bitcast.4.arrived, ...), custom_call_target="tpu_custom_call" | custom-call | tf_op jit(solution)/shard_map/pallas_call | solution.py:223
  109.9 0.1 collective-permute-start.3
  110.0 0.1 pad_add_fusion
  110.1 5.7 %shard_map.124 = bf16[768,2048]{1,0:T(8,128)(2,1)} custom-call(s32[1]{0:T(128)} %bitcast.group, bf16[768,768]{1,0:T(8,128)(2,1)} %get-tuple-element.88.hidden_ref, bf16[768,2048]{1,0:T(8,128)(2,1)} %bitcast.73), custom_call_target="tpu_custom_call" | custom-call | tf_op jit(solution)/shard_map/pallas_call | solution.py:109
  115.8 9.4 %all-to-all-start.1 = ((bf16[32,24,2048]{2,1,0:T(8,128)(2,1)}), bf16[32,24,2048]{2,1,0:T(8,128)(2,1)S(1)}, u32[]{:S(2)}, u32[]{:S(2)}) async-start(bf16[32,24,2048]{2,1,0:T(8,128)(2,1)} %bitcast.72), calls=%async_computation.1 | async-start | bytes 6291456 | tf_op jit(solution)/shard_map/all_to_all | solution.py:473
  125.2 15.4 %shard_map.121 = (bf16[768,768]{1,0:T(8,128)(2,1)}, bf16[768,768]{1,0:T(8,128)(2,1)}, bf16[2,1024,768]{2,1,0:T(8,128)(2,1)}) custom-call(s32[1]{0:T(128)} %bitcast.group, bf16[2,768,1024]{2,1,0:T(8,128)(2,1)} %get-tuple-element.62.x_ref, bf16[2,768,1024]{2,1,0:T(8,128)(2,1)} %get-tuple-element.63.c_ref, bf16[768,2048]{1,0:T(8,128)(2,1)} %bitcast.74, ...), custom_call_target="tpu_custom_call" | custom-call | tf_op jit(solution)/shard_map/pallas_call | solution.py:109
  140.6 1.7 collective-permute-start.4
  142.3 7.7 %shard_map.122 = bf16[768,1280]{1,0:T(8,128)(2,1)} custom-call(s32[1]{0:T(128)} %bitcast.group, bf16[768,768]{1,0:T(8,128)(2,1)} %get-tuple-element.69.dg_ref, bf16[768,768]{1,0:T(8,128)(2,1)} %get-tuple-element.67.du_ref, bf16[2048,768]{1,0:T(8,128)(2,1)} %bitcast.76, bf16[2048,768]{1,0:T(8,128)(2,1)} %bitcast.79), custom_call_target="tpu_custom_call" | custom-call | tf_op jit(solution)/shard_map/pallas_call | solution.py:109
  150.0 0.0 collective-permute-done.3
  150.0 5.6 %shard_map.123 = bf16[768,768]{1,0:T(8,128)(2,1)} custom-call(s32[1]{0:T(128)} %bitcast.group, bf16[768,768]{1,0:T(8,128)(2,1)} %get-tuple-element.69.dg_ref, bf16[768,768]{1,0:T(8,128)(2,1)} %get-tuple-element.67.du_ref, bf16[2048,768]{1,0:T(8,128)(2,1)} %bitcast.77, bf16[2048,768]{1,0:T(8,128)(2,1)} %bitcast.80), custom_call_target="tpu_custom_call" | custom-call | flops 40000000000 | tf_op jit(solution)/shard_map/pallas_call | solution.py:109
  155.6 0.1 fusion.15
  155.7 3.3 %add_convert_fusion = (bf16[768,512]{1,0:T(8,128)(2,1)}, bf16[768,512]{1,0:T(8,128)(2,1)}, bf16[768,512]{1,0:T(8,128)(2,1)}) fusion(f32[512]{0:T(512)S(1)} %bitcast.99, f32[512]{0:T(512)S(1)} %bitcast.100, f32[512]{0:T(512)S(1)} %bitcast.101, f32[512]{0:T(512)S(1)} %bitcast.98, s32[512]{0:T(512)S(1)} %bitcast.103, s32[512]{0:T(512)S(1)} %bitcast.104, ...), kind=kLoop, calls=%fused_computation.18 | loop fusion | flops 11010048 | bytes 2383872 | tf_op jit(solution)/shard_map/convert_element_type | solution.py:467
  159.0 5.9 %all-to-all-done.1 = bf16[32,24,2048]{2,1,0:T(8,128)(2,1)S(1)} async-done(((bf16[32,24,2048]{2,1,0:T(8,128)(2,1)}), bf16[32,24,2048]{2,1,0:T(8,128)(2,1)S(1)}, u32[]{:S(2)}, u32[]{:S(2)}) %all-to-all-start.1) | async-done | bytes 3145760 | tf_op jit(solution)/shard_map/all_to_all | solution.py:473
  165.0 1.7 copy-done
  166.7 5.0 %all-to-all-start.3 = ((bf16[32,24,1280]{2,1,0:T(8,128)(2,1)}), bf16[32,24,1280]{2,1,0:T(8,128)(2,1)}, u32[]{:S(2)}, u32[]{:S(2)}) async-start(bf16[32,24,1280]{2,1,0:T(8,128)(2,1)} %bitcast.81), calls=%async_computation.3 | async-start | bytes 3932160 | tf_op jit(solution)/shard_map/all_to_all | solution.py:473
  171.7 6.7 %shard_map.125 = (bf16[256,2048]{1,0:T(8,128)(2,1)}, f32[256,2048]{1,0:T(8,128)}) custom-call(s32[1]{0:T(128)} %bitcast.group, bf16[768,512]{1,0:T(8,128)(2,1)} %get-tuple-element.112.refs_0_, bf16[768,512]{1,0:T(8,128)(2,1)} %get-tuple-element.111.refs_1_, bf16[768,2048]{1,0:T(8,128)(2,1)} %bitcast.71), custom_call_target="tpu_custom_call" | custom-call | tf_op jit(solution)/shard_map/pallas_call | solution.py:109
  178.3 0.1 collective-permute-start.5
  178.4 8.5 %shard_map.128 = (bf16[768,1024]{1,0:T(8,128)(2,1)}, bf16[1024,768]{1,0:T(8,128)(2,1)}, bf16[1024,768]{1,0:T(8,128)(2,1)}) custom-call(s32[1]{0:T(128)} %bitcast.group, bf16[2,768,1024]{2,1,0:T(8,128)(2,1)} %get-tuple-element.62.x_ref, bf16[2,768,1024]{2,1,0:T(8,128)(2,1)} %get-tuple-element.63.c_ref, bf16[768,768]{1,0:T(8,128)(2,1)} %get-tuple-element.88.hidden_ref, ...), custom_call_target="tpu_custom_call" | custom-call | tf_op jit(solution)/shard_map/pallas_call | solution.py:109
  186.9 11.7 %all-to-all-done.3 = bf16[32,24,1280]{2,1,0:T(8,128)(2,1)} async-done(((bf16[32,24,1280]{2,1,0:T(8,128)(2,1)}), bf16[32,24,1280]{2,1,0:T(8,128)(2,1)}, u32[]{:S(2)}, u32[]{:S(2)}) %all-to-all-start.3) | async-done | bytes 1966112 | tf_op jit(solution)/shard_map/all_to_all | solution.py:473
  198.6 4.4 %all-to-all-start.2 = ((bf16[32,24,768]{2,1,0:T(8,128)(2,1)}), bf16[32,24,768]{2,1,0:T(8,128)(2,1)S(1)}, u32[]{:S(2)}, u32[]{:S(2)}) async-start(bf16[32,24,768]{2,1,0:T(8,128)(2,1)} %bitcast.34), calls=%async_computation.2 | async-start | bytes 2359296 | tf_op jit(solution)/shard_map/all_to_all | solution.py:473
  203.1 4.2 %shard_map.126 = (bf16[256,1280]{1,0:T(8,128)(2,1)}, f32[256,1280]{1,0:T(8,128)}) custom-call(s32[1]{0:T(128)} %bitcast.group, bf16[768,512]{1,0:T(8,128)(2,1)} %get-tuple-element.113.refs_0_, bf16[768,1280]{1,0:T(8,128)(2,1)} %bitcast.37.refs_1_), custom_call_target="tpu_custom_call" | custom-call | tf_op jit(solution)/shard_map/pallas_call | solution.py:109
  207.2 0.1 collective-permute-start.7
  207.3 0.0 collective-permute-done.5
  207.3 1.0 copy-done.8
  208.3 1.6 convert_add_fusion
  209.9 0.9 slice.130
  210.8 2.8 %broadcast_select_fusion = bf16[768,1024]{1,0:T(8,128)(2,1)} fusion(bf16[768,1024]{1,0:T(8,128)(2,1)} %collective-permute-done.3, bf16[768,1024]{1,0:T(8,128)(2,1)S(1)} %copy-done.3, pred[]{:T(512)S(6)} %eq.105), kind=kLoop, calls=%fused_computation.25 | loop fusion | flops 786432 | bytes 4718593 | tf_op jit(solution)/shard_map/jit(_where)/select_n | solution.py:497
  213.5 3.7 %collective-permute-start.9 = (bf16[768,1024]{1,0:T(8,128)(2,1)}, bf16[768,1024]{1,0:T(8,128)(2,1)}, u32[]{:S(2)}, u32[]{:S(2)}) collective-permute-start(bf16[768,1024]{1,0:T(8,128)(2,1)} %broadcast_select_fusion), channel_id=1, source_target_pairs={{1,0},{3,2},{5,4},{7,6},{9,8},{11,10},{13,12},{15,14},{17,16},{19,... | collective-permute-start | bytes 4718600 | tf_op jit(solution)/shard_map/ppermute | solution.py:497
  217.2 0.6 fusion.23
  219.1 0.3 collective-permute-start.11
  219.5 0.0 collective-permute-done.4
  219.5 3.9 %bitcast_select_fusion = (bf16[1024,768]{1,0:T(8,128)(2,1)}, bf16[1024,768]{1,0:T(8,128)(2,1)}) fusion(bf16[1024,768]{1,0:T(8,128)(2,1)} %get-tuple-element.98, pred[]{:T(512)S(6)} %eq.105, bf16[2,1024,768]{2,1,0:T(8,128)(2,1)} %collective-permute-done.4, bf16[1024,768]{1,0:T(8,128)(2,1)} %get-tuple-element.97), kind=kLoop, calls=%fused_computation.16 | loop fusion | flops 1572864 | bytes 9437185 | tf_op jit(solution)/shard_map/jit(_where)/select_n | solution.py:497
  223.4 2.5 collective-permute-start.13
  225.9 2.4 collective-permute-start.12
  228.3 0.0 all-to-all-done.2
  228.3 1.0 copy-done.5
  229.4 3.4 %shard_map.127 = (bf16[256,768]{1,0:T(8,128)(2,1)}, f32[256,768]{1,0:T(8,128)}) custom-call(s32[1]{0:T(128)} %bitcast.group, bf16[768,512]{1,0:T(8,128)(2,1)} %get-tuple-element.113.refs_0_, bf16[768,768]{1,0:T(8,128)(2,1)} %bitcast.83), custom_call_target="tpu_custom_call" | custom-call | tf_op jit(solution)/shard_map/pallas_call | solution.py:109
  232.7 0.0 collective-permute-done.7
  232.7 4.6 %collective-permute-start.6 = (bf16[256,768]{1,0:T(8,128)(2,1)}, bf16[256,768]{1,0:T(8,128)(2,1)S(1)}, u32[]{:S(2)}, u32[]{:S(2)}) collective-permute-start(bf16[256,768]{1,0:T(8,128)(2,1)} %get-tuple-element.85), channel_id=1, source_target_pairs={{0,96},{32,64},{64,32},{96,0},{1,97},{33,65},{65,33},{97,1},{2,98}... | collective-permute-start | bytes 1179656 | tf_op jit(solution)/shard_map/ppermute | solution.py:410
  237.4 1.2 convert_add_fusion.1
  238.6 0.0 copy-start.4
  238.6 0.0 collective-permute-done.11
  238.6 0.1 collective-permute-start.8
  238.7 2.0 fusion.9
  240.8 0.0 collective-permute-done.9
  240.8 4.8 %fusion.1 = f32[768,1024]{1,0:T(8,128)} fusion(bf16[768,1024]{1,0:T(8,128)(2,1)} %collective-permute-done.3, bf16[768,1024]{1,0:T(8,128)(2,1)S(1)} %copy-done.4, bf16[768,1024]{1,0:T(8,128)(2,1)} %collective-permute-done.9, pred[]{:T(512)S(6)} %and.16, pred[]{:T(512)S(6)} %eq.106, pred[]{:T(512)S(6)} %eq.105), kind=kLoop, calls=%fused_computation.7 | loop fusion | flops 7077888 | bytes 7864323 | tf_op jit(solution)/shard_map/add | solution.py:501
  245.6 0.0 collective-permute-done.8
  245.6 0.0 collective-permute-done.6
  245.6 0.1 convert_add_fusion.2
  245.7 1.4 collective-permute-start.10
  247.1 0.0 collective-permute-done.13
  247.1 0.0 collective-permute-done.12
  247.2 5.5 %fusion.7 = (f32[1024,768]{1,0:T(8,128)}, f32[1024,768]{1,0:T(8,128)}) fusion(bf16[1024,768]{1,0:T(8,128)(2,1)S(1)} %copy-done.2, bf16[1024,768]{1,0:T(8,128)(2,1)} %collective-permute-done.13, pred[]{:T(512)S(6)} %and.16, pred[]{:T(512)S(6)} %eq.106, pred[]{:T(512)S(6)} %eq.105, bf16[2,1024,768]{2,1,0:T(8,128)(2,1)} %collective-permute-done.4, ...), kind=kLoop, calls=%fused_computation.13 | loop fusion | flops 14155776 | bytes 15728643 | tf_op jit(solution)/shard_map/add | solution.py:501
  252.7 0.1 fusion.10
  252.8 0.8 pad_maximum_fusion
  (36 shorter events, 0.2 us)
Async XLA Ops:
  7.3 11.9 %copy-start.13 = (s32[4,128]{1,0:T(4,128)S(1)}, s32[4,128]{1,0:T(4,128)}, u32[]{:S(2)}) copy-start(s32[4,128]{1,0:T(4,128)} %get-tuple-element.56) | copy-start | bytes 6148
  7.3 11.9 %copy-start.11 = (s32[128,4]{0,1:T(4,128)S(1)}, s32[128,4]{0,1:T(4,128)}, u32[]{:S(2)}) copy-start(s32[128,4]{0,1:T(4,128)} %param.11) | copy-start | bytes 6148
  7.3 12.0 %copy-start.10 = (f32[128,4]{0,1:T(4,128)S(1)}, f32[128,4]{0,1:T(4,128)}, u32[]{:S(2)}) copy-start(f32[128,4]{0,1:T(4,128)} %param.10) | copy-start | bytes 6148
  7.3 89.9 %all-to-all-start = ((bf16[128,192,128]{2,1,0:T(8,128)(2,1)}), bf16[128,192,128]{2,1,0:T(8,128)(2,1)}, u32[]{:S(2)}, u32[]{:S(2)}) async-start(bf16[128,192,128]{2,1,0:T(8,128)(2,1)} %bitcast.82), calls=%async_computation | async-start | bytes 12582912 | tf_op jit(solution)/shard_map/all_to_all | solution.py:434
  19.3 70.6 %collective-permute-start = (f32[16,128]{1,0:T(8,128)S(1)}, f32[16,128]{1,0:T(8,128)S(1)}, u32[]{:S(2)}, u32[]{:S(2)}) collective-permute-start(f32[16,128]{1,0:T(8,128)S(1)} %pad_maximum_fusion.4), channel_id=1, source_target_pairs={{0,96},{32,64},{64,32},{96,0},{1,97},{33,65},{65,33},{97,1},{2,98}... | collective-permute-start | bytes 24584 | tf_op jit(solution)/shard_map/ppermute | solution.py:410
  21.9 69.3 %collective-permute-start.1 = (f32[16,128]{1,0:T(8,128)S(1)}, f32[16,128]{1,0:T(8,128)S(1)}, u32[]{:S(2)}, u32[]{:S(2)}) collective-permute-start(f32[16,128]{1,0:T(8,128)S(1)} %pad_maximum_fusion.4), channel_id=1, source_target_pairs={{0,32},{32,0},{1,33},{33,1},{2,34},{34,2},{3,35},{35,3},{4,36},{36... | collective-permute-start | bytes 24584 | tf_op jit(solution)/shard_map/ppermute | solution.py:439
  22.5 68.7 %collective-permute-start.2 = (f32[16,128]{1,0:T(8,128)S(1)}, f32[16,128]{1,0:T(8,128)S(1)}, u32[]{:S(2)}, u32[]{:S(2)}) collective-permute-start(f32[16,128]{1,0:T(8,128)S(1)} %pad_maximum_fusion.4), channel_id=1, source_target_pairs={{0,64},{64,0},{1,65},{65,1},{2,66},{66,2},{3,67},{67,3},{4,68},{68... | collective-permute-start | bytes 24584 | tf_op jit(solution)/shard_map/ppermute | solution.py:405
  109.9 40.1 %collective-permute-start.3 = (bf16[768,1024]{1,0:T(8,128)(2,1)}, bf16[768,1024]{1,0:T(8,128)(2,1)}, u32[]{:S(2)}, u32[]{:S(2)}) collective-permute-start(bf16[768,1024]{1,0:T(8,128)(2,1)} %get-tuple-element.68), channel_id=1, source_target_pairs={{0,64},{64,0},{1,65},{65,1},{2,66},{66,2},{3,67},{67,3},{4,68},{68... | collective-permute-start | bytes 4718600 | tf_op jit(solution)/shard_map/ppermute | solution.py:405
  115.8 49.2 %all-to-all-start.1 = ((bf16[32,24,2048]{2,1,0:T(8,128)(2,1)}), bf16[32,24,2048]{2,1,0:T(8,128)(2,1)S(1)}, u32[]{:S(2)}, u32[]{:S(2)}) async-start(bf16[32,24,2048]{2,1,0:T(8,128)(2,1)} %bitcast.72), calls=%async_computation.1 | async-start | bytes 6291456 | tf_op jit(solution)/shard_map/all_to_all | solution.py:473
  140.6 78.8 %collective-permute-start.4 = (bf16[2,1024,768]{2,1,0:T(8,128)(2,1)}, bf16[2,1024,768]{2,1,0:T(8,128)(2,1)}, u32[]{:S(2)}, u32[]{:S(2)}) collective-permute-start(bf16[2,1024,768]{2,1,0:T(8,128)(2,1)} %get-tuple-element.80), channel_id=1, source_target_pairs={{0,64},{64,0},{1,65},{65,1},{2,66},{66,2},{3,67},{67,3},{4,68},{68... | collective-permute-start | bytes 9437192 | tf_op jit(solution)/shard_map/ppermute | solution.py:405
  165.0 1.7 copy-start
  166.7 32.0 %all-to-all-start.3 = ((bf16[32,24,1280]{2,1,0:T(8,128)(2,1)}), bf16[32,24,1280]{2,1,0:T(8,128)(2,1)}, u32[]{:S(2)}, u32[]{:S(2)}) async-start(bf16[32,24,1280]{2,1,0:T(8,128)(2,1)} %bitcast.81), calls=%async_computation.3 | async-start | bytes 3932160 | tf_op jit(solution)/shard_map/all_to_all | solution.py:473
  178.3 29.0 %collective-permute-start.5 = (bf16[256,2048]{1,0:T(8,128)(2,1)}, bf16[256,2048]{1,0:T(8,128)(2,1)S(1)}, u32[]{:S(2)}, u32[]{:S(2)}) collective-permute-start(bf16[256,2048]{1,0:T(8,128)(2,1)} %get-tuple-element.75), channel_id=1, source_target_pairs={{0,96},{32,64},{64,32},{96,0},{1,97},{33,65},{65,33},{97,1},{2,98}... | collective-permute-start | bytes 3145736 | tf_op jit(solution)/shard_map/ppermute | solution.py:410
  198.6 29.7 %all-to-all-start.2 = ((bf16[32,24,768]{2,1,0:T(8,128)(2,1)}), bf16[32,24,768]{2,1,0:T(8,128)(2,1)S(1)}, u32[]{:S(2)}, u32[]{:S(2)}) async-start(bf16[32,24,768]{2,1,0:T(8,128)(2,1)} %bitcast.34), calls=%async_computation.2 | async-start | bytes 2359296 | tf_op jit(solution)/shard_map/all_to_all | solution.py:473
  203.1 5.2 %copy-start.6 = (f32[256,2048]{1,0:T(8,128)S(1)}, f32[256,2048]{1,0:T(8,128)}, u32[]{:S(2)}) copy-start(f32[256,2048]{1,0:T(8,128)} %get-tuple-element.81) | copy-start | bytes 6291460
  207.2 25.5 %collective-permute-start.7 = (bf16[256,1280]{1,0:T(8,128)(2,1)}, bf16[256,1280]{1,0:T(8,128)(2,1)}, u32[]{:S(2)}, u32[]{:S(2)}) collective-permute-start(bf16[256,1280]{1,0:T(8,128)(2,1)} %get-tuple-element.79), channel_id=1, source_target_pairs={{0,96},{32,64},{64,32},{96,0},{1,97},{33,65},{65,33},{97,1},{2,98}... | collective-permute-start | bytes 1966088 | tf_op jit(solution)/shard_map/ppermute | solution.py:410
  207.3 1.0 copy-start.8
  208.3 2.5 copy-start.3
  210.8 6.4 %copy-start.12 = (s32[64]{0:T(128)S(1)}, s32[64]{0:T(128)}, u32[]{:S(2)}) copy-start(s32[64]{0:T(128)} %param.12) | copy-start | bytes 772
  213.5 27.2 %collective-permute-start.9 = (bf16[768,1024]{1,0:T(8,128)(2,1)}, bf16[768,1024]{1,0:T(8,128)(2,1)}, u32[]{:S(2)}, u32[]{:S(2)}) collective-permute-start(bf16[768,1024]{1,0:T(8,128)(2,1)} %broadcast_select_fusion), channel_id=1, source_target_pairs={{1,0},{3,2},{5,4},{7,6},{9,8},{11,10},{13,12},{15,14},{17,16},{19,... | collective-permute-start | bytes 4718600 | tf_op jit(solution)/shard_map/ppermute | solution.py:497
  219.1 19.5 %collective-permute-start.11 = (bf16[128,2048]{1,0:T(8,128)(2,1)}, bf16[128,2048]{1,0:T(8,128)(2,1)}, u32[]{:S(2)}, u32[]{:S(2)}) collective-permute-start(bf16[128,2048]{1,0:T(8,128)(2,1)} %slice.130), channel_id=1, source_target_pairs={{0,64},{64,0},{1,65},{65,1},{2,66},{66,2},{3,67},{67,3},{4,68},{68... | collective-permute-start | bytes 1572872 | tf_op jit(solution)/shard_map/ppermute | solution.py:405
  223.4 23.8 %collective-permute-start.13 = (bf16[1024,768]{1,0:T(8,128)(2,1)}, bf16[1024,768]{1,0:T(8,128)(2,1)}, u32[]{:S(2)}, u32[]{:S(2)}) collective-permute-start(bf16[1024,768]{1,0:T(8,128)(2,1)} %get-tuple-element.109), channel_id=1, source_target_pairs={{1,0},{3,2},{5,4},{7,6},{9,8},{11,10},{13,12},{15,14},{17,16},{19,... | collective-permute-start | bytes 4718600 | tf_op jit(solution)/shard_map/ppermute | solution.py:497
  225.9 21.3 %collective-permute-start.12 = (bf16[1024,768]{1,0:T(8,128)(2,1)}, bf16[1024,768]{1,0:T(8,128)(2,1)}, u32[]{:S(2)}, u32[]{:S(2)}) collective-permute-start(bf16[1024,768]{1,0:T(8,128)(2,1)} %get-tuple-element.110), channel_id=1, source_target_pairs={{1,0},{3,2},{5,4},{7,6},{9,8},{11,10},{13,12},{15,14},{17,16},{19,... | collective-permute-start | bytes 4718600 | tf_op jit(solution)/shard_map/ppermute | solution.py:497
  228.3 1.0 copy-start.5
  228.3 9.0 %copy-start.7 = (f32[256,1280]{1,0:T(8,128)S(1)}, f32[256,1280]{1,0:T(8,128)}, u32[]{:S(2)}) copy-start(f32[256,1280]{1,0:T(8,128)} %get-tuple-element.86) | copy-start | bytes 3932164
  232.7 12.8 %collective-permute-start.6 = (bf16[256,768]{1,0:T(8,128)(2,1)}, bf16[256,768]{1,0:T(8,128)(2,1)S(1)}, u32[]{:S(2)}, u32[]{:S(2)}) collective-permute-start(bf16[256,768]{1,0:T(8,128)(2,1)} %get-tuple-element.85), channel_id=1, source_target_pairs={{0,96},{32,64},{64,32},{96,0},{1,97},{33,65},{65,33},{97,1},{2,98}... | collective-permute-start | bytes 1179656 | tf_op jit(solution)/shard_map/ppermute | solution.py:410
  238.6 2.2 copy-start.4
  238.6 6.9 %collective-permute-start.8 = (bf16[128,1280]{1,0:T(8,128)(2,1)S(1)}, bf16[128,1280]{1,0:T(8,128)(2,1)S(1)}, u32[]{:S(2)}, u32[]{:S(2)}) collective-permute-start(bf16[128,1280]{1,0:T(8,128)(2,1)S(1)} %slice.131), channel_id=1, source_target_pairs={{0,64},{64,0},{1,65},{65,1},{2,66},{66,2},{3,67},{67,3},{4,68},{68... | collective-permute-start | bytes 983048 | tf_op jit(solution)/shard_map/ppermute | solution.py:405
  240.8 4.8 %copy-start.9 = (f32[256,768]{1,0:T(8,128)S(1)}, f32[256,768]{1,0:T(8,128)}, u32[]{:S(2)}) copy-start(f32[256,768]{1,0:T(8,128)} %get-tuple-element.93) | copy-start | bytes 2359300
  240.8 6.4 %copy-start.2 = (bf16[1024,768]{1,0:T(8,128)(2,1)S(1)}, bf16[1024,768]{1,0:T(8,128)(2,1)}, u32[]{:S(2)}) copy-start(bf16[1024,768]{1,0:T(8,128)(2,1)} %get-tuple-element.98) | copy-start | bytes 4718596
  245.6 1.6 copy-start.1
  245.7 6.9 %collective-permute-start.10 = (bf16[128,768]{1,0:T(8,128)(2,1)S(1)}, bf16[128,768]{1,0:T(8,128)(2,1)S(1)}, u32[]{:S(2)}, u32[]{:S(2)}) collective-permute-start(bf16[128,768]{1,0:T(8,128)(2,1)S(1)} %slice.132), channel_id=1, source_target_pairs={{0,64},{64,0},{1,65},{65,1},{2,66},{66,2},{3,67},{67,3},{4,68},{68... | collective-permute-start | bytes 589832 | tf_op jit(solution)/shard_map/ppermute | solution.py:405
